TPU v7x, 256 devices: a whole 4x4x8 slice. The times are simulated.
256 devices in a mesh: dp: 32 (over z, y), seq: 8 (over x, core).
Axes of the slice: x: 4, y: 4, z: 8, core: 2. Of those that a mesh axis runs over, the one named last changes fastest.
Arguments:
- projected: bfloat16 [32, 1024, 9216], P('dp', 'seq'), may hold values from -12 to 12
- cotangent: bfloat16 [32, 1024, 3072], P('dp', 'seq'), may hold values from -6 to 6
- lengths: int32 [32], replicated, may hold values from 64 to 512, as said below
- text_lengths: int32 [32], replicated, may hold values from 128 to 512, as said below
- destinations: int32 [32], replicated, may hold values from 0 to 31, as said below
Outputs:
- attended: bfloat16 [32, 1024, 3072], P('dp', 'seq')
- projected_grad: bfloat16 [32, 1024, 9216], P('dp', 'seq')
Inputs may be any that keep to these rules, and one draw needn't show every extreme that they name: `lengths`: live latent tokens are the first slots of a clip; some clip has exactly 512. `text_lengths`: live text tokens are the first of the clip's 512 text slots; some clip has exactly 512. destinations is a permutation of 0..31.
All inputs are finite; a program needn't handle non-finite values.
Results may differ from a plain program's by a relative error of at most 0.005.
Values may be sent and summed in bfloat16 or wider, within the bound.
No kernel may reach another device: no remote copies, remote signals or barrier semaphores. Data moves between devices by JAX's collectives and lax.ppermute only.
A program may use at most 64 MiB of HBM per device.

v0:
```python
import jax
import jax.numpy as jnp
from jax import lax
from jax.sharding import PartitionSpec as P

HEADS = 24
HEAD_DIM = 128
CAP = 512
SEQ_LEN = 1024


def relocate(data, senders):
    slot_count, row_count, width = data.shape
    rank_count = senders.shape[0]
    sender_order = jnp.transpose(senders)
    moving = data.reshape(slot_count, rank_count, row_count // rank_count, width)
    for step_index in range(2):
        if step_index == 1:
            moving = jnp.take_along_axis(moving, sender_order[:, :, None, None], axis=1)
        moving = lax.all_to_all(moving, "dp", split_axis=1, concat_axis=1, tiled=True)
    return moving.reshape(slot_count, row_count, width)


def head_pass(items):
    queries, key_rows, value_rows, grad_out, live_mask = items
    scaling = queries.shape[-1] ** (-0.5)
    scores = jnp.dot(queries, key_rows.T, preferred_element_type=jnp.float32) * scaling
    scores = jnp.where(live_mask[None, :] > 0, scores, -1e30)
    row_top = jnp.max(scores, axis=-1, keepdims=True)
    exponent = jnp.exp(scores - row_top)
    probabilities = exponent / jnp.sum(exponent, axis=-1, keepdims=True)
    prob_half = probabilities.astype(jnp.bfloat16)
    outputs = jnp.dot(prob_half, value_rows, preferred_element_type=jnp.float32)
    outputs = (outputs * live_mask[:, None]).astype(jnp.bfloat16)
    grad_value = jnp.dot(prob_half.T, grad_out, preferred_element_type=jnp.float32)
    grad_prob = jnp.dot(grad_out, value_rows.T, preferred_element_type=jnp.float32)
    row_dot = jnp.sum(probabilities * grad_prob, axis=-1, keepdims=True)
    grad_scores = (probabilities * (grad_prob - row_dot)).astype(jnp.bfloat16)
    grad_query = jnp.dot(grad_scores, key_rows, preferred_element_type=jnp.float32) * scaling
    grad_key = jnp.dot(grad_scores.T, queries, preferred_element_type=jnp.float32) * scaling
    return (outputs, jnp.stack([grad_query, grad_key, grad_value], axis=1).astype(jnp.bfloat16))


def local_pass(items):
    block, grad_block, live_mask = items
    by_head = jnp.moveaxis(block, 2, 0)
    grad_heads = jnp.moveaxis(grad_block[:, 0], 1, 0)
    grad_heads = jnp.where(live_mask[None, :, None] > 0, grad_heads, jnp.zeros_like(grad_heads))
    masks = jnp.broadcast_to(live_mask[None, :], (by_head.shape[0], live_mask.shape[0]))
    outputs, gradients = lax.map(
        head_pass, (by_head[:, :, 0], by_head[:, :, 1], by_head[:, :, 2], grad_heads, masks)
    )
    outputs = jnp.moveaxis(outputs, 0, 1)[:, None]
    gradients = jnp.moveaxis(gradients, 0, 2)
    return (outputs, gradients)


def on_device(projected, cotangent, lengths, text_lengths, destinations):
    rank_count = lax.axis_size("dp")
    my_rank = lax.axis_index("dp")
    slot_count, local_tokens, width_three = projected.shape
    width = cotangent.shape[2]
    dest_table = destinations.reshape(rank_count, slot_count)
    rank_ids = jnp.arange(rank_count, dtype=jnp.int32)
    senders = jnp.sum(
        jnp.where(dest_table[:, None, :] == rank_ids[None, :, None], rank_ids[:, None, None], 0),
        axis=0,
    )
    moved = relocate(projected.reshape(slot_count, local_tokens * 3 * HEADS, HEAD_DIM), senders)
    here_projected = moved.reshape(slot_count, local_tokens, 3, HEADS, HEAD_DIM)
    here_cotangent = cotangent.reshape(slot_count, local_tokens, 1, HEADS, HEAD_DIM)
    anchor = senders[my_rank]
    clip_ids = anchor * slot_count + jnp.arange(slot_count, dtype=jnp.int32)
    latent_len = lengths[clip_ids]
    text_len = text_lengths[clip_ids]
    full_projected, full_cotangent = (
        lax.all_to_all(here_projected, "seq", split_axis=3, concat_axis=1, tiled=True),
        lax.all_to_all(here_cotangent, "seq", split_axis=3, concat_axis=1, tiled=True),
    )
    position = jnp.arange(SEQ_LEN, dtype=jnp.int32)[None, :]
    live_mask = (
        (position < latent_len[:, None]) | (position >= CAP) & (position < CAP + text_len[:, None])
    ).astype(jnp.float32)
    outputs, gradients = lax.map(local_pass, (full_projected, full_cotangent, live_mask))
    back_outputs, back_gradients = (
        lax.all_to_all(outputs, "seq", split_axis=1, concat_axis=3, tiled=True),
        lax.all_to_all(gradients, "seq", split_axis=1, concat_axis=3, tiled=True),
    )
    attended = back_outputs.reshape(slot_count, local_tokens, width)
    returned = relocate(
        back_gradients.reshape(slot_count, local_tokens * 3 * HEADS, HEAD_DIM), dest_table
    )
    projected_grad = returned.reshape(slot_count, local_tokens, width_three)
    return (attended, projected_grad)


def solution(mesh):
    in_specs = (P("dp", "seq", None), P("dp", "seq", None), P(), P(), P())
    out_specs = (P("dp", "seq", None), P("dp", "seq", None))
    return jax.shard_map(
        on_device, mesh=mesh, in_specs=in_specs, out_specs=out_specs, check_vma=False
    )
```

profile of v0, /device:TPU:6, one launch (start us, length us, event | category | flops | bytes accessed | tf_op | source)
XLA Modules:
  0.0 415.2 jit_solution(5932237533275373228)
XLA Ops:
  0.6 4.3 %reshape_reshape.12 = bf16[1,32,288,128]{3,2,0,1:T(8,128)(2,1)} reshape(bf16[1,128,9216]{2,1,0:T(8,128)(2,1)} %param.9) | data formatting | bytes 4718592 | tf_op jit(solution)/shard_map/reshape;reshape | solution.py:16
  5.0 11.5 %all-to-all-start = ((bf16[1,32,288,128]{3,2,0,1:T(8,128)(2,1)}), bf16[1,32,288,128]{3,2,0,1:T(8,128)(2,1)S(1)}, u32[]{:S(2)}, u32[]{:S(2)}) async-start(bf16[1,32,288,128]{3,2,0,1:T(8,128)(2,1)} %reshape_reshape.12), calls=%async_computation | async-start | bytes 4718592 | tf_op jit(solution)/shard_map/all_to_all | solution.py:20
  16.6 55.6 %all-to-all-done = bf16[1,32,288,128]{3,2,0,1:T(8,128)(2,1)S(1)} async-done(((bf16[1,32,288,128]{3,2,0,1:T(8,128)(2,1)}), bf16[1,32,288,128]{3,2,0,1:T(8,128)(2,1)S(1)}, u32[]{:S(2)}, u32[]{:S(2)}) %all-to-all-start) | async-done | bytes 2359328 | tf_op jit(solution)/shard_map/all_to_all | solution.py:20
  72.2 2.3 gather_fusion
  74.4 3.4 fusion.40
  77.8 6.0 %all-to-all-start.1 = ((bf16[1,32,288,128]{3,2,0,1:T(8,128)(2,1)}), bf16[1,32,288,128]{3,2,0,1:T(8,128)(2,1)S(1)}, u32[]{:S(2)}, u32[]{:S(2)}) async-start(bf16[1,32,288,128]{3,2,0,1:T(8,128)(2,1)} %fusion.40), calls=%async_computation.1 | async-start | bytes 4718592 | tf_op jit(solution)/shard_map/all_to_all | solution.py:20
  85.0 53.6 %all-to-all-done.1 = bf16[1,32,288,128]{3,2,0,1:T(8,128)(2,1)S(1)} async-done(((bf16[1,32,288,128]{3,2,0,1:T(8,128)(2,1)}), bf16[1,32,288,128]{3,2,0,1:T(8,128)(2,1)S(1)}, u32[]{:S(2)}, u32[]{:S(2)}) %all-to-all-start.1) | async-done | bytes 2359328 | tf_op jit(solution)/shard_map/all_to_all | solution.py:20
  138.7 4.8 %all-to-all-start.3 = ((bf16[1,128,1,24,128]{1,4,2,0,3:T(8,128)(2,1)}), bf16[1,128,1,24,128]{1,4,2,0,3:T(8,128)(2,1)S(1)}, u32[]{:S(2)}, u32[]{:S(2)}) async-start(bf16[1,128,1,24,128]{1,4,2,0,3:T(8,128)(2,1)} %bitcast.164), calls=%async_computation.3 | async-start | bytes 1572864 | tf_op jit(solution)/shard_map/all_to_all | solution.py:78
  143.4 2.0 copy.51
  145.5 9.1 %all-to-all-done.3 = bf16[1,128,1,24,128]{1,4,2,0,3:T(8,128)(2,1)S(1)} async-done(((bf16[1,128,1,24,128]{1,4,2,0,3:T(8,128)(2,1)}), bf16[1,128,1,24,128]{1,4,2,0,3:T(8,128)(2,1)S(1)}, u32[]{:S(2)}, u32[]{:S(2)}) %all-to-all-start.3) | async-done | bytes 786464 | tf_op jit(solution)/shard_map/all_to_all | solution.py:78
  154.5 5.6 %all-to-all-start.2 = ((bf16[1,128,3,24,128]{4,1,2,0,3:T(8,128)(2,1)}), bf16[1,128,3,24,128]{4,1,2,0,3:T(8,128)(2,1)S(1)}, u32[]{:S(2)}, u32[]{:S(2)}) async-start(bf16[1,128,3,24,128]{4,1,2,0,3:T(8,128)(2,1)} %copy.51), calls=%async_computation.2 | async-start | bytes 4718592 | tf_op jit(solution)/shard_map/all_to_all | solution.py:77
  168.6 19.5 %all-to-all-done.2 = bf16[1,128,3,24,128]{4,1,2,0,3:T(8,128)(2,1)S(1)} async-done(((bf16[1,128,3,24,128]{4,1,2,0,3:T(8,128)(2,1)}), bf16[1,128,3,24,128]{4,1,2,0,3:T(8,128)(2,1)S(1)}, u32[]{:S(2)}, u32[]{:S(2)}) %all-to-all-start.2) | async-done | bytes 2359328 | tf_op jit(solution)/shard_map/all_to_all | solution.py:77
  189.5 30.1 %while.23 = (s32[]{:T(128)}, bf16[3,1024,128]{2,1,0:T(8,128)(2,1)S(1)}, bf16[3,1024,3,128]{3,1,2,0:T(8,128)(2,1)}, f32[3,1024]{1,0:T(4,128)S(1)}, bf16[3,1024,12...) while((s32[]{:T(128)}, ...), condition=%wide.region_5.7_spmd, body=%wide.region_1.6_spmd.sunk | while | flops 1645344768 | bytes 47786632 | solution.py:50
  192.6 1.7 multiply_convert_fusion.2
  198.0 1.5 fusion.72
  202.6 1.7 multiply_convert_fusion.2
  208.0 1.5 fusion.72
  212.7 1.7 multiply_convert_fusion.2
  218.0 1.5 fusion.72
  219.6 4.0 copy.70
  223.6 41.3 %all_to_all.80 = bf16[1,1024,3,3,128]{4,2,3,0,1:T(4,128)(2,1)S(1)} all-to-all(bf16[1,1024,3,3,128]{4,2,3,0,1:T(4,128)(2,1)S(1)} %bitcast.154), channel_id=1, replica_groups=mesh['dp'=32,'seq'=8] {'seq'}, dimensions={1} | all-to-all | bytes 4718592 | tf_op jit(solution)/shard_map/all_to_all | solution.py:87
  266.3 4.0 reshape_reshape.14
  270.3 6.2 %all-to-all-start.6 = ((bf16[1,32,288,128]{3,2,0,1:T(8,128)(2,1)}), bf16[1,32,288,128]{3,2,0,1:T(8,128)(2,1)S(1)}, u32[]{:S(2)}, u32[]{:S(2)}) async-start(bf16[1,32,288,128]{3,2,0,1:T(8,128)(2,1)} %bitcast.161), calls=%async_computation.6 | async-start | bytes 4718592 | tf_op jit(solution)/shard_map/all_to_all | solution.py:20
  276.5 1.6 copy.71
  278.1 53.7 %all-to-all-done.6 = bf16[1,32,288,128]{3,2,0,1:T(8,128)(2,1)S(1)} async-done(((bf16[1,32,288,128]{3,2,0,1:T(8,128)(2,1)}), bf16[1,32,288,128]{3,2,0,1:T(8,128)(2,1)S(1)}, u32[]{:S(2)}, u32[]{:S(2)}) %all-to-all-start.6) | async-done | bytes 2359328 | tf_op jit(solution)/shard_map/all_to_all | solution.py:20
  331.8 5.6 %all-to-all-start.4 = ((bf16[1,1024,1,3,128]{4,3,2,0,1:T(4,128)(2,1)}), bf16[1,1024,1,3,128]{4,3,2,0,1:T(4,128)(2,1)S(1)}, u32[]{:S(2)}, u32[]{:S(2)}) async-start(bf16[1,1024,1,3,128]{4,3,2,0,1:T(4,128)(2,1)} %bitcast.162), calls=%async_computation.4 | async-start | bytes 2097152 | tf_op jit(solution)/shard_map/all_to_all | solution.py:86
  337.4 2.3 gather_fusion.1
  339.7 3.3 fusion.39
  343.0 8.2 %all-to-all-done.4 = bf16[1,1024,1,3,128]{4,3,2,0,1:T(4,128)(2,1)S(1)} async-done(((bf16[1,1024,1,3,128]{4,3,2,0,1:T(4,128)(2,1)}), bf16[1,1024,1,3,128]{4,3,2,0,1:T(4,128)(2,1)S(1)}, u32[]{:S(2)}, u32[]{:S(2)}) %all-to-all-start.4) | async-done | bytes 786464 | tf_op jit(solution)/shard_map/all_to_all | solution.py:86
  351.3 6.0 %all-to-all-start.7 = ((bf16[1,32,288,128]{3,2,0,1:T(8,128)(2,1)}), bf16[1,32,288,128]{3,2,0,1:T(8,128)(2,1)S(1)}, u32[]{:S(2)}, u32[]{:S(2)}) async-start(bf16[1,32,288,128]{3,2,0,1:T(8,128)(2,1)} %fusion.39), calls=%async_computation.7 | async-start | bytes 4718592 | tf_op jit(solution)/shard_map/all_to_all | solution.py:20
  361.0 51.8 %all-to-all-done.7 = bf16[1,32,288,128]{3,2,0,1:T(8,128)(2,1)S(1)} async-done(((bf16[1,32,288,128]{3,2,0,1:T(8,128)(2,1)}), bf16[1,32,288,128]{3,2,0,1:T(8,128)(2,1)S(1)}, u32[]{:S(2)}, u32[]{:S(2)}) %all-to-all-start.7) | async-done | bytes 2359328 | tf_op jit(solution)/shard_map/all_to_all | solution.py:20
  412.8 2.4 reshape_reshape.15
  (69 shorter events, 33.7 us)
Async XLA Ops:
  0.6 15.9 %copy-start.7 = (s32[32]{0:T(128)S(1)}, s32[32]{0:T(128)}, u32[]{:S(2)}) copy-start(s32[32]{0:T(128)} %param.13) | copy-start | bytes 388
  5.0 67.2 %all-to-all-start = ((bf16[1,32,288,128]{3,2,0,1:T(8,128)(2,1)}), bf16[1,32,288,128]{3,2,0,1:T(8,128)(2,1)S(1)}, u32[]{:S(2)}, u32[]{:S(2)}) async-start(bf16[1,32,288,128]{3,2,0,1:T(8,128)(2,1)} %reshape_reshape.12), calls=%async_computation | async-start | bytes 4718592 | tf_op jit(solution)/shard_map/all_to_all | solution.py:20
  74.4 9.5 %copy-start.3 = (bf16[1,128,3072]{2,1,0:T(8,128)(2,1)S(1)}, bf16[1,128,3072]{2,1,0:T(8,128)(2,1)}, u32[]{:S(2)}) copy-start(bf16[1,128,3072]{2,1,0:T(8,128)(2,1)} %param.10) | copy-start | bytes 2359300
  77.8 60.8 %all-to-all-start.1 = ((bf16[1,32,288,128]{3,2,0,1:T(8,128)(2,1)}), bf16[1,32,288,128]{3,2,0,1:T(8,128)(2,1)S(1)}, u32[]{:S(2)}, u32[]{:S(2)}) async-start(bf16[1,32,288,128]{3,2,0,1:T(8,128)(2,1)} %fusion.40), calls=%async_computation.1 | async-start | bytes 4718592 | tf_op jit(solution)/shard_map/all_to_all | solution.py:20
  138.7 15.9 %all-to-all-start.3 = ((bf16[1,128,1,24,128]{1,4,2,0,3:T(8,128)(2,1)}), bf16[1,128,1,24,128]{1,4,2,0,3:T(8,128)(2,1)S(1)}, u32[]{:S(2)}, u32[]{:S(2)}) async-start(bf16[1,128,1,24,128]{1,4,2,0,3:T(8,128)(2,1)} %bitcast.164), calls=%async_computation.3 | async-start | bytes 1572864 | tf_op jit(solution)/shard_map/all_to_all | solution.py:78
  143.4 19.2 %copy-start.5 = (s32[32]{0:T(128)S(1)}, s32[32]{0:T(128)}, u32[]{:S(2)}) copy-start(s32[32]{0:T(128)} %param.12) | copy-start | bytes 388
  143.4 19.8 %copy-start.6 = (s32[32]{0:T(128)S(1)}, s32[32]{0:T(128)}, u32[]{:S(2)}) copy-start(s32[32]{0:T(128)} %param.11) | copy-start | bytes 388
  154.5 33.5 %all-to-all-start.2 = ((bf16[1,128,3,24,128]{4,1,2,0,3:T(8,128)(2,1)}), bf16[1,128,3,24,128]{4,1,2,0,3:T(8,128)(2,1)S(1)}, u32[]{:S(2)}, u32[]{:S(2)}) async-start(bf16[1,128,3,24,128]{4,1,2,0,3:T(8,128)(2,1)} %copy.51), calls=%async_computation.2 | async-start | bytes 4718592 | tf_op jit(solution)/shard_map/all_to_all | solution.py:77
  188.4 1.1 copy-start
  189.5 1.7 copy-start.4
  199.6 1.7 copy-start.4
  209.6 1.7 copy-start.4
  219.6 45.3 %copy-start.1 = (bf16[3,1024,128]{2,1,0:T(8,128)(2,1)}, bf16[3,1024,128]{2,1,0:T(8,128)(2,1)S(1)}, u32[]{:S(2)}) copy-start(bf16[3,1024,128]{2,1,0:T(8,128)(2,1)S(1)} %get-tuple-element.64) | copy-start | bytes 2359300
  270.3 6.2 %copy-start.2 = (bf16[3,1024,128]{2,1,0:T(8,128)(2,1)S(1)}, bf16[3,1024,128]{2,1,0:T(8,128)(2,1)}, u32[]{:S(2)}) copy-start(bf16[3,1024,128]{2,1,0:T(8,128)(2,1)} %copy-done.1) | copy-start | bytes 2359300
  270.3 61.5 %all-to-all-start.6 = ((bf16[1,32,288,128]{3,2,0,1:T(8,128)(2,1)}), bf16[1,32,288,128]{3,2,0,1:T(8,128)(2,1)S(1)}, u32[]{:S(2)}, u32[]{:S(2)}) async-start(bf16[1,32,288,128]{3,2,0,1:T(8,128)(2,1)} %bitcast.161), calls=%async_computation.6 | async-start | bytes 4718592 | tf_op jit(solution)/shard_map/all_to_all | solution.py:20
  331.8 19.5 %all-to-all-start.4 = ((bf16[1,1024,1,3,128]{4,3,2,0,1:T(4,128)(2,1)}), bf16[1,1024,1,3,128]{4,3,2,0,1:T(4,128)(2,1)S(1)}, u32[]{:S(2)}, u32[]{:S(2)}) async-start(bf16[1,1024,1,3,128]{4,3,2,0,1:T(4,128)(2,1)} %bitcast.162), calls=%async_computation.4 | async-start | bytes 2097152 | tf_op jit(solution)/shard_map/all_to_all | solution.py:86
  351.3 61.5 %all-to-all-start.7 = ((bf16[1,32,288,128]{3,2,0,1:T(8,128)(2,1)}), bf16[1,32,288,128]{3,2,0,1:T(8,128)(2,1)S(1)}, u32[]{:S(2)}, u32[]{:S(2)}) async-start(bf16[1,32,288,128]{3,2,0,1:T(8,128)(2,1)} %fusion.39), calls=%async_computation.7 | async-start | bytes 4718592 | tf_op jit(solution)/shard_map/all_to_all | solution.py:20
where the time goes:
time: 418 us; the launch traced here: 415 us
  waiting for transfers between devices  251 us (60%)
  starting transfers between devices  45.7 us (11%)
  blocking collectives  41.3 us (10%)
  local copies, waits for them, and re-layouts  34.7 us (8%)
  other arithmetic  19.3 us (5%)
  matrix products  19.1 us (5%)
    all_to_all x4, waiting for transfers between devices, relocate(): lax.all_to_all(moving, 'dp', split_axis=1, concat_axis=1, tiled=True)  215 us
    all_to_all x1, blocking collectives, on_device(): lax.all_to_all(gradients, 'seq', split_axis=1, concat_axis=3, tiled=True)  41.3 us
    all_to_all x4, starting transfers between devices, relocate(): lax.all_to_all(moving, 'dp', split_axis=1, concat_axis=1, tiled=True)  29.7 us
    all_to_all x1, waiting for transfers between devices, on_device(): lax.all_to_all(here_projected, 'seq', split_axis=3, concat_axis=1, tiled=...  19.5 us
    all_to_all x1, waiting for transfers between devices, on_device(): lax.all_to_all(here_cotangent, 'seq', split_axis=3, concat_axis=1, tiled=...  9.06 us
  transfers between devices with their start and end apart: 7, of which 7 were waited for; matrix products, arithmetic and copies ran while one was open for 5% of the time, Pallas kernels for 0%

commit v1 on v0

v1 whole, which is shorter than its diff:
```python
import functools
import jax
import jax.numpy as jnp
from jax import lax
from jax.experimental import pallas as pl
from jax.experimental.pallas import tpu as pltpu
from jax.sharding import PartitionSpec as P

HEADS = 24
DH = 128
CAP = 512
SEQ = 1024
RANKS = 32
SHARDS = 8
ROWS = SEQ // SHARDS
MINE = HEADS // SHARDS
GRP = MINE * DH
WIDTH = HEADS * DH
CHIPS = SHARDS // 2
CH = 2 * ROWS
SCALE = DH ** -0.5
LOG2E = 1.4426950408889634
NT = (((1,), (1,)), ((), ()))

ANY = pl.BlockSpec(memory_space=pl.ANY)
SMEM = pl.BlockSpec(memory_space=pltpu.SMEM)
BF = jnp.bfloat16
F32 = jnp.float32


def copies(body, count, given, late, cost=4):
    def kernel(*refs):
        sems = refs[-1]
        started = []
        used = refs[:given] + refs[given + late : -1]
        for n, (src, dst) in enumerate(body(*used)):
            cp = pltpu.make_async_copy(src, dst, sems.at[n])
            cp.start()
            started.append(cp)
        for cp in started:
            cp.wait()

    return functools.partial(
        pl.pallas_call,
        kernel,
        scratch_shapes=[pltpu.SemaphoreType.DMA((count,))],
        compiler_params=pltpu.CompilerParams(vmem_limit_bytes=1 << 20),
        cost_estimate=pl.CostEstimate(flops=0, bytes_accessed=cost << 20, transcendentals=0),
    )


def place(at, k):
    return lax.bitwise_and(lax.shift_right_logical(at[0], 1) + k, CHIPS - 1), at[0] & 1


def split_projected(at, projected, *late):
    def body(at_ref, x_ref, own, other):
        for k in range(CHIPS):
            chip, core = place(at_ref, k)
            for out, head in ((own, 2 * chip + core), (other, 2 * chip + 1 - core)):
                for t in range(3):
                    start = pl.multiple_of(t * WIDTH + head * GRP, GRP)
                    yield x_ref.at[:, pl.ds(start, GRP)], out.at[k, :, pl.ds(t * GRP, GRP)]

    return copies(body, 6 * CHIPS, 2, len(late))(
        out_shape=[pltpu.HBM((CHIPS, ROWS, 3 * GRP), BF)] * 2,
        in_specs=[SMEM, ANY] + [ANY] * len(late),
        out_specs=[ANY] * 2,
        name="split_projected",
    )(at, projected, *late)


def join_gradient(at, blocks, sibling, *late):
    def body(at_ref, *refs):
        out = refs[-1]
        for k in range(CHIPS):
            chip, core = place(at_ref, k)
            mine = refs[k].at[pl.ds(0, ROWS)], 2 * chip + core
            for src, head in (mine, (refs[CHIPS].at[k], 2 * chip + 1 - core)):
                for t in range(3):
                    start = pl.multiple_of(t * WIDTH + head * GRP, GRP)
                    yield src.at[:, pl.ds(t * GRP, GRP)], out.at[:, pl.ds(start, GRP)]

    return copies(body, 6 * CHIPS, 2 + CHIPS, len(late))(
        out_shape=jax.ShapeDtypeStruct((ROWS, 3 * WIDTH), BF),
        in_specs=[SMEM] + [ANY] * (1 + CHIPS + len(late)),
        out_specs=ANY,
        name="join_gradient",
    )(at, *blocks, sibling, *late)


def pair(own, recv, *late):
    width = own.shape[2]

    def body(own_ref, recv_ref, *outs):
        for k in range(CHIPS):
            yield own_ref.at[k], outs[k].at[pl.ds(0, ROWS)]
            yield recv_ref.at[k], outs[k].at[pl.ds(ROWS, ROWS)]

    return copies(body, 2 * CHIPS, 2, len(late))(
        out_shape=[jax.ShapeDtypeStruct((2 * ROWS, width), BF)] * CHIPS,
        in_specs=[ANY] * (2 + len(late)),
        out_specs=[ANY] * CHIPS,
        name="pair",
    )(own, recv, *late)


def for_sibling(blocks, *late):
    width = blocks[0].shape[1]

    def body(*refs):
        for k in range(CHIPS):
            yield refs[k].at[pl.ds(ROWS, ROWS)], refs[CHIPS].at[k]

    return copies(body, CHIPS, CHIPS, len(late))(
        out_shape=jax.ShapeDtypeStruct((CHIPS, ROWS, width), BF),
        in_specs=[ANY] * (CHIPS + len(late)),
        out_specs=ANY,
        name="for_sibling",
    )(*blocks, *late)


def to_pieces(rows, *late):
    def body(x_ref, out):
        for a in range(8):
            for b in range(4):
                yield x_ref.at[pl.ds(16 * a, 16), pl.ds(768 * b, 768)], out.at[4 * a + b]

    return copies(body, RANKS, 1, len(late))(
        out_shape=jax.ShapeDtypeStruct((RANKS, 16, 768), BF),
        in_specs=[ANY] + [ANY] * len(late),
        out_specs=ANY,
        name="to_pieces",
    )(rows, *late)


def from_pieces(pieces, *late):
    def body(x_ref, out):
        for a in range(8):
            for b in range(4):
                yield x_ref.at[4 * a + b], out.at[pl.ds(16 * a, 16), pl.ds(768 * b, 768)]

    return copies(body, RANKS, 1, len(late))(
        out_shape=jax.ShapeDtypeStruct((ROWS, WIDTH), BF),
        in_specs=[ANY] + [ANY] * len(late),
        out_specs=ANY,
        name="from_pieces",
    )(pieces, *late)


def reorder(destinations, pieces, back, *late):
    def body(d_ref, x_ref, out):
        for c in range(RANKS):
            if back:
                yield x_ref.at[c], out.at[d_ref[c]]
            else:
                yield x_ref.at[d_ref[c]], out.at[c]

    return copies(body, RANKS, 2, len(late), 100)(
        out_shape=jax.ShapeDtypeStruct((RANKS, 16, 768), BF),
        in_specs=[SMEM, ANY] + [ANY] * len(late),
        out_specs=ANY,
        name="reorder",
    )(destinations, pieces, *late)


def split_cotangent(at, pieces, *late):
    def body(at_ref, x_ref, own, other):
        for k in range(CHIPS):
            chip, core = place(at_ref, k)
            for out, half in ((own, core), (other, 1 - core)):
                start = pl.multiple_of(half * GRP, GRP)
                for a in range(8):
                    src = x_ref.at[4 * a + chip, :, pl.ds(start, GRP)]
                    yield src, out.at[k, pl.ds(16 * a, 16)]

    return copies(body, 16 * CHIPS, 2, len(late))(
        out_shape=[jax.ShapeDtypeStruct((CHIPS, ROWS, GRP), BF)] * 2,
        in_specs=[SMEM, ANY] + [ANY] * len(late),
        out_specs=[ANY] * 2,
        name="split_cotangent",
    )(at, pieces, *late)


def join_pieces(at, blocks, sibling, *late):
    def body(at_ref, *refs):
        out = refs[-1]
        for k in range(CHIPS):
            chip, core = place(at_ref, k)
            for src, half in ((refs[k], core), (refs[CHIPS].at[k], 1 - core)):
                start = pl.multiple_of(half * GRP, GRP)
                for a in range(8):
                    yield src.at[pl.ds(16 * a, 16)], out.at[4 * a + chip, :, pl.ds(start, GRP)]

    return copies(body, 16 * CHIPS, 2 + CHIPS, len(late))(
        out_shape=jax.ShapeDtypeStruct((RANKS, 16, 768), BF),
        in_specs=[SMEM] + [ANY] * (1 + CHIPS + len(late)),
        out_specs=ANY,
        name="join_pieces",
    )(at, *blocks, sibling, *late)


def live_rows(at, lengths, text_lengths):
    row = lax.broadcasted_iota(jnp.int32, (SEQ, DH), 0)
    chip = lax.bitwise_and((at[0] >> 1) + CHIPS - lax.shift_right_logical(row, 8), CHIPS - 1)
    core = lax.bitwise_xor(at[0] & 1, lax.bitwise_and(lax.shift_right_logical(row, 7), 1))
    pos = (2 * chip + core) * ROWS + lax.bitwise_and(row, ROWS - 1)
    latent, text = lengths[at[1]], text_lengths[at[1]]
    return (pos < latent) | ((pos >= CAP) & (pos < CAP + text))


def fetch(srcs, dst, sems):
    started = []
    for k in range(CHIPS):
        cp = pltpu.make_async_copy(srcs[k], dst.at[pl.ds(k * CH, CH)], sems.at[k])
        cp.start()
        started.append(cp)
    for cp in started:
        cp.wait()


def cols(part, head):
    return pl.ds(pl.multiple_of(part * GRP + head * DH, DH), DH)


def forward_kernel(at, lengths, text_lengths, *refs):
    xs = refs[:CHIPS]
    outs = refs[CHIPS : 2 * CHIPS]
    wide, prob, kept, held, sems, kept_sem = refs[2 * CHIPS :]
    g = pl.program_id(0)
    keep = pltpu.make_async_copy(held, kept, kept_sem)

    @pl.when(g == 0)
    def _():
        fetch(xs, held, sems)
        keep.start()

    @pl.when(g == MINE - 1)
    def _():
        keep.wait()

    live = live_rows(at, lengths, text_lengths)
    lane = lax.broadcasted_iota(jnp.int32, (SEQ, DH), 1)
    dead = jnp.where(live | (lane > 0), 0.0, -1e30).astype(BF)
    unit = jnp.where(lane == 0, 1.0, 0.0).astype(BF)
    q = jnp.concatenate([held[:, cols(0, g)], unit], axis=1)
    k = jnp.concatenate([held[:, cols(1, g)], dead], axis=1)
    vt = held[:, cols(2, g)].T
    livef = live.astype(F32)
    for n in range(SEQ // CH):
        part = slice(n * CH, (n + 1) * CH)
        s = lax.dot_general(k, q[part], NT, preferred_element_type=F32)
        top = jnp.max(s, axis=0, keepdims=True)
        e = jnp.exp2((s - top) * (SCALE * LOG2E))
        full = e * (1.0 / jnp.sum(e, axis=0, keepdims=True))
        p = full.astype(BF)
        rest = (full - p.astype(F32)).astype(BF)
        prob[0, :, part] = full
        o = jnp.dot(vt, p, preferred_element_type=F32)
        more = jnp.dot(vt, rest, preferred_element_type=F32)
        wide[part, pl.ds(pl.multiple_of(g * DH, DH), DH)] = (o + more).T
        o = o.T * livef[part]
        outs[n][:, pl.ds(pl.multiple_of(g * DH, DH), DH)] = o.astype(BF)


def backward_kernel(at, lengths, text_lengths, *refs):
    cs = refs[:CHIPS]
    kept, wide, prob = refs[CHIPS : CHIPS + 3]
    outs = refs[CHIPS + 3 : 2 * CHIPS + 3]
    held, cot, dst, pst, sems, kept_sem = refs[2 * CHIPS + 3 :]
    g = pl.program_id(0)

    @pl.when(g == 0)
    def _():
        back = pltpu.make_async_copy(kept, held, kept_sem)
        back.start()
        fetch(cs, cot, sems)
        back.wait()

    live = live_rows(at, lengths, text_lengths)
    lane = lax.broadcasted_iota(jnp.int32, (SEQ, DH), 1)
    mine = pl.ds(pl.multiple_of(g * DH, DH), DH)
    do = jnp.where(live, cot[:, mine], jnp.zeros((), BF))
    dot = jnp.sum(do.astype(F32) * wide[:, mine], axis=1, keepdims=True)
    hi = dot.astype(BF).astype(F32)
    mid = (dot - hi).astype(BF).astype(F32)
    low = dot - hi - mid
    less = jnp.where(lane == 0, -hi, jnp.where(lane == 1, -mid, jnp.where(lane == 2, -low, 0.0)))
    dox = jnp.concatenate([do, less.astype(BF)], axis=1)
    units = jnp.where(lane < 3, 1.0, 0.0).astype(BF)
    vx = jnp.concatenate([held[:, cols(2, g)], units], axis=1)
    kt = held[:, cols(1, g)].T
    for n in range(SEQ // CH):
        part = slice(n * CH, (n + 1) * CH)
        dp = lax.dot_general(vx, dox[part], NT, preferred_element_type=F32)
        p = prob[0, :, part]
        pst[:, part] = p.astype(BF)
        ds = (p * dp).astype(BF)
        dst[:, part] = ds
        dq = jnp.dot(kt, ds, preferred_element_type=F32).T * SCALE
        outs[n][:, cols(0, g)] = dq.astype(BF)
    q = held[:, cols(0, g)]
    for n in range(SEQ // CH):
        part = slice(n * CH, (n + 1) * CH)
        dk = jnp.dot(dst[part, :], q, preferred_element_type=F32) * SCALE
        dv = jnp.dot(pst[part, :], do, preferred_element_type=F32)
        outs[n][:, cols(1, g)] = dk.astype(BF)
        outs[n][:, cols(2, g)] = dv.astype(BF)


def whole(shape):
    return pl.BlockSpec(shape, lambda g: (0,) * len(shape))


def forward(where, xs):
    return pl.pallas_call(
        forward_kernel,
        grid=(MINE,),
        out_shape=[jax.ShapeDtypeStruct((CH, GRP), BF)] * CHIPS
        + [
            pltpu.HBM((SEQ, GRP), F32),
            pltpu.HBM((MINE, SEQ, SEQ), F32),
            pltpu.HBM((SEQ, 3 * GRP), BF),
        ],
        in_specs=[SMEM] * 3 + [ANY] * CHIPS,
        out_specs=[whole((CH, GRP))] * CHIPS
        + [
            whole((SEQ, GRP)),
            pl.BlockSpec((1, SEQ, SEQ), lambda g: (g, 0, 0)),
            pl.BlockSpec(memory_space=pltpu.HBM),
        ],
        scratch_shapes=[
            pltpu.VMEM((SEQ, 3 * GRP), BF),
            pltpu.SemaphoreType.DMA((CHIPS,)),
            pltpu.SemaphoreType.DMA,
        ],
        compiler_params=pltpu.CompilerParams(vmem_limit_bytes=60 << 20),
        cost_estimate=pl.CostEstimate(
            flops=MINE * 2 * 5 * SEQ * SEQ * DH, bytes_accessed=12 << 20, transcendentals=MINE * SEQ * SEQ
        ),
        name="attend",
    )(*where, *xs)


def backward(where, cs, kept, wide, prob):
    return pl.pallas_call(
        backward_kernel,
        grid=(MINE,),
        out_shape=[jax.ShapeDtypeStruct((CH, 3 * GRP), BF)] * CHIPS,
        in_specs=[SMEM] * 3
        + [ANY] * CHIPS
        + [
            pl.BlockSpec(memory_space=pltpu.HBM),
            whole((SEQ, GRP)),
            pl.BlockSpec((1, SEQ, SEQ), lambda g: (g, 0, 0)),
        ],
        out_specs=[whole((CH, 3 * GRP))] * CHIPS,
        scratch_shapes=[
            pltpu.VMEM((SEQ, 3 * GRP), BF),
            pltpu.VMEM((SEQ, GRP), BF),
            pltpu.VMEM((SEQ, SEQ), BF),
            pltpu.VMEM((SEQ, SEQ), BF),
            pltpu.SemaphoreType.DMA((CHIPS,)),
            pltpu.SemaphoreType.DMA,
        ],
        compiler_params=pltpu.CompilerParams(vmem_limit_bytes=60 << 20),
        cost_estimate=pl.CostEstimate(
            flops=MINE * 2 * 8 * SEQ * SEQ * DH, bytes_accessed=16 << 20, transcendentals=0
        ),
        name="attend_grad",
    )(*where, *cs, kept, wide, prob)


def turn(blocks, sign):
    out = [blocks[0]]
    for k in range(1, CHIPS):
        pairs = [(s, (s + sign * 2 * k) % SHARDS) for s in range(SHARDS)]
        out.append(lax.ppermute(blocks[k], "seq", pairs))
    return out


def swap(block):
    return lax.ppermute(block, "seq", [(s, s ^ 1) for s in range(SHARDS)])


def spread(pieces):
    return lax.all_to_all(pieces, "dp", split_axis=0, concat_axis=0, tiled=True)


def on_device(projected, cotangent, lengths, text_lengths, destinations):
    me = lax.axis_index("seq").astype(jnp.int32)
    at = jnp.stack([me, lax.axis_index("dp").astype(jnp.int32)])
    where = (at, lengths, text_lengths)

    own, other = split_projected(at, projected[0])
    xs = turn(pair(own, swap(other)), 1)
    there = spread(to_pieces(cotangent[0], other))
    here = spread(reorder(destinations, there, False))

    *outs, wide, prob, kept = forward(where, xs)
    os = turn(outs, -1)
    own, other = split_cotangent(at, here, outs[0])
    cs = pair(own, swap(other))
    halfway = spread(join_pieces(at, os, swap(for_sibling(os)), cs[0]))
    cs = turn(cs, 1)

    gs = turn(backward(where, cs, kept, wide, prob), -1)
    home = spread(reorder(destinations, halfway, True, gs[0]))
    projected_grad = join_gradient(at, gs, swap(for_sibling(gs)))
    attended = from_pieces(home)
    return attended[None], projected_grad[None]


def solution(mesh):
    in_specs = (P("dp", "seq", None), P("dp", "seq", None), P(), P(), P())
    out_specs = (P("dp", "seq", None), P("dp", "seq", None))
    return jax.shard_map(
        on_device, mesh=mesh, in_specs=in_specs, out_specs=out_specs, check_vma=False
    )
```

time: 418 us -> 192 us (0.46)
  waiting for transfers between devices: 251 us -> 84.7 us
  Pallas kernels: 0 us -> 45.3 us
  blocking collectives: 41.3 us -> 0 us
  local copies, waits for them, and re-layouts: 34.7 us -> 8.2 us
  other arithmetic: 19.3 us -> 0.08 us
  matrix products: 19.1 us -> 0 us
  starting transfers between devices: 45.7 us -> 50.3 us
    all_to_all x7 -> x4, waiting for transfers between devices: 251 us -> 25.3 us  [spread(): return lax.all_to_all(pieces, 'dp', split_axis=0, concat_axis=0, tiled=True)]
    ppermute x0 -> x16, waiting for transfers between devices: none -> 59.4 us  [the longest x12 56 us: turn(): out.append(lax.ppermute(blocks[k], 'seq', pairs))]
    pallas_call x0 -> x14, Pallas kernels: none -> 45.3 us  [the longest x1 15.6 us: backward(): pl.pallas_call(backward_kernel, grid=(MINE,), out_shape=[jax.ShapeDtypeSt...]
    all_to_all x1 -> x0, blocking collectives: 41.3 us -> none  [on_device(): lax.all_to_all(gradients, 'seq', split_axis=1, concat_axis=3, tiled=True)]
    dot_general x18 -> x0, matrix products: 19.1 us -> none  [the longest x3 4.61 us: head_pass(): outputs = jnp.dot(prob_half, value_rows, preferred_element_type=jnp.float32)]
    ppermute x0 -> x16, starting transfers between devices: none -> 14.7 us  [the longest x12 14.3 us: turn(): out.append(lax.ppermute(blocks[k], 'seq', pairs))]
    another operation x4 -> x0, local copies, waits for them, and re-layouts: 12.8 us -> none  [the longest x2 8.35 us: relocate(): data.reshape(slot_count, rank_count, row_count // rank_count, width)]
    all_to_all x7 -> x4, starting transfers between devices: 45.7 us -> 35.6 us  [spread(): return lax.all_to_all(pieces, 'dp', split_axis=0, concat_axis=0, tiled=True)]
  transfers between devices with their start and end apart: 7 -> 20, of which waited for: 7 -> 14; matrix products, arithmetic and copies ran while one was open for 5% -> 0% of each run, Pallas kernels for 0% -> 21%
where the time goes in v1:
time: 192 us; the launch traced here: 190 us
  waiting for transfers between devices  84.7 us (44%)
  starting transfers between devices  50.3 us (26%)
  Pallas kernels  45.3 us (24%)
  local copies, waits for them, and re-layouts  8.2 us (4%)
    ppermute x12, waiting for transfers between devices, turn(): out.append(lax.ppermute(blocks[k], 'seq', pairs))  56 us
    all_to_all x4, starting transfers between devices, spread(): return lax.all_to_all(pieces, 'dp', split_axis=0, concat_axis=0, tiled=True)  35.6 us
    all_to_all x4, waiting for transfers between devices, spread(): return lax.all_to_all(pieces, 'dp', split_axis=0, concat_axis=0, tiled=True)  25.3 us
    pallas_call x1, Pallas kernels, backward(): pl.pallas_call(backward_kernel, grid=(MINE,), out_shape=[jax.ShapeDtypeSt...  15.6 us
    ppermute x12, starting transfers between devices, turn(): out.append(lax.ppermute(blocks[k], 'seq', pairs))  14.3 us
    pallas_call x1, Pallas kernels, forward(): pl.pallas_call(forward_kernel, grid=(MINE,), out_shape=[jax.ShapeDtypeStr...  13.8 us
    unnamed x42, local copies, waits for them, and re-layouts  8.2 us
  transfers between devices with their start and end apart: 20, of which 14 were waited for; matrix products, arithmetic and copies ran while one was open for 0% of the time, Pallas kernels for 21%

profile of v1, /device:TPU:6, one launch (start us, length us, event | category | flops | bytes accessed | tf_op | source)
XLA Modules:
  0.0 189.7 jit_solution(2242405144021607328)
XLA Ops:
  0.7 1.7 copy-done.2
  2.4 2.1 %split_projected.1 = (bf16[4,128,1152]{2,1,0:T(8,128)(2,1)}, bf16[4,128,1152]{2,1,0:T(8,128)(2,1)}) custom-call(s32[2]{0:T(128)S(1)} %pad_add_fusion.refs_0_.at, bf16[128,9216]{1,0:T(8,128)(2,1)S(1)} %bitcast.6), custom_call_target="tpu_custom_call" | custom-call | bytes 4194304 | tf_op jit(solution)/shard_map/split_projected/pallas_call | solution.py:65
  4.6 1.3 copy-done.7
  5.8 1.1 to_pieces.1
  7.0 11.5 %all-to-all-start = ((bf16[32,16,768]{2,1,0:T(8,128)(2,1)}), bf16[32,16,768]{2,1,0:T(8,128)(2,1)S(1)}, u32[]{:S(2)}, u32[]{:S(2)}) async-start(bf16[32,16,768]{2,1,0:T(8,128)(2,1)} %to_pieces.1), calls=%async_computation | async-start | bytes 1572864 | tf_op jit(solution)/shard_map/all_to_all | solution.py:387
  18.6 22.8 %all-to-all-done.refs_1_ = bf16[32,16,768]{2,1,0:T(8,128)(2,1)S(1)} async-done(((bf16[32,16,768]{2,1,0:T(8,128)(2,1)}), bf16[32,16,768]{2,1,0:T(8,128)(2,1)S(1)}, u32[]{:S(2)}, u32[]{:S(2)}) %all-to-all-start) | async-done | bytes 786464 | tf_op jit(solution)/shard_map/all_to_all | solution.py:387
  41.4 1.7 reorder.2
  43.1 5.1 %all-to-all-start.1 = ((bf16[32,16,768]{2,1,0:T(8,128)(2,1)}), bf16[32,16,768]{2,1,0:T(8,128)(2,1)S(1)}, u32[]{:S(2)}, u32[]{:S(2)}) async-start(bf16[32,16,768]{2,1,0:T(8,128)(2,1)} %reorder.2), calls=%async_computation.1 | async-start | bytes 1572864 | tf_op jit(solution)/shard_map/all_to_all | solution.py:387
  50.1 2.4 %collective-permute-start.2 = (bf16[256,1152]{1,0:T(8,128)(2,1)S(1)}, bf16[256,1152]{1,0:T(8,128)(2,1)S(1)}, u32[]{:S(2)}, u32[]{:S(2)}) collective-permute-start(bf16[256,1152]{1,0:T(8,128)(2,1)S(1)} %get-tuple-element.29), channel_id=1, source_target_pairs={{0,4},{1,5},{2,6},{3,7},{4,0},{5,1},{6,2},{7,3},{8,12},{9,13},{10,... | collective-permute-start | bytes 1769480 | tf_op jit(solution)/shard_map/ppermute | solution.py:378
  52.5 13.4 %collective-permute-done.1.refs_1_ = bf16[256,1152]{1,0:T(8,128)(2,1)S(1)} collective-permute-done((bf16[256,1152]{1,0:T(8,128)(2,1)S(1)}, bf16[256,1152]{1,0:T(8,128)(2,1)S(1)}, u32[]{:S(2)}, u32[]{:S(2)}) %collective-permute-start.1) | collective-permute-done | bytes 589856 | tf_op jit(solution)/shard_map/ppermute | solution.py:378
  65.9 2.0 %collective-permute-done.2.refs_2_ = bf16[256,1152]{1,0:T(8,128)(2,1)S(1)} collective-permute-done((bf16[256,1152]{1,0:T(8,128)(2,1)S(1)}, bf16[256,1152]{1,0:T(8,128)(2,1)S(1)}, u32[]{:S(2)}, u32[]{:S(2)}) %collective-permute-start.2) | collective-permute-done | bytes 589856 | tf_op jit(solution)/shard_map/ppermute | solution.py:378
  67.9 9.7 %collective-permute-done.3.refs_3_ = bf16[256,1152]{1,0:T(8,128)(2,1)S(1)} collective-permute-done((bf16[256,1152]{1,0:T(8,128)(2,1)S(1)}, bf16[256,1152]{1,0:T(8,128)(2,1)S(1)}, u32[]{:S(2)}, u32[]{:S(2)}) %collective-permute-start.3) | collective-permute-done | bytes 589856 | tf_op jit(solution)/shard_map/ppermute | solution.py:378
  78.4 13.8 %attend.1 = (bf16[256,384]{1,0:T(8,128)(2,1)}, bf16[256,384]{1,0:T(8,128)(2,1)}, bf16[256,384]{1,0:T(8,128)(2,1)}, bf16[256,384]{1,0:T(8,128)(2,1)}, f32[1024,38...) custom-call(s32[2]{0:T(128)} %copy-done.10, s32[32]{0:T(128)} %lengths.3, s32[32]{0:T(128)} %text_lengths.3, ...), custom_call_target="tpu_custom_call" | custom-call | flops 4026531840 | bytes 12582912 | tf_op jit(solution)/shard_map/attend/pallas_call | solution.py:316
  93.2 1.7 collective-permute-start.5
  94.9 1.7 collective-permute-start.6
  97.6 1.6 split_cotangent.1
  99.3 5.4 %collective-permute-done.4.refs_1_.refs_2_ = bf16[256,384]{1,0:T(8,128)(2,1)S(1)} collective-permute-done((bf16[256,384]{1,0:T(8,128)(2,1)}, bf16[256,384]{1,0:T(8,128)(2,1)S(1)}, u32[]{:S(2)}, u32[]{:S(2)}) %collective-permute-start.4) | collective-permute-done | bytes 196640 | tf_op jit(solution)/shard_map/ppermute | solution.py:378
  106.9 1.1 pair.3
  108.6 1.9 %join_pieces.1 = bf16[32,16,768]{2,1,0:T(8,128)(2,1)} custom-call(s32[2]{0:T(128)S(1)} %copy-done.11, bf16[256,384]{1,0:T(8,128)(2,1)S(1)} %copy-done.5, bf16[256,384]{1,0:T(8,128)(2,1)S(1)} %collective-permute-done.4.refs_1_.refs_2_, bf16[256,384]{1,0:T(8,128)(2,1)S(1)} %collective-permute-done.5.refs_2_.refs_3_, ...), custom_call_target="tpu_custom_call" | custom-call | bytes 4194304 | tf_op jit(solution)/shard_map/join_pieces/pallas_call | solution.py:195
  110.6 9.5 %all-to-all-start.2 = ((bf16[32,16,768]{2,1,0:T(8,128)(2,1)}), bf16[32,16,768]{2,1,0:T(8,128)(2,1)S(1)}, u32[]{:S(2)}, u32[]{:S(2)}) async-start(bf16[32,16,768]{2,1,0:T(8,128)(2,1)} %join_pieces.1), calls=%async_computation.2 | async-start | bytes 1572864 | tf_op jit(solution)/shard_map/all_to_all | solution.py:387
  120.1 2.7 %collective-permute-start.9 = (bf16[256,384]{1,0:T(8,128)(2,1)S(1)}, bf16[256,384]{1,0:T(8,128)(2,1)S(1)}, u32[]{:S(2)}, u32[]{:S(2)}) collective-permute-start(bf16[256,384]{1,0:T(8,128)(2,1)S(1)} %get-tuple-element.38), channel_id=1, source_target_pairs={{0,2},{1,3},{2,4},{3,5},{4,6},{5,7},{6,0},{7,1},{8,10},{9,11},{10,... | collective-permute-start | bytes 589832 | tf_op jit(solution)/shard_map/ppermute | solution.py:378
  123.8 7.5 %collective-permute-done.9.refs_1_ = bf16[256,384]{1,0:T(8,128)(2,1)S(1)} collective-permute-done((bf16[256,384]{1,0:T(8,128)(2,1)S(1)}, bf16[256,384]{1,0:T(8,128)(2,1)S(1)}, u32[]{:S(2)}, u32[]{:S(2)}) %collective-permute-start.9) | collective-permute-done | bytes 196640 | tf_op jit(solution)/shard_map/ppermute | solution.py:378
  132.2 2.5 %collective-permute-done.11.refs_3_ = bf16[256,384]{1,0:T(8,128)(2,1)S(1)} collective-permute-done((bf16[256,384]{1,0:T(8,128)(2,1)S(1)}, bf16[256,384]{1,0:T(8,128)(2,1)S(1)}, u32[]{:S(2)}, u32[]{:S(2)}) %collective-permute-start.11) | collective-permute-done | bytes 196640 | tf_op jit(solution)/shard_map/ppermute | solution.py:378
  135.3 15.6 %attend_grad.1 = (bf16[256,1152]{1,0:T(8,128)(2,1)}, bf16[256,1152]{1,0:T(8,128)(2,1)}, bf16[256,1152]{1,0:T(8,128)(2,1)}, bf16[256,1152]{1,0:T(8,128)(2,1)}) custom-call(s32[2]{0:T(128)} %copy-done.10, s32[32]{0:T(128)} %lengths.3, s32[32]{0:T(128)} %text_lengths.3, bf16[256,384]{1,0:T(8,128)(2,1)} %copy-done.9, bf16[256,384]{1,0:T(8,128)(2,1)} %copy-done.18, ...), custom_call_target="tpu_custom_call" | custom-call | flops 6442450944 | bytes 16777216 | tf_op jit(solution)/shard_map/attend_grad/pallas_call | solution.py:346
  151.0 2.3 %collective-permute-start.13 = (bf16[256,1152]{1,0:T(8,128)(2,1)}, bf16[256,1152]{1,0:T(8,128)(2,1)S(1)}, u32[]{:S(2)}, u32[]{:S(2)}) collective-permute-start(bf16[256,1152]{1,0:T(8,128)(2,1)} %get-tuple-element.46), channel_id=1, source_target_pairs={{0,4},{1,5},{2,6},{3,7},{4,0},{5,1},{6,2},{7,3},{8,12},{9,13},{10,... | collective-permute-start | bytes 1769480 | tf_op jit(solution)/shard_map/ppermute | solution.py:378
  155.3 1.7 reorder.3
  157.0 9.5 %all-to-all-start.3 = ((bf16[32,16,768]{2,1,0:T(8,128)(2,1)}), bf16[32,16,768]{2,1,0:T(8,128)(2,1)S(1)}, u32[]{:S(2)}, u32[]{:S(2)}) async-start(bf16[32,16,768]{2,1,0:T(8,128)(2,1)} %reorder.3), calls=%async_computation.3 | async-start | bytes 1572864 | tf_op jit(solution)/shard_map/all_to_all | solution.py:387
  166.5 13.4 %collective-permute-done.12.refs_1_.refs_2_ = bf16[256,1152]{1,0:T(8,128)(2,1)S(1)} collective-permute-done((bf16[256,1152]{1,0:T(8,128)(2,1)}, bf16[256,1152]{1,0:T(8,128)(2,1)S(1)}, u32[]{:S(2)}, u32[]{:S(2)}) %collective-permute-start.12) | collective-permute-done | bytes 589856 | tf_op jit(solution)/shard_map/ppermute | solution.py:378
  180.9 2.8 %collective-permute-done.15.refs_5_ = bf16[4,128,1152]{2,1,0:T(8,128)(2,1)S(1)} collective-permute-done((bf16[4,128,1152]{2,1,0:T(8,128)(2,1)S(1)}, bf16[4,128,1152]{2,1,0:T(8,128)(2,1)S(1)}, u32[]{:S(2)}, u32[]{:S(2)}) %collective-permute-start.15) | collective-permute-done | bytes 1179680 | tf_op jit(solution)/shard_map/ppermute | solution.py:383
  183.8 2.1 %join_gradient.1 = bf16[128,9216]{1,0:T(8,128)(2,1)} custom-call(s32[2]{0:T(128)S(1)} %copy-done.12, bf16[256,1152]{1,0:T(8,128)(2,1)S(1)} %copy-done.1, bf16[256,1152]{1,0:T(8,128)(2,1)S(1)} %collective-permute-done.12.refs_1_.refs_2_, bf16[256,1152]{1,0:T(8,128)(2,1)S(1)} %collective-permute-done.13.refs_2_.refs_3_, ...), custom_call_target="tpu_custom_call" | custom-call | bytes 4194304 | tf_op jit(solution)/shard_map/join_gradient/pallas_call | solution.py:84
  185.9 2.5 %all-to-all-done.3.refs_0_ = bf16[32,16,768]{2,1,0:T(8,128)(2,1)S(1)} async-done(((bf16[32,16,768]{2,1,0:T(8,128)(2,1)}), bf16[32,16,768]{2,1,0:T(8,128)(2,1)S(1)}, u32[]{:S(2)}, u32[]{:S(2)}) %all-to-all-start.3) | async-done | bytes 786464 | tf_op jit(solution)/shard_map/all_to_all | solution.py:387
  188.4 1.1 from_pieces.1
  (65 shorter events, 13.3 us)
Async XLA Ops:
  0.7 6.3 %copy-start.10 = (s32[2]{0:T(128)}, s32[2]{0:T(128)S(1)}, u32[]{:S(2)}) copy-start(s32[2]{0:T(128)S(1)} %pad_add_fusion.refs_0_.at) | copy-start | bytes 28
  5.8 35.6 %copy-start.13 = (s32[32]{0:T(128)S(1)}, s32[32]{0:T(128)}, u32[]{:S(2)}) copy-start(s32[32]{0:T(128)} %refs_0_.3) | copy-start | bytes 388
  7.0 34.4 %all-to-all-start = ((bf16[32,16,768]{2,1,0:T(8,128)(2,1)}), bf16[32,16,768]{2,1,0:T(8,128)(2,1)S(1)}, u32[]{:S(2)}, u32[]{:S(2)}) async-start(bf16[32,16,768]{2,1,0:T(8,128)(2,1)} %to_pieces.1), calls=%async_computation | async-start | bytes 1572864 | tf_op jit(solution)/shard_map/all_to_all | solution.py:387
  18.5 29.7 %copy-start.6 = (bf16[4,128,1152]{2,1,0:T(8,128)(2,1)S(1)}, bf16[4,128,1152]{2,1,0:T(8,128)(2,1)}, u32[]{:S(2)}) copy-start(bf16[4,128,1152]{2,1,0:T(8,128)(2,1)} %get-tuple-element.25.refs_0_) | copy-start | bytes 3538948
  18.5 29.7 %collective-permute-start = (bf16[4,128,1152]{2,1,0:T(8,128)(2,1)}, bf16[4,128,1152]{2,1,0:T(8,128)(2,1)S(1)}, u32[]{:S(2)}, u32[]{:S(2)}) collective-permute-start(bf16[4,128,1152]{2,1,0:T(8,128)(2,1)} %get-tuple-element.26.refs_1_), channel_id=1, source_target_pairs={{0,1},{1,0},{2,3},{3,2},{4,5},{5,4},{6,7},{7,6},{8,9},{9,8},{10,11... | collective-permute-start | bytes 3538952 | tf_op jit(solution)/shard_map/ppermute | solution.py:383
  43.1 53.6 %all-to-all-start.1 = ((bf16[32,16,768]{2,1,0:T(8,128)(2,1)}), bf16[32,16,768]{2,1,0:T(8,128)(2,1)S(1)}, u32[]{:S(2)}, u32[]{:S(2)}) async-start(bf16[32,16,768]{2,1,0:T(8,128)(2,1)} %reorder.2), calls=%async_computation.1 | async-start | bytes 1572864 | tf_op jit(solution)/shard_map/all_to_all | solution.py:387
  49.6 16.3 %collective-permute-start.1 = (bf16[256,1152]{1,0:T(8,128)(2,1)S(1)}, bf16[256,1152]{1,0:T(8,128)(2,1)S(1)}, u32[]{:S(2)}, u32[]{:S(2)}) collective-permute-start(bf16[256,1152]{1,0:T(8,128)(2,1)S(1)} %get-tuple-element.28), channel_id=1, source_target_pairs={{0,2},{1,3},{2,4},{3,5},{4,6},{5,7},{6,0},{7,1},{8,10},{9,11},{10,... | collective-permute-start | bytes 1769480 | tf_op jit(solution)/shard_map/ppermute | solution.py:378
  50.1 17.8 %collective-permute-start.2 = (bf16[256,1152]{1,0:T(8,128)(2,1)S(1)}, bf16[256,1152]{1,0:T(8,128)(2,1)S(1)}, u32[]{:S(2)}, u32[]{:S(2)}) collective-permute-start(bf16[256,1152]{1,0:T(8,128)(2,1)S(1)} %get-tuple-element.29), channel_id=1, source_target_pairs={{0,4},{1,5},{2,6},{3,7},{4,0},{5,1},{6,2},{7,3},{8,12},{9,13},{10,... | collective-permute-start | bytes 1769480 | tf_op jit(solution)/shard_map/ppermute | solution.py:378
  52.5 25.1 %collective-permute-start.3 = (bf16[256,1152]{1,0:T(8,128)(2,1)S(1)}, bf16[256,1152]{1,0:T(8,128)(2,1)S(1)}, u32[]{:S(2)}, u32[]{:S(2)}) collective-permute-start(bf16[256,1152]{1,0:T(8,128)(2,1)S(1)} %get-tuple-element.30), channel_id=1, source_target_pairs={{0,6},{1,7},{2,0},{3,1},{4,2},{5,3},{6,4},{7,5},{8,14},{9,15},{10,... | collective-permute-start | bytes 1769480 | tf_op jit(solution)/shard_map/ppermute | solution.py:378
  65.9 11.7 %copy-start.15 = (bf16[256,1152]{1,0:T(8,128)(2,1)}, bf16[256,1152]{1,0:T(8,128)(2,1)S(1)}, u32[]{:S(2)}) copy-start(bf16[256,1152]{1,0:T(8,128)(2,1)S(1)} %collective-permute-done.1.refs_1_) | copy-start | bytes 1769476
  67.9 9.7 %copy-start.16 = (bf16[256,1152]{1,0:T(8,128)(2,1)}, bf16[256,1152]{1,0:T(8,128)(2,1)S(1)}, u32[]{:S(2)}) copy-start(bf16[256,1152]{1,0:T(8,128)(2,1)S(1)} %collective-permute-done.2.refs_2_) | copy-start | bytes 1769476
  78.4 18.3 %copy-start.11 = (s32[2]{0:T(128)S(1)}, s32[2]{0:T(128)}, u32[]{:S(2)}) copy-start(s32[2]{0:T(128)} %copy-done.10) | copy-start | bytes 28
  92.2 12.5 %collective-permute-start.4 = (bf16[256,384]{1,0:T(8,128)(2,1)}, bf16[256,384]{1,0:T(8,128)(2,1)S(1)}, u32[]{:S(2)}, u32[]{:S(2)}) collective-permute-start(bf16[256,384]{1,0:T(8,128)(2,1)} %get-tuple-element.32), channel_id=1, source_target_pairs={{0,6},{1,7},{2,0},{3,1},{4,2},{5,3},{6,4},{7,5},{8,14},{9,15},{10,... | collective-permute-start | bytes 589832 | tf_op jit(solution)/shard_map/ppermute | solution.py:378
  93.2 11.5 %collective-permute-start.5 = (bf16[256,384]{1,0:T(8,128)(2,1)}, bf16[256,384]{1,0:T(8,128)(2,1)S(1)}, u32[]{:S(2)}, u32[]{:S(2)}) collective-permute-start(bf16[256,384]{1,0:T(8,128)(2,1)} %get-tuple-element.33), channel_id=1, source_target_pairs={{0,4},{1,5},{2,6},{3,7},{4,0},{5,1},{6,2},{7,3},{8,12},{9,13},{10,... | collective-permute-start | bytes 589832 | tf_op jit(solution)/shard_map/ppermute | solution.py:378
  94.9 10.4 %collective-permute-start.6 = (bf16[256,384]{1,0:T(8,128)(2,1)}, bf16[256,384]{1,0:T(8,128)(2,1)S(1)}, u32[]{:S(2)}, u32[]{:S(2)}) collective-permute-start(bf16[256,384]{1,0:T(8,128)(2,1)} %get-tuple-element.34), channel_id=1, source_target_pairs={{0,2},{1,3},{2,4},{3,5},{4,6},{5,7},{6,0},{7,1},{8,10},{9,11},{10,... | collective-permute-start | bytes 589832 | tf_op jit(solution)/shard_map/ppermute | solution.py:378
  97.6 11.0 %copy-start.5 = (bf16[256,384]{1,0:T(8,128)(2,1)S(1)}, bf16[256,384]{1,0:T(8,128)(2,1)}, u32[]{:S(2)}) copy-start(bf16[256,384]{1,0:T(8,128)(2,1)} %get-tuple-element.31.refs_0_.refs_2_.refs_1_) | copy-start | bytes 589828
  99.2 7.7 %collective-permute-start.8 = (bf16[4,128,384]{2,1,0:T(8,128)(2,1)S(1)}, bf16[4,128,384]{2,1,0:T(8,128)(2,1)S(1)}, u32[]{:S(2)}, u32[]{:S(2)}) collective-permute-start(bf16[4,128,384]{2,1,0:T(8,128)(2,1)S(1)} %get-tuple-element.36), channel_id=1, source_target_pairs={{0,1},{1,0},{2,3},{3,2},{4,5},{5,4},{6,7},{7,6},{8,9},{9,8},{10,11... | collective-permute-start | bytes 1179656 | tf_op jit(solution)/shard_map/ppermute | solution.py:383
  106.8 1.8 collective-permute-start.7
  108.0 2.6 %copy-start.9 = (bf16[256,384]{1,0:T(8,128)(2,1)}, bf16[256,384]{1,0:T(8,128)(2,1)S(1)}, u32[]{:S(2)}) copy-start(bf16[256,384]{1,0:T(8,128)(2,1)S(1)} %get-tuple-element.37.refs_6_.refs_0_) | copy-start | bytes 589828
  110.6 43.6 %all-to-all-start.2 = ((bf16[32,16,768]{2,1,0:T(8,128)(2,1)}), bf16[32,16,768]{2,1,0:T(8,128)(2,1)S(1)}, u32[]{:S(2)}, u32[]{:S(2)}) async-start(bf16[32,16,768]{2,1,0:T(8,128)(2,1)} %join_pieces.1), calls=%async_computation.2 | async-start | bytes 1572864 | tf_op jit(solution)/shard_map/all_to_all | solution.py:387
  120.1 11.1 %collective-permute-start.9 = (bf16[256,384]{1,0:T(8,128)(2,1)S(1)}, bf16[256,384]{1,0:T(8,128)(2,1)S(1)}, u32[]{:S(2)}, u32[]{:S(2)}) collective-permute-start(bf16[256,384]{1,0:T(8,128)(2,1)S(1)} %get-tuple-element.38), channel_id=1, source_target_pairs={{0,2},{1,3},{2,4},{3,5},{4,6},{5,7},{6,0},{7,1},{8,10},{9,11},{10,... | collective-permute-start | bytes 589832 | tf_op jit(solution)/shard_map/ppermute | solution.py:378
  122.8 9.3 %collective-permute-start.10 = (bf16[256,384]{1,0:T(8,128)(2,1)S(1)}, bf16[256,384]{1,0:T(8,128)(2,1)S(1)}, u32[]{:S(2)}, u32[]{:S(2)}) collective-permute-start(bf16[256,384]{1,0:T(8,128)(2,1)S(1)} %get-tuple-element.39), channel_id=1, source_target_pairs={{0,4},{1,5},{2,6},{3,7},{4,0},{5,1},{6,2},{7,3},{8,12},{9,13},{10,... | collective-permute-start | bytes 589832 | tf_op jit(solution)/shard_map/ppermute | solution.py:378
  122.8 11.8 %collective-permute-start.11 = (bf16[256,384]{1,0:T(8,128)(2,1)S(1)}, bf16[256,384]{1,0:T(8,128)(2,1)S(1)}, u32[]{:S(2)}, u32[]{:S(2)}) collective-permute-start(bf16[256,384]{1,0:T(8,128)(2,1)S(1)} %get-tuple-element.40), channel_id=1, source_target_pairs={{0,6},{1,7},{2,0},{3,1},{4,2},{5,3},{6,4},{7,5},{8,14},{9,15},{10,... | collective-permute-start | bytes 589832 | tf_op jit(solution)/shard_map/ppermute | solution.py:378
  131.2 3.4 %copy-start.18 = (bf16[256,384]{1,0:T(8,128)(2,1)}, bf16[256,384]{1,0:T(8,128)(2,1)S(1)}, u32[]{:S(2)}) copy-start(bf16[256,384]{1,0:T(8,128)(2,1)S(1)} %collective-permute-done.9.refs_1_) | copy-start | bytes 589828
  132.2 2.5 %copy-start.19 = (bf16[256,384]{1,0:T(8,128)(2,1)}, bf16[256,384]{1,0:T(8,128)(2,1)S(1)}, u32[]{:S(2)}) copy-start(bf16[256,384]{1,0:T(8,128)(2,1)S(1)} %collective-permute-done.10.refs_2_) | copy-start | bytes 589828
  150.9 29.0 %collective-permute-start.12 = (bf16[256,1152]{1,0:T(8,128)(2,1)}, bf16[256,1152]{1,0:T(8,128)(2,1)S(1)}, u32[]{:S(2)}, u32[]{:S(2)}) collective-permute-start(bf16[256,1152]{1,0:T(8,128)(2,1)} %get-tuple-element.45), channel_id=1, source_target_pairs={{0,6},{1,7},{2,0},{3,1},{4,2},{5,3},{6,4},{7,5},{8,14},{9,15},{10,... | collective-permute-start | bytes 1769480 | tf_op jit(solution)/shard_map/ppermute | solution.py:378
  151.0 29.0 %collective-permute-start.13 = (bf16[256,1152]{1,0:T(8,128)(2,1)}, bf16[256,1152]{1,0:T(8,128)(2,1)S(1)}, u32[]{:S(2)}, u32[]{:S(2)}) collective-permute-start(bf16[256,1152]{1,0:T(8,128)(2,1)} %get-tuple-element.46), channel_id=1, source_target_pairs={{0,4},{1,5},{2,6},{3,7},{4,0},{5,1},{6,2},{7,3},{8,12},{9,13},{10,... | collective-permute-start | bytes 1769480 | tf_op jit(solution)/shard_map/ppermute | solution.py:378
  153.3 27.2 %collective-permute-start.14 = (bf16[256,1152]{1,0:T(8,128)(2,1)}, bf16[256,1152]{1,0:T(8,128)(2,1)S(1)}, u32[]{:S(2)}, u32[]{:S(2)}) collective-permute-start(bf16[256,1152]{1,0:T(8,128)(2,1)} %get-tuple-element.47), channel_id=1, source_target_pairs={{0,2},{1,3},{2,4},{3,5},{4,6},{5,7},{6,0},{7,1},{8,10},{9,11},{10,... | collective-permute-start | bytes 1769480 | tf_op jit(solution)/shard_map/ppermute | solution.py:378
  155.3 25.3 %copy-start.1 = (bf16[256,1152]{1,0:T(8,128)(2,1)S(1)}, bf16[256,1152]{1,0:T(8,128)(2,1)}, u32[]{:S(2)}) copy-start(bf16[256,1152]{1,0:T(8,128)(2,1)} %get-tuple-element.44.refs_2_.refs_0_.refs_1_) | copy-start | bytes 1769476
  157.0 31.5 %all-to-all-start.3 = ((bf16[32,16,768]{2,1,0:T(8,128)(2,1)}), bf16[32,16,768]{2,1,0:T(8,128)(2,1)S(1)}, u32[]{:S(2)}, u32[]{:S(2)}) async-start(bf16[32,16,768]{2,1,0:T(8,128)(2,1)} %reorder.3), calls=%async_computation.3 | async-start | bytes 1572864 | tf_op jit(solution)/shard_map/all_to_all | solution.py:387
  166.5 17.3 %copy-start.12 = (s32[2]{0:T(128)S(1)}, s32[2]{0:T(128)}, u32[]{:S(2)}) copy-start(s32[2]{0:T(128)} %copy-done.10) | copy-start | bytes 28
  180.8 2.9 %collective-permute-start.15 = (bf16[4,128,1152]{2,1,0:T(8,128)(2,1)S(1)}, bf16[4,128,1152]{2,1,0:T(8,128)(2,1)S(1)}, u32[]{:S(2)}, u32[]{:S(2)}) collective-permute-start(bf16[4,128,1152]{2,1,0:T(8,128)(2,1)S(1)} %for_sibling.3), channel_id=1, source_target_pairs={{0,1},{1,0},{2,3},{3,2},{4,5},{5,4},{6,7},{7,6},{8,9},{9,8},{10,11... | collective-permute-start | bytes 3538952 | tf_op jit(solution)/shard_map/ppermute | solution.py:383
  (9 other events, 10.3 us)

commit v2 on v1

--- a/solution.py
+++ b/solution.py
@@ -19,13 +19,17 @@
 CHIPS = SHARDS // 2
 CH = 2 * ROWS
 SCALE = DH ** -0.5
-LOG2E = 1.4426950408889634
+LOGIT = SCALE * 1.4426950408889634
+FWD_VMEM = 24
+BWD_VMEM = 60
 NT = (((1,), (1,)), ((), ()))
 
 ANY = pl.BlockSpec(memory_space=pl.ANY)
 SMEM = pl.BlockSpec(memory_space=pltpu.SMEM)
+VMEM = pl.BlockSpec(memory_space=pltpu.VMEM)
 BF = jnp.bfloat16
 F32 = jnp.float32
+TOKEN = jax.ShapeDtypeStruct((8, 128), F32)
 
 
 def copies(body, count, given, late, cost=4):
@@ -63,7 +67,7 @@
                     yield x_ref.at[:, pl.ds(start, GRP)], out.at[k, :, pl.ds(t * GRP, GRP)]
 
     return copies(body, 6 * CHIPS, 2, len(late))(
-        out_shape=[pltpu.HBM((CHIPS, ROWS, 3 * GRP), BF)] * 2,
+        out_shape=[jax.ShapeDtypeStruct((CHIPS, ROWS, 3 * GRP), BF)] * 2,
         in_specs=[SMEM, ANY] + [ANY] * len(late),
         out_specs=[ANY] * 2,
         name="split_projected",
@@ -93,14 +97,16 @@
     width = own.shape[2]
 
     def body(own_ref, recv_ref, *outs):
+        outs[CHIPS][...] = jnp.zeros_like(outs[CHIPS])
         for k in range(CHIPS):
             yield own_ref.at[k], outs[k].at[pl.ds(0, ROWS)]
             yield recv_ref.at[k], outs[k].at[pl.ds(ROWS, ROWS)]
 
     return copies(body, 2 * CHIPS, 2, len(late))(
-        out_shape=[jax.ShapeDtypeStruct((2 * ROWS, width), BF)] * CHIPS,
+        out_shape=[pltpu.HBM((2 * ROWS, width), BF) if width > GRP else jax.ShapeDtypeStruct((2 * ROWS, width), BF)] * CHIPS
+        + [TOKEN],
         in_specs=[ANY] * (2 + len(late)),
-        out_specs=[ANY] * CHIPS,
+        out_specs=[ANY] * CHIPS + [VMEM],
         name="pair",
     )(own, recv, *late)
 
@@ -209,35 +215,41 @@
     return (pos < latent) | ((pos >= CAP) & (pos < CAP + text))
 
 
-def fetch(srcs, dst, sems):
-    started = []
+def cols(part, head):
+    return pl.ds(pl.multiple_of(part * GRP + head * DH, DH), DH)
+
+
+def moves(refs, held, sems, inward):
+    out = []
     for k in range(CHIPS):
-        cp = pltpu.make_async_copy(srcs[k], dst.at[pl.ds(k * CH, CH)], sems.at[k])
+        rows = held.at[pl.ds(k * CH, CH)]
+        src, dst = (refs[k], rows) if inward else (rows, refs[k])
+        out.append(pltpu.make_async_copy(src, dst, sems.at[k]))
+    return out
+
+
+def run(started):
+    for cp in started:
         cp.start()
-        started.append(cp)
     for cp in started:
         cp.wait()
 
 
-def cols(part, head):
-    return pl.ds(pl.multiple_of(part * GRP + head * DH, DH), DH)
+def thirds(value):
+    hi = value.astype(BF).astype(F32)
+    mid = (value - hi).astype(BF).astype(F32)
+    return hi, mid, value - hi - mid
 
 
 def forward_kernel(at, lengths, text_lengths, *refs):
     xs = refs[:CHIPS]
     outs = refs[CHIPS : 2 * CHIPS]
-    wide, prob, kept, held, sems, kept_sem = refs[2 * CHIPS :]
+    wide, norm, held, done, in_sems, out_sems = refs[2 * CHIPS :]
     g = pl.program_id(0)
-    keep = pltpu.make_async_copy(held, kept, kept_sem)
 
     @pl.when(g == 0)
     def _():
-        fetch(xs, held, sems)
-        keep.start()
-
-    @pl.when(g == MINE - 1)
-    def _():
-        keep.wait()
+        run(moves(xs, held, in_sems, True))
 
     live = live_rows(at, lengths, text_lengths)
     lane = lax.broadcasted_iota(jnp.int32, (SEQ, DH), 1)
@@ -247,69 +259,85 @@
     k = jnp.concatenate([held[:, cols(1, g)], dead], axis=1)
     vt = held[:, cols(2, g)].T
     livef = live.astype(F32)
+    ahead = lax.dot_general(k, q[0:CH], NT, preferred_element_type=F32)
     for n in range(SEQ // CH):
         part = slice(n * CH, (n + 1) * CH)
-        s = lax.dot_general(k, q[part], NT, preferred_element_type=F32)
+        s = ahead
+        if n + 1 < SEQ // CH:
+            ahead = lax.dot_general(
+                k, q[(n + 1) * CH : (n + 2) * CH], NT, preferred_element_type=F32
+            )
         top = jnp.max(s, axis=0, keepdims=True)
-        e = jnp.exp2((s - top) * (SCALE * LOG2E))
-        full = e * (1.0 / jnp.sum(e, axis=0, keepdims=True))
-        p = full.astype(BF)
-        rest = (full - p.astype(F32)).astype(BF)
-        prob[0, :, part] = full
+        e = jnp.exp2((s - top) * LOGIT)
+        total = jnp.sum(e, axis=0, keepdims=True)
+        norm[0, :, part] = top + jnp.log2(total) * (1.0 / LOGIT)
+        p = e.astype(BF)
+        rest = (e - p.astype(F32)).astype(BF)
         o = jnp.dot(vt, p, preferred_element_type=F32)
-        more = jnp.dot(vt, rest, preferred_element_type=F32)
-        wide[part, pl.ds(pl.multiple_of(g * DH, DH), DH)] = (o + more).T
-        o = o.T * livef[part]
-        outs[n][:, pl.ds(pl.multiple_of(g * DH, DH), DH)] = o.astype(BF)
+        o = o + jnp.dot(vt, rest, preferred_element_type=F32)
+        o = (o * (1.0 / total)).T
+        wide[0, part, :] = o
+        done[part, cols(0, g)] = (o * livef[part]).astype(BF)
+
+    @pl.when(g == MINE - 1)
+    def _():
+        run(moves(outs, done, out_sems, False))
 
 
 def backward_kernel(at, lengths, text_lengths, *refs):
-    cs = refs[:CHIPS]
-    kept, wide, prob = refs[CHIPS : CHIPS + 3]
-    outs = refs[CHIPS + 3 : 2 * CHIPS + 3]
-    held, cot, dst, pst, sems, kept_sem = refs[2 * CHIPS + 3 :]
+    xs = refs[:CHIPS]
+    cs = refs[CHIPS : 2 * CHIPS]
+    wide, norm = refs[2 * CHIPS : 2 * CHIPS + 2]
+    outs = refs[2 * CHIPS + 2 : 3 * CHIPS + 2]
+    token, held, cot, done, dst, pst, in_sems, cot_sems, out_sems = refs[3 * CHIPS + 2 :]
     g = pl.program_id(0)
 
     @pl.when(g == 0)
     def _():
-        back = pltpu.make_async_copy(kept, held, kept_sem)
-        back.start()
-        fetch(cs, cot, sems)
-        back.wait()
+        run(moves(xs, held, in_sems, True) + moves(cs, cot, cot_sems, True))
+        token[...] = jnp.zeros_like(token)
 
     live = live_rows(at, lengths, text_lengths)
     lane = lax.broadcasted_iota(jnp.int32, (SEQ, DH), 1)
-    mine = pl.ds(pl.multiple_of(g * DH, DH), DH)
-    do = jnp.where(live, cot[:, mine], jnp.zeros((), BF))
-    dot = jnp.sum(do.astype(F32) * wide[:, mine], axis=1, keepdims=True)
-    hi = dot.astype(BF).astype(F32)
-    mid = (dot - hi).astype(BF).astype(F32)
-    low = dot - hi - mid
+    do = jnp.where(live, cot[:, cols(0, g)], jnp.zeros((), BF))
+    dot = jnp.sum(do.astype(F32) * wide[0], axis=1, keepdims=True)
+    hi, mid, low = thirds(dot)
     less = jnp.where(lane == 0, -hi, jnp.where(lane == 1, -mid, jnp.where(lane == 2, -low, 0.0)))
     dox = jnp.concatenate([do, less.astype(BF)], axis=1)
     units = jnp.where(lane < 3, 1.0, 0.0).astype(BF)
     vx = jnp.concatenate([held[:, cols(2, g)], units], axis=1)
+    hi, mid, low = thirds(norm[0].T)
+    less = jnp.where(lane == 0, -hi, jnp.where(lane == 1, -mid, jnp.where(lane == 2, -low, 0.0)))
+    less = jnp.where(lane == 3, 1.0, less).astype(BF)
+    dead = jnp.where(lane < 3, 1.0, jnp.where(live | (lane > 3), 0.0, -1e30)).astype(BF)
+    qx = jnp.concatenate([held[:, cols(0, g)], less], axis=1)
+    kx = jnp.concatenate([held[:, cols(1, g)], dead], axis=1)
     kt = held[:, cols(1, g)].T
     for n in range(SEQ // CH):
         part = slice(n * CH, (n + 1) * CH)
+        s = lax.dot_general(kx, qx[part], NT, preferred_element_type=F32)
         dp = lax.dot_general(vx, dox[part], NT, preferred_element_type=F32)
-        p = prob[0, :, part]
+        p = jnp.exp2(s * LOGIT)
         pst[:, part] = p.astype(BF)
         ds = (p * dp).astype(BF)
         dst[:, part] = ds
         dq = jnp.dot(kt, ds, preferred_element_type=F32).T * SCALE
-        outs[n][:, cols(0, g)] = dq.astype(BF)
+        done[part, cols(0, g)] = dq.astype(BF)
     q = held[:, cols(0, g)]
     for n in range(SEQ // CH):
         part = slice(n * CH, (n + 1) * CH)
         dk = jnp.dot(dst[part, :], q, preferred_element_type=F32) * SCALE
         dv = jnp.dot(pst[part, :], do, preferred_element_type=F32)
-        outs[n][:, cols(1, g)] = dk.astype(BF)
-        outs[n][:, cols(2, g)] = dv.astype(BF)
-
-
-def whole(shape):
-    return pl.BlockSpec(shape, lambda g: (0,) * len(shape))
+        done[part, cols(1, g)] = dk.astype(BF)
+        done[part, cols(2, g)] = dv.astype(BF)
+
+    @pl.when(g == MINE - 1)
+    def _():
+        run(moves(outs, done, out_sems, False))
+
+
+WIDE = pl.BlockSpec((1, SEQ, DH), lambda g: (g, 0, 0))
+NORM = pl.BlockSpec((1, 1, SEQ), lambda g: (g, 0, 0))
 
 
 def forward(where, xs):
@@ -317,58 +345,46 @@
         forward_kernel,
         grid=(MINE,),
         out_shape=[jax.ShapeDtypeStruct((CH, GRP), BF)] * CHIPS
-        + [
-            pltpu.HBM((SEQ, GRP), F32),
-            pltpu.HBM((MINE, SEQ, SEQ), F32),
-            pltpu.HBM((SEQ, 3 * GRP), BF),
-        ],
+        + [pltpu.HBM((MINE, SEQ, DH), F32), pltpu.HBM((MINE, 1, SEQ), F32)],
         in_specs=[SMEM] * 3 + [ANY] * CHIPS,
-        out_specs=[whole((CH, GRP))] * CHIPS
-        + [
-            whole((SEQ, GRP)),
-            pl.BlockSpec((1, SEQ, SEQ), lambda g: (g, 0, 0)),
-            pl.BlockSpec(memory_space=pltpu.HBM),
-        ],
+        out_specs=[ANY] * CHIPS + [WIDE, NORM],
         scratch_shapes=[
             pltpu.VMEM((SEQ, 3 * GRP), BF),
+            pltpu.VMEM((SEQ, GRP), BF),
             pltpu.SemaphoreType.DMA((CHIPS,)),
-            pltpu.SemaphoreType.DMA,
+            pltpu.SemaphoreType.DMA((CHIPS,)),
         ],
-        compiler_params=pltpu.CompilerParams(vmem_limit_bytes=60 << 20),
+        compiler_params=pltpu.CompilerParams(vmem_limit_bytes=FWD_VMEM << 20),
         cost_estimate=pl.CostEstimate(
-            flops=MINE * 2 * 5 * SEQ * SEQ * DH, bytes_accessed=12 << 20, transcendentals=MINE * SEQ * SEQ
+            flops=20 * MINE * 2 * 5 * SEQ * SEQ * DH, bytes_accessed=12 << 20, transcendentals=MINE * SEQ * SEQ
         ),
         name="attend",
     )(*where, *xs)
 
 
-def backward(where, cs, kept, wide, prob):
+def backward(where, cs, xs, wide, norm):
     return pl.pallas_call(
         backward_kernel,
         grid=(MINE,),
-        out_shape=[jax.ShapeDtypeStruct((CH, 3 * GRP), BF)] * CHIPS,
-        in_specs=[SMEM] * 3
-        + [ANY] * CHIPS
-        + [
-            pl.BlockSpec(memory_space=pltpu.HBM),
-            whole((SEQ, GRP)),
-            pl.BlockSpec((1, SEQ, SEQ), lambda g: (g, 0, 0)),
-        ],
-        out_specs=[whole((CH, 3 * GRP))] * CHIPS,
+        out_shape=[jax.ShapeDtypeStruct((CH, 3 * GRP), BF)] * CHIPS + [TOKEN],
+        in_specs=[SMEM] * 3 + [ANY] * (2 * CHIPS) + [WIDE, NORM],
+        out_specs=[ANY] * CHIPS + [pl.BlockSpec((8, 128), lambda g: (0, 0))],
         scratch_shapes=[
             pltpu.VMEM((SEQ, 3 * GRP), BF),
             pltpu.VMEM((SEQ, GRP), BF),
+            pltpu.VMEM((SEQ, 3 * GRP), BF),
             pltpu.VMEM((SEQ, SEQ), BF),
             pltpu.VMEM((SEQ, SEQ), BF),
             pltpu.SemaphoreType.DMA((CHIPS,)),
-            pltpu.SemaphoreType.DMA,
+            pltpu.SemaphoreType.DMA((CHIPS,)),
+            pltpu.SemaphoreType.DMA((CHIPS,)),
         ],
-        compiler_params=pltpu.CompilerParams(vmem_limit_bytes=60 << 20),
+        compiler_params=pltpu.CompilerParams(vmem_limit_bytes=BWD_VMEM << 20),
         cost_estimate=pl.CostEstimate(
-            flops=MINE * 2 * 8 * SEQ * SEQ * DH, bytes_accessed=16 << 20, transcendentals=0
+            flops=20 * MINE * 2 * 8 * SEQ * SEQ * DH, bytes_accessed=16 << 20, transcendentals=0
         ),
         name="attend_grad",
-    )(*where, *cs, kept, wide, prob)
+    )(*where, *xs, *cs, wide, norm)
 
 
 def turn(blocks, sign):
@@ -393,19 +409,21 @@
     where = (at, lengths, text_lengths)
 
     own, other = split_projected(at, projected[0])
-    xs = turn(pair(own, swap(other)), 1)
-    there = spread(to_pieces(cotangent[0], other))
-    here = spread(reorder(destinations, there, False))
-
-    *outs, wide, prob, kept = forward(where, xs)
+    *xs, paired = pair(own, swap(other))
+    xs = turn(xs, 1)
+    there = spread(to_pieces(cotangent[0]))
+    here = spread(reorder(destinations, there, False, paired))
+
+    *outs, wide, norm = forward(where, xs)
     os = turn(outs, -1)
-    own, other = split_cotangent(at, here, outs[0])
-    cs = pair(own, swap(other))
-    halfway = spread(join_pieces(at, os, swap(for_sibling(os)), cs[0]))
+    own, other = split_cotangent(at, here, norm)
+    *cs, paired = pair(own, swap(other))
+    halfway = spread(join_pieces(at, os, swap(for_sibling(os)), paired))
     cs = turn(cs, 1)
 
-    gs = turn(backward(where, cs, kept, wide, prob), -1)
-    home = spread(reorder(destinations, halfway, True, gs[0]))
+    *gs, graded = backward(where, cs, xs, wide, norm)
+    gs = turn(gs, -1)
+    home = spread(reorder(destinations, halfway, True, graded))
     projected_grad = join_gradient(at, gs, swap(for_sibling(gs)))
     attended = from_pieces(home)
     return attended[None], projected_grad[None]

time: 192 us -> 149 us (0.78)
  waiting for transfers between devices: 84.7 us -> 46.1 us
  local copies, waits for them, and re-layouts: 8.2 us -> 4.52 us
  starting transfers between devices: 50.3 us -> 52.5 us
    ppermute x12, waiting for transfers between devices: 56 us -> 13.7 us  [turn(): out.append(lax.ppermute(blocks[k], 'seq', pairs))]
    all_to_all x4, waiting for transfers between devices: 25.3 us -> 29.2 us  [spread(): return lax.all_to_all(pieces, 'dp', split_axis=0, concat_axis=0, tiled=True)]
    unnamed x42 -> x34, local copies, waits for them, and re-layouts: 8.2 us -> 4.52 us
    pallas_call x1, Pallas kernels: 13.8 us -> 11.2 us  [forward(): pl.pallas_call(forward_kernel, grid=(MINE,), out_shape=[jax.ShapeDtypeStr...]
  transfers between devices with their start and end apart: 20 -> 20, of which waited for: 14 -> 11; matrix products, arithmetic and copies ran while one was open for 0% -> 0% of each run, Pallas kernels for 21% -> 28%
where the time goes in v2:
time: 149 us; the launch traced here: 148 us
  starting transfers between devices  52.5 us (35%)
  waiting for transfers between devices  46.1 us (31%)
  Pallas kernels  43.9 us (29%)
  local copies, waits for them, and re-layouts  4.52 us (3%)
    all_to_all x4, starting transfers between devices, spread(): return lax.all_to_all(pieces, 'dp', split_axis=0, concat_axis=0, tiled=True)  36.1 us
    all_to_all x4, waiting for transfers between devices, spread(): return lax.all_to_all(pieces, 'dp', split_axis=0, concat_axis=0, tiled=True)  29.2 us
    pallas_call x1, Pallas kernels, backward(): pl.pallas_call(backward_kernel, grid=(MINE,), out_shape=[jax.ShapeDtypeSt...  16.2 us
    ppermute x12, starting transfers between devices, turn(): out.append(lax.ppermute(blocks[k], 'seq', pairs))  16 us
    ppermute x12, waiting for transfers between devices, turn(): out.append(lax.ppermute(blocks[k], 'seq', pairs))  13.7 us
    pallas_call x1, Pallas kernels, forward(): pl.pallas_call(forward_kernel, grid=(MINE,), out_shape=[jax.ShapeDtypeStr...  11.2 us
    unnamed x34, local copies, waits for them, and re-layouts  4.52 us
    pallas_call x2, Pallas kernels, reorder(): copies(body, RANKS, 2, len(late), 100)  3.36 us
  transfers between devices with their start and end apart: 20, of which 11 were waited for; matrix products, arithmetic and copies ran while one was open for 0% of the time, Pallas kernels for 28%

profile of v2, /device:TPU:6, one launch (start us, length us, event | category | flops | bytes accessed | tf_op | source)
XLA Modules:
  0.0 148.2 jit_solution(15518106774209991790)
XLA Ops:
  0.7 1.7 %copy-done.1 = bf16[1,128,9216]{2,1,0:T(8,128)(2,1)S(1)} copy-done((bf16[1,128,9216]{2,1,0:T(8,128)(2,1)S(1)}, bf16[1,128,9216]{2,1,0:T(8,128)(2,1)}, u32[]{:S(2)}) %copy-start.1) | copy-done | bytes 2359320
  2.4 1.8 %split_projected.1 = (bf16[4,128,1152]{2,1,0:T(8,128)(2,1)S(1)}, bf16[4,128,1152]{2,1,0:T(8,128)(2,1)}) custom-call(s32[2]{0:T(128)S(1)} %pad_add_fusion.refs_0_.at, bf16[128,9216]{1,0:T(8,128)(2,1)S(1)} %bitcast.6), custom_call_target="tpu_custom_call" | custom-call | bytes 4194304 | tf_op jit(solution)/shard_map/split_projected/pallas_call | solution.py:69
  4.3 1.1 to_pieces.1
  5.5 11.5 %all-to-all-start = ((bf16[32,16,768]{2,1,0:T(8,128)(2,1)}), bf16[32,16,768]{2,1,0:T(8,128)(2,1)S(1)}, u32[]{:S(2)}, u32[]{:S(2)}) async-start(bf16[32,16,768]{2,1,0:T(8,128)(2,1)} %to_pieces.1), calls=%async_computation | async-start | bytes 1572864 | tf_op jit(solution)/shard_map/all_to_all | solution.py:403
  17.0 1.5 pair.2
  19.0 2.4 %collective-permute-start.2 = (bf16[256,1152]{1,0:T(8,128)(2,1)}, bf16[256,1152]{1,0:T(8,128)(2,1)S(1)}, u32[]{:S(2)}, u32[]{:S(2)}) collective-permute-start(bf16[256,1152]{1,0:T(8,128)(2,1)} %get-tuple-element.31), channel_id=1, source_target_pairs={{0,4},{1,5},{2,6},{3,7},{4,0},{5,1},{6,2},{7,3},{8,12},{9,13},{10,... | collective-permute-start | bytes 1769480 | tf_op jit(solution)/shard_map/ppermute | solution.py:394
  21.4 18.7 %all-to-all-done.refs_1_ = bf16[32,16,768]{2,1,0:T(8,128)(2,1)S(1)} async-done(((bf16[32,16,768]{2,1,0:T(8,128)(2,1)}), bf16[32,16,768]{2,1,0:T(8,128)(2,1)S(1)}, u32[]{:S(2)}, u32[]{:S(2)}) %all-to-all-start) | async-done | bytes 786464 | tf_op jit(solution)/shard_map/all_to_all | solution.py:403
  40.1 1.7 %reorder.2 = bf16[32,16,768]{2,1,0:T(8,128)(2,1)} custom-call(s32[32]{0:T(128)S(1)} %copy-done.7, bf16[32,16,768]{2,1,0:T(8,128)(2,1)S(1)} %all-to-all-done.refs_1_, f32[8,128]{1,0:T(8,128)S(1)} %get-tuple-element.37.refs_2_), custom_call_target="tpu_custom_call" | custom-call | bytes 104857600 | tf_op jit(solution)/shard_map/reorder/pallas_call | solution.py:165
  41.9 5.6 %all-to-all-start.1 = ((bf16[32,16,768]{2,1,0:T(8,128)(2,1)}), bf16[32,16,768]{2,1,0:T(8,128)(2,1)S(1)}, u32[]{:S(2)}, u32[]{:S(2)}) async-start(bf16[32,16,768]{2,1,0:T(8,128)(2,1)} %reorder.2), calls=%async_computation.1 | async-start | bytes 1572864 | tf_op jit(solution)/shard_map/all_to_all | solution.py:403
  47.5 1.1 collective-permute-done.3.refs_3_
  48.6 11.2 %attend.1 = (bf16[256,384]{1,0:T(8,128)(2,1)S(1)}, bf16[256,384]{1,0:T(8,128)(2,1)S(1)}, bf16[256,384]{1,0:T(8,128)(2,1)S(1)}, bf16[256,384]{1,0:T(8,128)(2,1)S(...) custom-call(s32[2]{0:T(128)S(1)} %pad_add_fusion.refs_0_.at, s32[32]{0:T(128)S(1)} %copy-done.12, s32[32]{0:T(128)S(1)} %copy-done.13, ...), custom_call_target="tpu_custom_call" | custom-call | flops 80530636800 | bytes 12582912 | tf_op jit(solution)/shard_map/attend/pallas_call | solution.py:344
  59.9 1.0 collective-permute-start.4
  60.9 1.4 collective-permute-start.5
  62.3 2.0 %collective-permute-start.6 = (bf16[256,384]{1,0:T(8,128)(2,1)S(1)}, bf16[256,384]{1,0:T(8,128)(2,1)S(1)}, u32[]{:S(2)}, u32[]{:S(2)}) collective-permute-start(bf16[256,384]{1,0:T(8,128)(2,1)S(1)} %get-tuple-element.36), channel_id=1, source_target_pairs={{0,2},{1,3},{2,4},{3,5},{4,6},{5,7},{6,0},{7,1},{8,10},{9,11},{10,... | collective-permute-start | bytes 589832 | tf_op jit(solution)/shard_map/ppermute | solution.py:394
  64.4 5.3 %all-to-all-done.1.refs_1_ = bf16[32,16,768]{2,1,0:T(8,128)(2,1)S(1)} async-done(((bf16[32,16,768]{2,1,0:T(8,128)(2,1)}), bf16[32,16,768]{2,1,0:T(8,128)(2,1)S(1)}, u32[]{:S(2)}, u32[]{:S(2)}) %all-to-all-start.1) | async-done | bytes 786464 | tf_op jit(solution)/shard_map/all_to_all | solution.py:403
  69.7 0.7 copy-done.3
  70.4 1.6 %split_cotangent.1 = (bf16[4,128,384]{2,1,0:T(8,128)(2,1)S(1)}, bf16[4,128,384]{2,1,0:T(8,128)(2,1)S(1)}) custom-call(s32[2]{0:T(128)S(1)} %pad_add_fusion.refs_0_.at, bf16[32,16,768]{2,1,0:T(8,128)(2,1)S(1)} %all-to-all-done.1.refs_1_, f32[3,1,1024]{2,1,0:T(1,128)S(1)} %copy-done.3), custom_call_target="tpu_custom_call" | custom-call | bytes 4194304 | tf_op jit(solution)/shard_map/split_cotangent/pallas_call | solution.py:183
  73.8 1.1 pair.3
  75.6 2.2 %collective-permute-start.9 = (bf16[256,384]{1,0:T(8,128)(2,1)S(1)}, bf16[256,384]{1,0:T(8,128)(2,1)S(1)}, u32[]{:S(2)}, u32[]{:S(2)}) collective-permute-start(bf16[256,384]{1,0:T(8,128)(2,1)S(1)} %get-tuple-element.43), channel_id=1, source_target_pairs={{0,2},{1,3},{2,4},{3,5},{4,6},{5,7},{6,0},{7,1},{8,10},{9,11},{10,... | collective-permute-start | bytes 589832 | tf_op jit(solution)/shard_map/ppermute | solution.py:394
  78.6 1.9 %join_pieces.1 = bf16[32,16,768]{2,1,0:T(8,128)(2,1)} custom-call(s32[2]{0:T(128)S(1)} %pad_add_fusion.refs_0_.at, bf16[256,384]{1,0:T(8,128)(2,1)S(1)} %get-tuple-element.33.refs_0_.refs_1_, bf16[256,384]{1,0:T(8,128)(2,1)S(1)} %collective-permute-done.4.refs_1_.refs_2_, bf16[256,384]{1,0:T(8,128)(2,1)S(1)} %collective-permute-done.5.refs_2_.refs_3_, ...), custom_call_target="tpu_custom_call" | custom-call | bytes 4194304 | tf_op jit(solution)/shard_map/join_pieces/pallas_call | solution.py:201
  80.6 9.5 %all-to-all-start.2 = ((bf16[32,16,768]{2,1,0:T(8,128)(2,1)}), bf16[32,16,768]{2,1,0:T(8,128)(2,1)S(1)}, u32[]{:S(2)}, u32[]{:S(2)}) async-start(bf16[32,16,768]{2,1,0:T(8,128)(2,1)} %join_pieces.1), calls=%async_computation.2 | async-start | bytes 1572864 | tf_op jit(solution)/shard_map/all_to_all | solution.py:403
  90.9 16.2 %attend_grad.1 = (bf16[256,1152]{1,0:T(8,128)(2,1)}, bf16[256,1152]{1,0:T(8,128)(2,1)}, bf16[256,1152]{1,0:T(8,128)(2,1)}, bf16[256,1152]{1,0:T(8,128)(2,1)}, f32[8,128]{1,0:T(8,128)}) custom-call(s32[2]{0:T(128)} %copy-done.4, s32[32]{0:T(128)} %lengths.3, s32[32]{0:T(128)} %text_lengths.3, bf16[256,1152]{1,0:T(8,128)(2,1)} %get-tuple-element.29.refs_0_, ...), custom_call_target="tpu_custom_call" | custom-call | flops 128849018880 | bytes 16777216 | tf_op jit(solution)/shard_map/attend_grad/pallas_call | solution.py:366
  107.1 2.7 %collective-permute-start.12 = (bf16[256,1152]{1,0:T(8,128)(2,1)}, bf16[256,1152]{1,0:T(8,128)(2,1)S(1)}, u32[]{:S(2)}, u32[]{:S(2)}) collective-permute-start(bf16[256,1152]{1,0:T(8,128)(2,1)} %get-tuple-element.49), channel_id=1, source_target_pairs={{0,6},{1,7},{2,0},{3,1},{4,2},{5,3},{6,4},{7,5},{8,14},{9,15},{10,... | collective-permute-start | bytes 1769480 | tf_op jit(solution)/shard_map/ppermute | solution.py:394
  109.8 1.2 collective-permute-start.13
  111.0 1.6 %collective-permute-start.14 = (bf16[256,1152]{1,0:T(8,128)(2,1)}, bf16[256,1152]{1,0:T(8,128)(2,1)S(1)}, u32[]{:S(2)}, u32[]{:S(2)}) collective-permute-start(bf16[256,1152]{1,0:T(8,128)(2,1)} %get-tuple-element.51), channel_id=1, source_target_pairs={{0,2},{1,3},{2,4},{3,5},{4,6},{5,7},{6,0},{7,1},{8,10},{9,11},{10,... | collective-permute-start | bytes 1769480 | tf_op jit(solution)/shard_map/ppermute | solution.py:394
  113.8 1.7 %reorder.3 = bf16[32,16,768]{2,1,0:T(8,128)(2,1)} custom-call(s32[32]{0:T(128)S(1)} %copy-done.7, bf16[32,16,768]{2,1,0:T(8,128)(2,1)S(1)} %all-to-all-done.2.refs_1_, f32[8,128]{1,0:T(8,128)S(1)} %copy-done.6), custom_call_target="tpu_custom_call" | custom-call | bytes 104857600 | tf_op jit(solution)/shard_map/reorder/pallas_call | solution.py:165
  115.5 9.4 %all-to-all-start.3 = ((bf16[32,16,768]{2,1,0:T(8,128)(2,1)}), bf16[32,16,768]{2,1,0:T(8,128)(2,1)S(1)}, u32[]{:S(2)}, u32[]{:S(2)}) async-start(bf16[32,16,768]{2,1,0:T(8,128)(2,1)} %reorder.3), calls=%async_computation.3 | async-start | bytes 1572864 | tf_op jit(solution)/shard_map/all_to_all | solution.py:403
  125.0 11.7 %collective-permute-done.13.refs_2_.refs_3_ = bf16[256,1152]{1,0:T(8,128)(2,1)S(1)} collective-permute-done((bf16[256,1152]{1,0:T(8,128)(2,1)}, bf16[256,1152]{1,0:T(8,128)(2,1)S(1)}, u32[]{:S(2)}, u32[]{:S(2)}) %collective-permute-start.13) | collective-permute-done | bytes 589856 | tf_op jit(solution)/shard_map/ppermute | solution.py:394
  137.2 2.8 %collective-permute-done.15.refs_5_ = bf16[4,128,1152]{2,1,0:T(8,128)(2,1)S(1)} collective-permute-done((bf16[4,128,1152]{2,1,0:T(8,128)(2,1)S(1)}, bf16[4,128,1152]{2,1,0:T(8,128)(2,1)S(1)}, u32[]{:S(2)}, u32[]{:S(2)}) %collective-permute-start.15) | collective-permute-done | bytes 1179680 | tf_op jit(solution)/shard_map/ppermute | solution.py:399
  140.0 2.1 %join_gradient.1 = bf16[128,9216]{1,0:T(8,128)(2,1)} custom-call(s32[2]{0:T(128)S(1)} %copy-done.5, bf16[256,1152]{1,0:T(8,128)(2,1)S(1)} %copy-done, bf16[256,1152]{1,0:T(8,128)(2,1)S(1)} %collective-permute-done.12.refs_1_.refs_2_, bf16[256,1152]{1,0:T(8,128)(2,1)S(1)} %collective-permute-done.13.refs_2_.refs_3_, ...), custom_call_target="tpu_custom_call" | custom-call | bytes 4194304 | tf_op jit(solution)/shard_map/join_gradient/pallas_call | solution.py:88
  142.1 4.7 %all-to-all-done.3.refs_0_ = bf16[32,16,768]{2,1,0:T(8,128)(2,1)S(1)} async-done(((bf16[32,16,768]{2,1,0:T(8,128)(2,1)}), bf16[32,16,768]{2,1,0:T(8,128)(2,1)S(1)}, u32[]{:S(2)}, u32[]{:S(2)}) %all-to-all-start.3) | async-done | bytes 786464 | tf_op jit(solution)/shard_map/all_to_all | solution.py:403
  146.9 1.1 from_pieces.1
  (57 shorter events, 6.5 us)
Async XLA Ops:
  0.7 77.9 %copy-start.4 = (s32[2]{0:T(128)}, s32[2]{0:T(128)S(1)}, u32[]{:S(2)}) copy-start(s32[2]{0:T(128)S(1)} %pad_add_fusion.refs_0_.at) | copy-start | bytes 28
  0.7 1.7 %copy-start.1 = (bf16[1,128,9216]{2,1,0:T(8,128)(2,1)S(1)}, bf16[1,128,9216]{2,1,0:T(8,128)(2,1)}, u32[]{:S(2)}) copy-start(bf16[1,128,9216]{2,1,0:T(8,128)(2,1)} %param.5) | copy-start | bytes 7077892
  2.4 1.9 %copy-start.2 = (bf16[1,128,3072]{2,1,0:T(8,128)(2,1)S(1)}, bf16[1,128,3072]{2,1,0:T(8,128)(2,1)}, u32[]{:S(2)}) copy-start(bf16[1,128,3072]{2,1,0:T(8,128)(2,1)} %param.6) | copy-start | bytes 2359300
  4.2 12.8 %collective-permute-start = (bf16[4,128,1152]{2,1,0:T(8,128)(2,1)}, bf16[4,128,1152]{2,1,0:T(8,128)(2,1)S(1)}, u32[]{:S(2)}, u32[]{:S(2)}) collective-permute-start(bf16[4,128,1152]{2,1,0:T(8,128)(2,1)} %get-tuple-element.28), channel_id=1, source_target_pairs={{0,1},{1,0},{2,3},{3,2},{4,5},{5,4},{6,7},{7,6},{8,9},{9,8},{10,11... | collective-permute-start | bytes 3538952 | tf_op jit(solution)/shard_map/ppermute | solution.py:399
  5.5 34.7 %all-to-all-start = ((bf16[32,16,768]{2,1,0:T(8,128)(2,1)}), bf16[32,16,768]{2,1,0:T(8,128)(2,1)S(1)}, u32[]{:S(2)}, u32[]{:S(2)}) async-start(bf16[32,16,768]{2,1,0:T(8,128)(2,1)} %to_pieces.1), calls=%async_computation | async-start | bytes 1572864 | tf_op jit(solution)/shard_map/all_to_all | solution.py:403
  17.0 23.2 %copy-start.7 = (s32[32]{0:T(128)S(1)}, s32[32]{0:T(128)}, u32[]{:S(2)}) copy-start(s32[32]{0:T(128)} %refs_0_.3) | copy-start | bytes 388
  18.5 29.0 %collective-permute-start.1 = (bf16[256,1152]{1,0:T(8,128)(2,1)}, bf16[256,1152]{1,0:T(8,128)(2,1)S(1)}, u32[]{:S(2)}, u32[]{:S(2)}) collective-permute-start(bf16[256,1152]{1,0:T(8,128)(2,1)} %get-tuple-element.30), channel_id=1, source_target_pairs={{0,2},{1,3},{2,4},{3,5},{4,6},{5,7},{6,0},{7,1},{8,10},{9,11},{10,... | collective-permute-start | bytes 1769480 | tf_op jit(solution)/shard_map/ppermute | solution.py:394
  19.0 28.5 %collective-permute-start.2 = (bf16[256,1152]{1,0:T(8,128)(2,1)}, bf16[256,1152]{1,0:T(8,128)(2,1)S(1)}, u32[]{:S(2)}, u32[]{:S(2)}) collective-permute-start(bf16[256,1152]{1,0:T(8,128)(2,1)} %get-tuple-element.31), channel_id=1, source_target_pairs={{0,4},{1,5},{2,6},{3,7},{4,0},{5,1},{6,2},{7,3},{8,12},{9,13},{10,... | collective-permute-start | bytes 1769480 | tf_op jit(solution)/shard_map/ppermute | solution.py:394
  21.4 27.2 %collective-permute-start.3 = (bf16[256,1152]{1,0:T(8,128)(2,1)}, bf16[256,1152]{1,0:T(8,128)(2,1)}, u32[]{:S(2)}, u32[]{:S(2)}) collective-permute-start(bf16[256,1152]{1,0:T(8,128)(2,1)} %get-tuple-element.32), channel_id=1, source_target_pairs={{0,6},{1,7},{2,0},{3,1},{4,2},{5,3},{6,4},{7,5},{8,14},{9,15},{10,... | collective-permute-start | bytes 1769480 | tf_op jit(solution)/shard_map/ppermute | solution.py:394
  41.8 6.8 %copy-start.8 = (bf16[256,1152]{1,0:T(8,128)(2,1)S(1)}, bf16[256,1152]{1,0:T(8,128)(2,1)}, u32[]{:S(2)}) copy-start(bf16[256,1152]{1,0:T(8,128)(2,1)} %get-tuple-element.29.refs_0_) | copy-start | bytes 1769476
  41.8 6.8 %copy-start.12 = (s32[32]{0:T(128)S(1)}, s32[32]{0:T(128)}, u32[]{:S(2)}) copy-start(s32[32]{0:T(128)} %lengths.3) | copy-start | bytes 388
  41.8 6.8 %copy-start.13 = (s32[32]{0:T(128)S(1)}, s32[32]{0:T(128)}, u32[]{:S(2)}) copy-start(s32[32]{0:T(128)} %text_lengths.3) | copy-start | bytes 388
  41.9 27.8 %all-to-all-start.1 = ((bf16[32,16,768]{2,1,0:T(8,128)(2,1)}), bf16[32,16,768]{2,1,0:T(8,128)(2,1)S(1)}, u32[]{:S(2)}, u32[]{:S(2)}) async-start(bf16[32,16,768]{2,1,0:T(8,128)(2,1)} %reorder.2), calls=%async_computation.1 | async-start | bytes 1572864 | tf_op jit(solution)/shard_map/all_to_all | solution.py:403
  47.5 12.4 %copy-start.9 = (bf16[256,1152]{1,0:T(8,128)(2,1)}, bf16[256,1152]{1,0:T(8,128)(2,1)S(1)}, u32[]{:S(2)}) copy-start(bf16[256,1152]{1,0:T(8,128)(2,1)S(1)} %collective-permute-done.1.refs_1_) | copy-start | bytes 1769476
  47.5 12.3 %copy-start.10 = (bf16[256,1152]{1,0:T(8,128)(2,1)}, bf16[256,1152]{1,0:T(8,128)(2,1)S(1)}, u32[]{:S(2)}) copy-start(bf16[256,1152]{1,0:T(8,128)(2,1)S(1)} %collective-permute-done.2.refs_2_) | copy-start | bytes 1769476
  59.9 12.3 %collective-permute-start.4 = (bf16[256,384]{1,0:T(8,128)(2,1)S(1)}, bf16[256,384]{1,0:T(8,128)(2,1)S(1)}, u32[]{:S(2)}, u32[]{:S(2)}) collective-permute-start(bf16[256,384]{1,0:T(8,128)(2,1)S(1)} %get-tuple-element.34), channel_id=1, source_target_pairs={{0,6},{1,7},{2,0},{3,1},{4,2},{5,3},{6,4},{7,5},{8,14},{9,15},{10,... | collective-permute-start | bytes 589832 | tf_op jit(solution)/shard_map/ppermute | solution.py:394
  60.9 11.3 %collective-permute-start.5 = (bf16[256,384]{1,0:T(8,128)(2,1)S(1)}, bf16[256,384]{1,0:T(8,128)(2,1)S(1)}, u32[]{:S(2)}, u32[]{:S(2)}) collective-permute-start(bf16[256,384]{1,0:T(8,128)(2,1)S(1)} %get-tuple-element.35), channel_id=1, source_target_pairs={{0,4},{1,5},{2,6},{3,7},{4,0},{5,1},{6,2},{7,3},{8,12},{9,13},{10,... | collective-permute-start | bytes 589832 | tf_op jit(solution)/shard_map/ppermute | solution.py:394
  62.3 10.5 %collective-permute-start.6 = (bf16[256,384]{1,0:T(8,128)(2,1)S(1)}, bf16[256,384]{1,0:T(8,128)(2,1)S(1)}, u32[]{:S(2)}, u32[]{:S(2)}) collective-permute-start(bf16[256,384]{1,0:T(8,128)(2,1)S(1)} %get-tuple-element.36), channel_id=1, source_target_pairs={{0,2},{1,3},{2,4},{3,5},{4,6},{5,7},{6,0},{7,1},{8,10},{9,11},{10,... | collective-permute-start | bytes 589832 | tf_op jit(solution)/shard_map/ppermute | solution.py:394
  72.0 1.8 %collective-permute-start.8 = (bf16[4,128,384]{2,1,0:T(8,128)(2,1)S(1)}, bf16[4,128,384]{2,1,0:T(8,128)(2,1)S(1)}, u32[]{:S(2)}, u32[]{:S(2)}) collective-permute-start(bf16[4,128,384]{2,1,0:T(8,128)(2,1)S(1)} %get-tuple-element.40), channel_id=1, source_target_pairs={{0,1},{1,0},{2,3},{3,2},{4,5},{5,4},{6,7},{7,6},{8,9},{9,8},{10,11... | collective-permute-start | bytes 1179656 | tf_op jit(solution)/shard_map/ppermute | solution.py:399
  73.4 5.3 %collective-permute-start.7 = (bf16[4,128,384]{2,1,0:T(8,128)(2,1)S(1)}, bf16[4,128,384]{2,1,0:T(8,128)(2,1)S(1)}, u32[]{:S(2)}, u32[]{:S(2)}) collective-permute-start(bf16[4,128,384]{2,1,0:T(8,128)(2,1)S(1)} %for_sibling.2), channel_id=1, source_target_pairs={{0,1},{1,0},{2,3},{3,2},{4,5},{5,4},{6,7},{7,6},{8,9},{9,8},{10,11... | collective-permute-start | bytes 1179656 | tf_op jit(solution)/shard_map/ppermute | solution.py:399
  75.6 14.5 %collective-permute-start.9 = (bf16[256,384]{1,0:T(8,128)(2,1)S(1)}, bf16[256,384]{1,0:T(8,128)(2,1)S(1)}, u32[]{:S(2)}, u32[]{:S(2)}) collective-permute-start(bf16[256,384]{1,0:T(8,128)(2,1)S(1)} %get-tuple-element.43), channel_id=1, source_target_pairs={{0,2},{1,3},{2,4},{3,5},{4,6},{5,7},{6,0},{7,1},{8,10},{9,11},{10,... | collective-permute-start | bytes 589832 | tf_op jit(solution)/shard_map/ppermute | solution.py:394
  77.8 12.3 %collective-permute-start.10 = (bf16[256,384]{1,0:T(8,128)(2,1)S(1)}, bf16[256,384]{1,0:T(8,128)(2,1)S(1)}, u32[]{:S(2)}, u32[]{:S(2)}) collective-permute-start(bf16[256,384]{1,0:T(8,128)(2,1)S(1)} %get-tuple-element.44), channel_id=1, source_target_pairs={{0,4},{1,5},{2,6},{3,7},{4,0},{5,1},{6,2},{7,3},{8,12},{9,13},{10,... | collective-permute-start | bytes 589832 | tf_op jit(solution)/shard_map/ppermute | solution.py:394
  78.2 12.0 %collective-permute-start.11 = (bf16[256,384]{1,0:T(8,128)(2,1)S(1)}, bf16[256,384]{1,0:T(8,128)(2,1)S(1)}, u32[]{:S(2)}, u32[]{:S(2)}) collective-permute-start(bf16[256,384]{1,0:T(8,128)(2,1)S(1)} %get-tuple-element.45), channel_id=1, source_target_pairs={{0,6},{1,7},{2,0},{3,1},{4,2},{5,3},{6,4},{7,5},{8,14},{9,15},{10,... | collective-permute-start | bytes 589832 | tf_op jit(solution)/shard_map/ppermute | solution.py:394
  80.6 32.6 %all-to-all-start.2 = ((bf16[32,16,768]{2,1,0:T(8,128)(2,1)}), bf16[32,16,768]{2,1,0:T(8,128)(2,1)S(1)}, u32[]{:S(2)}, u32[]{:S(2)}) async-start(bf16[32,16,768]{2,1,0:T(8,128)(2,1)} %join_pieces.1), calls=%async_computation.2 | async-start | bytes 1572864 | tf_op jit(solution)/shard_map/all_to_all | solution.py:403
  90.1 0.7 copy-start.15
  107.1 17.9 %collective-permute-start.12 = (bf16[256,1152]{1,0:T(8,128)(2,1)}, bf16[256,1152]{1,0:T(8,128)(2,1)S(1)}, u32[]{:S(2)}, u32[]{:S(2)}) collective-permute-start(bf16[256,1152]{1,0:T(8,128)(2,1)} %get-tuple-element.49), channel_id=1, source_target_pairs={{0,6},{1,7},{2,0},{3,1},{4,2},{5,3},{6,4},{7,5},{8,14},{9,15},{10,... | collective-permute-start | bytes 1769480 | tf_op jit(solution)/shard_map/ppermute | solution.py:394
  109.8 26.9 %collective-permute-start.13 = (bf16[256,1152]{1,0:T(8,128)(2,1)}, bf16[256,1152]{1,0:T(8,128)(2,1)S(1)}, u32[]{:S(2)}, u32[]{:S(2)}) collective-permute-start(bf16[256,1152]{1,0:T(8,128)(2,1)} %get-tuple-element.50), channel_id=1, source_target_pairs={{0,4},{1,5},{2,6},{3,7},{4,0},{5,1},{6,2},{7,3},{8,12},{9,13},{10,... | collective-permute-start | bytes 1769480 | tf_op jit(solution)/shard_map/ppermute | solution.py:394
  111.0 25.7 %collective-permute-start.14 = (bf16[256,1152]{1,0:T(8,128)(2,1)}, bf16[256,1152]{1,0:T(8,128)(2,1)S(1)}, u32[]{:S(2)}, u32[]{:S(2)}) collective-permute-start(bf16[256,1152]{1,0:T(8,128)(2,1)} %get-tuple-element.51), channel_id=1, source_target_pairs={{0,2},{1,3},{2,4},{3,5},{4,6},{5,7},{6,0},{7,1},{8,10},{9,11},{10,... | collective-permute-start | bytes 1769480 | tf_op jit(solution)/shard_map/ppermute | solution.py:394
  115.5 21.2 %copy-start = (bf16[256,1152]{1,0:T(8,128)(2,1)S(1)}, bf16[256,1152]{1,0:T(8,128)(2,1)}, u32[]{:S(2)}) copy-start(bf16[256,1152]{1,0:T(8,128)(2,1)} %get-tuple-element.48.refs_0_.refs_1_) | copy-start | bytes 1769476
  115.5 31.3 %all-to-all-start.3 = ((bf16[32,16,768]{2,1,0:T(8,128)(2,1)}), bf16[32,16,768]{2,1,0:T(8,128)(2,1)S(1)}, u32[]{:S(2)}, u32[]{:S(2)}) async-start(bf16[32,16,768]{2,1,0:T(8,128)(2,1)} %reorder.3), calls=%async_computation.3 | async-start | bytes 1572864 | tf_op jit(solution)/shard_map/all_to_all | solution.py:403
  136.8 3.2 %copy-start.5 = (s32[2]{0:T(128)S(1)}, s32[2]{0:T(128)}, u32[]{:S(2)}) copy-start(s32[2]{0:T(128)} %copy-done.4) | copy-start | bytes 28
  137.1 2.9 %collective-permute-start.15 = (bf16[4,128,1152]{2,1,0:T(8,128)(2,1)S(1)}, bf16[4,128,1152]{2,1,0:T(8,128)(2,1)S(1)}, u32[]{:S(2)}, u32[]{:S(2)}) collective-permute-start(bf16[4,128,1152]{2,1,0:T(8,128)(2,1)S(1)} %for_sibling.3), channel_id=1, source_target_pairs={{0,1},{1,0},{2,3},{3,2},{4,5},{5,4},{6,7},{7,6},{8,9},{9,8},{10,11... | collective-permute-start | bytes 3538952 | tf_op jit(solution)/shard_map/ppermute | solution.py:399
  (5 other events, 3.5 us)

commit v3 on v2

--- a/solution.py
+++ b/solution.py
@@ -17,11 +17,12 @@
 GRP = MINE * DH
 WIDTH = HEADS * DH
 CHIPS = SHARDS // 2
+IC = 512
 CH = 2 * ROWS
 SCALE = DH ** -0.5
 LOGIT = SCALE * 1.4426950408889634
 FWD_VMEM = 24
-BWD_VMEM = 60
+BWD_VMEM = 32
 NT = (((1,), (1,)), ((), ()))
 
 ANY = pl.BlockSpec(memory_space=pl.ANY)
@@ -103,7 +104,7 @@
             yield recv_ref.at[k], outs[k].at[pl.ds(ROWS, ROWS)]
 
     return copies(body, 2 * CHIPS, 2, len(late))(
-        out_shape=[pltpu.HBM((2 * ROWS, width), BF) if width > GRP else jax.ShapeDtypeStruct((2 * ROWS, width), BF)] * CHIPS
+        out_shape=[pltpu.HBM((2 * ROWS, width), BF)] * CHIPS
         + [TOKEN],
         in_specs=[ANY] * (2 + len(late)),
         out_specs=[ANY] * CHIPS + [VMEM],
@@ -216,21 +217,29 @@
 
 
 def cols(part, head):
-    return pl.ds(pl.multiple_of(part * GRP + head * DH, DH), DH)
-
-
-def moves(refs, held, sems, inward):
-    out = []
-    for k in range(CHIPS):
-        rows = held.at[pl.ds(k * CH, CH)]
-        src, dst = (refs[k], rows) if inward else (rows, refs[k])
-        out.append(pltpu.make_async_copy(src, dst, sems.at[k]))
-    return out
-
-
-def run(started):
+    return pl.ds(part * GRP + head * DH, DH)
+
+
+def moves(refs, held, sems, parts, inward):
+    heads = []
+    for g in range(MINE):
+        out = []
+        for k in range(CHIPS):
+            for t in range(parts):
+                block = refs[k].at[:, cols(t, g)]
+                rows = held.at[pl.ds(k * CH, CH), cols(t, g)]
+                src, dst = (block, rows) if inward else (rows, block)
+                out.append(pltpu.make_async_copy(src, dst, sems.at[g, k, t]))
+        heads.append(out)
+    return heads
+
+
+def begin(started):
     for cp in started:
         cp.start()
+
+
+def finish(started):
     for cp in started:
         cp.wait()
 
@@ -244,44 +253,48 @@
 def forward_kernel(at, lengths, text_lengths, *refs):
     xs = refs[:CHIPS]
     outs = refs[CHIPS : 2 * CHIPS]
-    wide, norm, held, done, in_sems, out_sems = refs[2 * CHIPS :]
-    g = pl.program_id(0)
-
-    @pl.when(g == 0)
-    def _():
-        run(moves(xs, held, in_sems, True))
+    wide, norm, token, held, done, wide_held, in_sems, out_sems, wide_sems = refs[2 * CHIPS :]
+    token[...] = jnp.zeros_like(token)
+
+    arriving = moves(xs, held, in_sems, 3, True)
+    leaving = moves(outs, done, out_sems, 1, False)
+    for g in range(MINE):
+        leaving[g].append(pltpu.make_async_copy(wide_held.at[g], wide.at[g], wide_sems.at[g]))
+        begin(arriving[g])
 
     live = live_rows(at, lengths, text_lengths)
-    lane = lax.broadcasted_iota(jnp.int32, (SEQ, DH), 1)
-    dead = jnp.where(live | (lane > 0), 0.0, -1e30).astype(BF)
-    unit = jnp.where(lane == 0, 1.0, 0.0).astype(BF)
-    q = jnp.concatenate([held[:, cols(0, g)], unit], axis=1)
-    k = jnp.concatenate([held[:, cols(1, g)], dead], axis=1)
-    vt = held[:, cols(2, g)].T
-    livef = live.astype(F32)
-    ahead = lax.dot_general(k, q[0:CH], NT, preferred_element_type=F32)
-    for n in range(SEQ // CH):
-        part = slice(n * CH, (n + 1) * CH)
-        s = ahead
-        if n + 1 < SEQ // CH:
-            ahead = lax.dot_general(
-                k, q[(n + 1) * CH : (n + 2) * CH], NT, preferred_element_type=F32
-            )
-        top = jnp.max(s, axis=0, keepdims=True)
-        e = jnp.exp2((s - top) * LOGIT)
-        total = jnp.sum(e, axis=0, keepdims=True)
-        norm[0, :, part] = top + jnp.log2(total) * (1.0 / LOGIT)
-        p = e.astype(BF)
-        rest = (e - p.astype(F32)).astype(BF)
-        o = jnp.dot(vt, p, preferred_element_type=F32)
-        o = o + jnp.dot(vt, rest, preferred_element_type=F32)
-        o = (o * (1.0 / total)).T
-        wide[0, part, :] = o
-        done[part, cols(0, g)] = (o * livef[part]).astype(BF)
-
-    @pl.when(g == MINE - 1)
-    def _():
-        run(moves(outs, done, out_sems, False))
+    for g in range(MINE):
+        finish(arriving[g])
+        lane = lax.broadcasted_iota(jnp.int32, (SEQ, DH), 1)
+        dead = jnp.where(live | (lane > 0), 0.0, -1e30).astype(BF)
+        unit = jnp.where(lane == 0, 1.0, 0.0).astype(BF)
+        q = jnp.concatenate([held[:, cols(0, g)], unit], axis=1)
+        k = jnp.concatenate([held[:, cols(1, g)], dead], axis=1)
+        vt = held[:, cols(2, g)].T
+        livef = live.astype(F32)
+        ahead = lax.dot_general(k, q[0:CH], NT, preferred_element_type=F32)
+        for n in range(SEQ // CH):
+            part = slice(n * CH, (n + 1) * CH)
+            s = ahead
+            if n + 1 < SEQ // CH:
+                ahead = lax.dot_general(
+                    k, q[(n + 1) * CH : (n + 2) * CH], NT, preferred_element_type=F32
+                )
+            top = jnp.max(s, axis=0, keepdims=True)
+            e = jnp.exp2((s - top) * LOGIT)
+            total = jnp.sum(e, axis=0, keepdims=True)
+            norm[g, :, part] = top + jnp.log2(total) * (1.0 / LOGIT)
+            p = e.astype(BF)
+            rest = (e - p.astype(F32)).astype(BF)
+            o = jnp.dot(vt, p, preferred_element_type=F32)
+            o = o + jnp.dot(vt, rest, preferred_element_type=F32)
+            o = (o * (1.0 / total)).T
+            wide_held[g, part, :] = o
+            done[part, cols(0, g)] = (o * livef[part]).astype(BF)
+
+        begin(leaving[g])
+    for g in range(MINE):
+        finish(leaving[g])
 
 
 def backward_kernel(at, lengths, text_lengths, *refs):
@@ -289,70 +302,75 @@
     cs = refs[CHIPS : 2 * CHIPS]
     wide, norm = refs[2 * CHIPS : 2 * CHIPS + 2]
     outs = refs[2 * CHIPS + 2 : 3 * CHIPS + 2]
-    token, held, cot, done, dst, pst, in_sems, cot_sems, out_sems = refs[3 * CHIPS + 2 :]
-    g = pl.program_id(0)
-
-    @pl.when(g == 0)
-    def _():
-        run(moves(xs, held, in_sems, True) + moves(cs, cot, cot_sems, True))
-        token[...] = jnp.zeros_like(token)
+    token, held, cot, done, dst, pst, wide_held, in_sems, cot_sems, out_sems, wide_sems = refs[3 * CHIPS + 2 :]
+
+    arriving = moves(xs, held, in_sems, 3, True)
+    coming = moves(cs, cot, cot_sems, 1, True)
+    leaving = moves(outs, done, out_sems, 3, False)
+    for g in range(MINE):
+        arriving[g].append(pltpu.make_async_copy(wide.at[g], wide_held.at[g], wide_sems.at[g]))
+        begin(arriving[g] + coming[g])
+    token[...] = jnp.zeros_like(token)
 
     live = live_rows(at, lengths, text_lengths)
-    lane = lax.broadcasted_iota(jnp.int32, (SEQ, DH), 1)
-    do = jnp.where(live, cot[:, cols(0, g)], jnp.zeros((), BF))
-    dot = jnp.sum(do.astype(F32) * wide[0], axis=1, keepdims=True)
-    hi, mid, low = thirds(dot)
-    less = jnp.where(lane == 0, -hi, jnp.where(lane == 1, -mid, jnp.where(lane == 2, -low, 0.0)))
-    dox = jnp.concatenate([do, less.astype(BF)], axis=1)
-    units = jnp.where(lane < 3, 1.0, 0.0).astype(BF)
-    vx = jnp.concatenate([held[:, cols(2, g)], units], axis=1)
-    hi, mid, low = thirds(norm[0].T)
-    less = jnp.where(lane == 0, -hi, jnp.where(lane == 1, -mid, jnp.where(lane == 2, -low, 0.0)))
-    less = jnp.where(lane == 3, 1.0, less).astype(BF)
-    dead = jnp.where(lane < 3, 1.0, jnp.where(live | (lane > 3), 0.0, -1e30)).astype(BF)
-    qx = jnp.concatenate([held[:, cols(0, g)], less], axis=1)
-    kx = jnp.concatenate([held[:, cols(1, g)], dead], axis=1)
-    kt = held[:, cols(1, g)].T
-    for n in range(SEQ // CH):
-        part = slice(n * CH, (n + 1) * CH)
-        s = lax.dot_general(kx, qx[part], NT, preferred_element_type=F32)
-        dp = lax.dot_general(vx, dox[part], NT, preferred_element_type=F32)
-        p = jnp.exp2(s * LOGIT)
-        pst[:, part] = p.astype(BF)
-        ds = (p * dp).astype(BF)
-        dst[:, part] = ds
-        dq = jnp.dot(kt, ds, preferred_element_type=F32).T * SCALE
-        done[part, cols(0, g)] = dq.astype(BF)
-    q = held[:, cols(0, g)]
-    for n in range(SEQ // CH):
-        part = slice(n * CH, (n + 1) * CH)
-        dk = jnp.dot(dst[part, :], q, preferred_element_type=F32) * SCALE
-        dv = jnp.dot(pst[part, :], do, preferred_element_type=F32)
-        done[part, cols(1, g)] = dk.astype(BF)
-        done[part, cols(2, g)] = dv.astype(BF)
-
-    @pl.when(g == MINE - 1)
-    def _():
-        run(moves(outs, done, out_sems, False))
-
-
-WIDE = pl.BlockSpec((1, SEQ, DH), lambda g: (g, 0, 0))
-NORM = pl.BlockSpec((1, 1, SEQ), lambda g: (g, 0, 0))
+    for g in range(MINE):
+        finish(arriving[g] + coming[g])
+        lane = lax.broadcasted_iota(jnp.int32, (SEQ, DH), 1)
+        do = jnp.where(live, cot[:, cols(0, g)], jnp.zeros((), BF))
+        dot = jnp.sum(do.astype(F32) * wide_held[g], axis=1, keepdims=True)
+        hi, mid, low = thirds(dot)
+        less = jnp.where(lane == 0, -hi, jnp.where(lane == 1, -mid, jnp.where(lane == 2, -low, 0.0)))
+        dox = jnp.concatenate([do, less.astype(BF)], axis=1)
+        units = jnp.where(lane < 3, 1.0, 0.0).astype(BF)
+        vx = jnp.concatenate([held[:, cols(2, g)], units], axis=1)
+        hi, mid, low = thirds(norm[g].T)
+        less = jnp.where(lane == 0, -hi, jnp.where(lane == 1, -mid, jnp.where(lane == 2, -low, 0.0)))
+        less = jnp.where(lane == 3, 1.0, less).astype(BF)
+        dead = jnp.where(lane < 3, 1.0, jnp.where(live | (lane > 3), 0.0, -1e30)).astype(BF)
+        qx = jnp.concatenate([held[:, cols(0, g)], less], axis=1)
+        kx = jnp.concatenate([held[:, cols(1, g)], dead], axis=1)
+        kt = held[:, cols(1, g)].T
+        for n in range(SEQ // IC):
+            part = slice(n * IC, (n + 1) * IC)
+            s = lax.dot_general(kx, qx[part], NT, preferred_element_type=F32)
+            dp = lax.dot_general(vx, dox[part], NT, preferred_element_type=F32)
+            p = jnp.exp2(s * LOGIT)
+            pst[:, part] = p.astype(BF)
+            ds = (p * dp).astype(BF)
+            dst[:, part] = ds
+            dq = jnp.dot(kt, ds, preferred_element_type=F32).T * SCALE
+            done[part, cols(0, g)] = dq.astype(BF)
+        q = held[:, cols(0, g)]
+        for n in range(SEQ // IC):
+            part = slice(n * IC, (n + 1) * IC)
+            dk = jnp.dot(dst[part, :], q, preferred_element_type=F32) * SCALE
+            dv = jnp.dot(pst[part, :], do, preferred_element_type=F32)
+            done[part, cols(1, g)] = dk.astype(BF)
+            done[part, cols(2, g)] = dv.astype(BF)
+
+        begin(leaving[g])
+    for g in range(MINE):
+        finish(leaving[g])
+
+
+NORM = pl.BlockSpec((MINE, 1, SEQ), lambda g: (0, 0, 0))
 
 
 def forward(where, xs):
     return pl.pallas_call(
         forward_kernel,
-        grid=(MINE,),
+        grid=(1,),
         out_shape=[jax.ShapeDtypeStruct((CH, GRP), BF)] * CHIPS
-        + [pltpu.HBM((MINE, SEQ, DH), F32), pltpu.HBM((MINE, 1, SEQ), F32)],
+        + [pltpu.HBM((MINE, SEQ, DH), F32), pltpu.HBM((MINE, 1, SEQ), F32), TOKEN],
         in_specs=[SMEM] * 3 + [ANY] * CHIPS,
-        out_specs=[ANY] * CHIPS + [WIDE, NORM],
+        out_specs=[ANY] * (CHIPS + 1) + [NORM, pl.BlockSpec((8, 128), lambda g: (0, 0))],
         scratch_shapes=[
             pltpu.VMEM((SEQ, 3 * GRP), BF),
             pltpu.VMEM((SEQ, GRP), BF),
-            pltpu.SemaphoreType.DMA((CHIPS,)),
-            pltpu.SemaphoreType.DMA((CHIPS,)),
+            pltpu.VMEM((MINE, SEQ, DH), F32),
+            pltpu.SemaphoreType.DMA((MINE, CHIPS, 3)),
+            pltpu.SemaphoreType.DMA((MINE, CHIPS, 1)),
+            pltpu.SemaphoreType.DMA((MINE,)),
         ],
         compiler_params=pltpu.CompilerParams(vmem_limit_bytes=FWD_VMEM << 20),
         cost_estimate=pl.CostEstimate(
@@ -365,9 +383,9 @@
 def backward(where, cs, xs, wide, norm):
     return pl.pallas_call(
         backward_kernel,
-        grid=(MINE,),
+        grid=(1,),
         out_shape=[jax.ShapeDtypeStruct((CH, 3 * GRP), BF)] * CHIPS + [TOKEN],
-        in_specs=[SMEM] * 3 + [ANY] * (2 * CHIPS) + [WIDE, NORM],
+        in_specs=[SMEM] * 3 + [ANY] * (2 * CHIPS) + [ANY, NORM],
         out_specs=[ANY] * CHIPS + [pl.BlockSpec((8, 128), lambda g: (0, 0))],
         scratch_shapes=[
             pltpu.VMEM((SEQ, 3 * GRP), BF),
@@ -375,9 +393,11 @@
             pltpu.VMEM((SEQ, 3 * GRP), BF),
             pltpu.VMEM((SEQ, SEQ), BF),
             pltpu.VMEM((SEQ, SEQ), BF),
-            pltpu.SemaphoreType.DMA((CHIPS,)),
-            pltpu.SemaphoreType.DMA((CHIPS,)),
-            pltpu.SemaphoreType.DMA((CHIPS,)),
+            pltpu.VMEM((MINE, SEQ, DH), F32),
+            pltpu.SemaphoreType.DMA((MINE, CHIPS, 3)),
+            pltpu.SemaphoreType.DMA((MINE, CHIPS, 1)),
+            pltpu.SemaphoreType.DMA((MINE, CHIPS, 3)),
+            pltpu.SemaphoreType.DMA((MINE,)),
         ],
         compiler_params=pltpu.CompilerParams(vmem_limit_bytes=BWD_VMEM << 20),
         cost_estimate=pl.CostEstimate(
@@ -414,9 +434,9 @@
     there = spread(to_pieces(cotangent[0]))
     here = spread(reorder(destinations, there, False, paired))
 
-    *outs, wide, norm = forward(where, xs)
+    *outs, wide, norm, attended_once = forward(where, xs)
     os = turn(outs, -1)
-    own, other = split_cotangent(at, here, norm)
+    own, other = split_cotangent(at, here, attended_once)
     *cs, paired = pair(own, swap(other))
     halfway = spread(join_pieces(at, os, swap(for_sibling(os)), paired))
     cs = turn(cs, 1)

time: 149 us -> 145 us (0.973)
  Pallas kernels: 43.9 us -> 39.8 us
  waiting for transfers between devices: 46.1 us -> 48.4 us
    pallas_call x2, Pallas kernels: 27.4 us -> 23.4 us  [the longest x1 13.1 us: backward(): pl.pallas_call(backward_kernel, grid=(1,), out_shape=[jax.ShapeDtypeStruc...]
    all_to_all x4, starting transfers between devices: 36.1 us -> 34.6 us  [spread(): return lax.all_to_all(pieces, 'dp', split_axis=0, concat_axis=0, tiled=True)]
    unnamed x34 -> x22, local copies, waits for them, and re-layouts: 4.52 us -> 4.18 us
  transfers between devices with their start and end apart: 20 -> 20, of which waited for: 11 -> 13; matrix products, arithmetic and copies ran while one was open for 0% -> 0% of each run, Pallas kernels for 28% -> 25%
where the time goes in v3:
time: 145 us
  starting transfers between devices  51.1 us (35%)
  waiting for transfers between devices  48.4 us (33%)
  Pallas kernels  39.8 us (27%)
  local copies, waits for them, and re-layouts  4.18 us (3%)
    all_to_all x4, starting transfers between devices, spread(): return lax.all_to_all(pieces, 'dp', split_axis=0, concat_axis=0, tiled=True)  34.6 us
    all_to_all x4, waiting for transfers between devices, spread(): return lax.all_to_all(pieces, 'dp', split_axis=0, concat_axis=0, tiled=True)  30.5 us
    ppermute x12, starting transfers between devices, turn(): out.append(lax.ppermute(blocks[k], 'seq', pairs))  16.2 us
    ppermute x12, waiting for transfers between devices, turn(): out.append(lax.ppermute(blocks[k], 'seq', pairs))  14.6 us
    pallas_call x1, Pallas kernels, backward(): pl.pallas_call(backward_kernel, grid=(1,), out_shape=[jax.ShapeDtypeStruc...  13.1 us
    pallas_call x1, Pallas kernels, forward(): pl.pallas_call(forward_kernel, grid=(1,), out_shape=[jax.ShapeDtypeStruct...  10.3 us
    unnamed x22, local copies, waits for them, and re-layouts  4.18 us
    pallas_call x2, Pallas kernels, reorder(): copies(body, RANKS, 2, len(late), 100)  3.36 us
  transfers between devices with their start and end apart: 20, of which 13 were waited for; matrix products, arithmetic and copies ran while one was open for 0% of the time, Pallas kernels for 25%

profile of v3, /device:TPU:6, one launch (start us, length us, event | category | flops | bytes accessed | tf_op | source)
XLA Modules:
  0.0 144.6 jit_solution(15043993441781557907)
XLA Ops:
  0.7 1.7 %copy-done = bf16[1,128,9216]{2,1,0:T(8,128)(2,1)S(1)} copy-done((bf16[1,128,9216]{2,1,0:T(8,128)(2,1)S(1)}, bf16[1,128,9216]{2,1,0:T(8,128)(2,1)}, u32[]{:S(2)}) %copy-start) | copy-done | bytes 2359320
  2.4 1.8 %split_projected.1 = (bf16[4,128,1152]{2,1,0:T(8,128)(2,1)S(1)}, bf16[4,128,1152]{2,1,0:T(8,128)(2,1)}) custom-call(s32[2]{0:T(128)S(1)} %pad_add_fusion.refs_0_.at, bf16[128,9216]{1,0:T(8,128)(2,1)S(1)} %bitcast.6), custom_call_target="tpu_custom_call" | custom-call | bytes 4194304 | tf_op jit(solution)/shard_map/split_projected/pallas_call | solution.py:70
  4.3 1.1 to_pieces.1
  5.4 11.5 %all-to-all-start = ((bf16[32,16,768]{2,1,0:T(8,128)(2,1)}), bf16[32,16,768]{2,1,0:T(8,128)(2,1)S(1)}, u32[]{:S(2)}, u32[]{:S(2)}) async-start(bf16[32,16,768]{2,1,0:T(8,128)(2,1)} %to_pieces.1), calls=%async_computation | async-start | bytes 1572864 | tf_op jit(solution)/shard_map/all_to_all | solution.py:423
  17.0 1.5 %pair.2 = (bf16[256,1152]{1,0:T(8,128)(2,1)}, bf16[256,1152]{1,0:T(8,128)(2,1)}, bf16[256,1152]{1,0:T(8,128)(2,1)}, bf16[256,1152]{1,0:T(8,128)(2,1)}, f32[8,128]{1,0:T(8,128)S(1)}) custom-call(bf16[4,128,1152]{2,1,0:T(8,128)(2,1)S(1)} %get-tuple-element.28.refs_0_, bf16[4,128,1152]{2,1,0:T(8,128)(2,1)S(1)} %collective-permute-done.refs_1_), custom_call_target="tpu_custom_call" | custom-call | bytes 4194304 | tf_op jit(solution)/shard_map/pair/pallas_call | solution.py:106
  19.0 2.4 %collective-permute-start.2 = (bf16[256,1152]{1,0:T(8,128)(2,1)}, bf16[256,1152]{1,0:T(8,128)(2,1)S(1)}, u32[]{:S(2)}, u32[]{:S(2)}) collective-permute-start(bf16[256,1152]{1,0:T(8,128)(2,1)} %get-tuple-element.32), channel_id=1, source_target_pairs={{0,4},{1,5},{2,6},{3,7},{4,0},{5,1},{6,2},{7,3},{8,12},{9,13},{10,... | collective-permute-start | bytes 1769480 | tf_op jit(solution)/shard_map/ppermute | solution.py:414
  21.5 18.7 %all-to-all-done.refs_1_ = bf16[32,16,768]{2,1,0:T(8,128)(2,1)S(1)} async-done(((bf16[32,16,768]{2,1,0:T(8,128)(2,1)}), bf16[32,16,768]{2,1,0:T(8,128)(2,1)S(1)}, u32[]{:S(2)}, u32[]{:S(2)}) %all-to-all-start) | async-done | bytes 786464 | tf_op jit(solution)/shard_map/all_to_all | solution.py:423
  40.1 1.7 %reorder.2 = bf16[32,16,768]{2,1,0:T(8,128)(2,1)} custom-call(s32[32]{0:T(128)S(1)} %copy-done.2, bf16[32,16,768]{2,1,0:T(8,128)(2,1)S(1)} %all-to-all-done.refs_1_, f32[8,128]{1,0:T(8,128)S(1)} %get-tuple-element.38.refs_2_), custom_call_target="tpu_custom_call" | custom-call | bytes 104857600 | tf_op jit(solution)/shard_map/reorder/pallas_call | solution.py:166
  41.8 5.6 %all-to-all-start.1 = ((bf16[32,16,768]{2,1,0:T(8,128)(2,1)}), bf16[32,16,768]{2,1,0:T(8,128)(2,1)S(1)}, u32[]{:S(2)}, u32[]{:S(2)}) async-start(bf16[32,16,768]{2,1,0:T(8,128)(2,1)} %reorder.2), calls=%async_computation.1 | async-start | bytes 1572864 | tf_op jit(solution)/shard_map/all_to_all | solution.py:423
  47.5 1.1 collective-permute-done.3.refs_3_
  48.7 10.3 %attend.1 = (bf16[256,384]{1,0:T(8,128)(2,1)S(1)}, bf16[256,384]{1,0:T(8,128)(2,1)S(1)}, bf16[256,384]{1,0:T(8,128)(2,1)S(1)}, bf16[256,384]{1,0:T(8,128)(2,1)S(...) custom-call(s32[2]{0:T(128)S(1)} %pad_add_fusion.refs_0_.at, s32[32]{0:T(128)S(1)} %copy-done.7, ...), custom_call_target="tpu_custom_call" | custom-call | flops 80530636800 | bytes 12582912 | tf_op jit(solution)/shard_map/attend/pallas_call | solution.py:360
  58.9 1.2 collective-permute-start.4
  60.2 1.4 collective-permute-start.5
  61.5 2.0 %collective-permute-start.6 = (bf16[256,384]{1,0:T(8,128)(2,1)S(1)}, bf16[256,384]{1,0:T(8,128)(2,1)S(1)}, u32[]{:S(2)}, u32[]{:S(2)}) collective-permute-start(bf16[256,384]{1,0:T(8,128)(2,1)S(1)} %get-tuple-element.37), channel_id=1, source_target_pairs={{0,2},{1,3},{2,4},{3,5},{4,6},{5,7},{6,0},{7,1},{8,10},{9,11},{10,... | collective-permute-start | bytes 589832 | tf_op jit(solution)/shard_map/ppermute | solution.py:414
  63.6 6.1 %all-to-all-done.1.refs_1_ = bf16[32,16,768]{2,1,0:T(8,128)(2,1)S(1)} async-done(((bf16[32,16,768]{2,1,0:T(8,128)(2,1)}), bf16[32,16,768]{2,1,0:T(8,128)(2,1)S(1)}, u32[]{:S(2)}, u32[]{:S(2)}) %all-to-all-start.1) | async-done | bytes 786464 | tf_op jit(solution)/shard_map/all_to_all | solution.py:423
  69.7 1.6 %split_cotangent.1 = (bf16[4,128,384]{2,1,0:T(8,128)(2,1)S(1)}, bf16[4,128,384]{2,1,0:T(8,128)(2,1)S(1)}) custom-call(s32[2]{0:T(128)S(1)} %pad_add_fusion.refs_0_.at, bf16[32,16,768]{2,1,0:T(8,128)(2,1)S(1)} %all-to-all-done.1.refs_1_, f32[8,128]{1,0:T(8,128)S(1)} %get-tuple-element.39.refs_2_), custom_call_target="tpu_custom_call" | custom-call | bytes 4194304 | tf_op jit(solution)/shard_map/split_cotangent/pallas_call | solution.py:184
  74.1 2.2 %collective-permute-start.9 = (bf16[256,384]{1,0:T(8,128)(2,1)}, bf16[256,384]{1,0:T(8,128)(2,1)S(1)}, u32[]{:S(2)}, u32[]{:S(2)}) collective-permute-start(bf16[256,384]{1,0:T(8,128)(2,1)} %get-tuple-element.44), channel_id=1, source_target_pairs={{0,2},{1,3},{2,4},{3,5},{4,6},{5,7},{6,0},{7,1},{8,10},{9,11},{10,... | collective-permute-start | bytes 589832 | tf_op jit(solution)/shard_map/ppermute | solution.py:414
  77.2 1.9 %join_pieces.1 = bf16[32,16,768]{2,1,0:T(8,128)(2,1)} custom-call(s32[2]{0:T(128)S(1)} %pad_add_fusion.refs_0_.at, bf16[256,384]{1,0:T(8,128)(2,1)S(1)} %get-tuple-element.34.refs_0_.refs_1_, bf16[256,384]{1,0:T(8,128)(2,1)S(1)} %collective-permute-done.4.refs_1_.refs_2_, bf16[256,384]{1,0:T(8,128)(2,1)S(1)} %collective-permute-done.5.refs_2_.refs_3_, ...), custom_call_target="tpu_custom_call" | custom-call | bytes 4194304 | tf_op jit(solution)/shard_map/join_pieces/pallas_call | solution.py:202
  79.2 9.6 %all-to-all-start.2 = ((bf16[32,16,768]{2,1,0:T(8,128)(2,1)}), bf16[32,16,768]{2,1,0:T(8,128)(2,1)S(1)}, u32[]{:S(2)}, u32[]{:S(2)}) async-start(bf16[32,16,768]{2,1,0:T(8,128)(2,1)} %join_pieces.1), calls=%async_computation.2 | async-start | bytes 1572864 | tf_op jit(solution)/shard_map/all_to_all | solution.py:423
  90.0 1.4 copy-done.9
  91.4 13.1 %attend_grad.1 = (bf16[256,1152]{1,0:T(8,128)(2,1)S(1)}, bf16[256,1152]{1,0:T(8,128)(2,1)}, bf16[256,1152]{1,0:T(8,128)(2,1)}, bf16[256,1152]{1,0:T(8,128)(2,1)}, f32[8,128]{1,0:T(8,128)S(1)}) custom-call(s32[2]{0:T(128)S(1)} %pad_add_fusion.refs_0_.at, s32[32]{0:T(128)S(1)} %copy-done.7, s32[32]{0:T(128)S(1)} %copy-done.8, bf16[256,1152]{1,0:T(8,128)(2,1)S(1)} %copy-done.3, ...), custom_call_target="tpu_custom_call" | custom-call | flops 128849018880 | bytes 16777216 | tf_op jit(solution)/shard_map/attend_grad/pallas_call | solution.py:384
  104.5 2.6 %collective-permute-start.12 = (bf16[256,1152]{1,0:T(8,128)(2,1)}, bf16[256,1152]{1,0:T(8,128)(2,1)S(1)}, u32[]{:S(2)}, u32[]{:S(2)}) collective-permute-start(bf16[256,1152]{1,0:T(8,128)(2,1)} %get-tuple-element.51), channel_id=1, source_target_pairs={{0,6},{1,7},{2,0},{3,1},{4,2},{5,3},{6,4},{7,5},{8,14},{9,15},{10,... | collective-permute-start | bytes 1769480 | tf_op jit(solution)/shard_map/ppermute | solution.py:414
  107.1 1.2 collective-permute-start.13
  108.2 1.7 %collective-permute-start.14 = (bf16[256,1152]{1,0:T(8,128)(2,1)}, bf16[256,1152]{1,0:T(8,128)(2,1)S(1)}, u32[]{:S(2)}, u32[]{:S(2)}) collective-permute-start(bf16[256,1152]{1,0:T(8,128)(2,1)} %get-tuple-element.53), channel_id=1, source_target_pairs={{0,2},{1,3},{2,4},{3,5},{4,6},{5,7},{6,0},{7,1},{8,10},{9,11},{10,... | collective-permute-start | bytes 1769480 | tf_op jit(solution)/shard_map/ppermute | solution.py:414
  109.9 2.0 %all-to-all-done.2.refs_1_ = bf16[32,16,768]{2,1,0:T(8,128)(2,1)S(1)} async-done(((bf16[32,16,768]{2,1,0:T(8,128)(2,1)}), bf16[32,16,768]{2,1,0:T(8,128)(2,1)S(1)}, u32[]{:S(2)}, u32[]{:S(2)}) %all-to-all-start.2) | async-done | bytes 786464 | tf_op jit(solution)/shard_map/all_to_all | solution.py:423
  111.9 1.7 %reorder.3 = bf16[32,16,768]{2,1,0:T(8,128)(2,1)} custom-call(s32[32]{0:T(128)S(1)} %copy-done.2, bf16[32,16,768]{2,1,0:T(8,128)(2,1)S(1)} %all-to-all-done.2.refs_1_, f32[8,128]{1,0:T(8,128)S(1)} %get-tuple-element.49.refs_2_), custom_call_target="tpu_custom_call" | custom-call | bytes 104857600 | tf_op jit(solution)/shard_map/reorder/pallas_call | solution.py:166
  113.6 7.8 %all-to-all-start.3 = ((bf16[32,16,768]{2,1,0:T(8,128)(2,1)}), bf16[32,16,768]{2,1,0:T(8,128)(2,1)S(1)}, u32[]{:S(2)}, u32[]{:S(2)}) async-start(bf16[32,16,768]{2,1,0:T(8,128)(2,1)} %reorder.3), calls=%async_computation.3 | async-start | bytes 1572864 | tf_op jit(solution)/shard_map/all_to_all | solution.py:423
  121.8 12.2 %collective-permute-done.13.refs_2_.refs_3_ = bf16[256,1152]{1,0:T(8,128)(2,1)S(1)} collective-permute-done((bf16[256,1152]{1,0:T(8,128)(2,1)}, bf16[256,1152]{1,0:T(8,128)(2,1)S(1)}, u32[]{:S(2)}, u32[]{:S(2)}) %collective-permute-start.13) | collective-permute-done | bytes 589856 | tf_op jit(solution)/shard_map/ppermute | solution.py:414
  134.5 2.8 %collective-permute-done.15.refs_5_ = bf16[4,128,1152]{2,1,0:T(8,128)(2,1)S(1)} collective-permute-done((bf16[4,128,1152]{2,1,0:T(8,128)(2,1)S(1)}, bf16[4,128,1152]{2,1,0:T(8,128)(2,1)S(1)}, u32[]{:S(2)}, u32[]{:S(2)}) %collective-permute-start.15) | collective-permute-done | bytes 1179680 | tf_op jit(solution)/shard_map/ppermute | solution.py:419
  137.4 2.1 %join_gradient.1 = bf16[128,9216]{1,0:T(8,128)(2,1)} custom-call(s32[2]{0:T(128)S(1)} %pad_add_fusion.refs_0_.at, bf16[256,1152]{1,0:T(8,128)(2,1)S(1)} %get-tuple-element.50.refs_0_.refs_1_, bf16[256,1152]{1,0:T(8,128)(2,1)S(1)} %collective-permute-done.12.refs_1_.refs_2_, bf16[256,1152]{1,0:T(8,128)(2,1)S(1)} %collective-permute-done.13.refs_2_.refs_3_, ...), custom_call_target="tpu_custom_call" | custom-call | bytes 4194304 | tf_op jit(solution)/shard_map/join_gradient/pallas_call | solution.py:89
  139.5 3.8 %all-to-all-done.3.refs_0_ = bf16[32,16,768]{2,1,0:T(8,128)(2,1)S(1)} async-done(((bf16[32,16,768]{2,1,0:T(8,128)(2,1)}), bf16[32,16,768]{2,1,0:T(8,128)(2,1)S(1)}, u32[]{:S(2)}, u32[]{:S(2)}) %all-to-all-start.3) | async-done | bytes 786464 | tf_op jit(solution)/shard_map/all_to_all | solution.py:423
  143.3 1.1 from_pieces.1
  (45 shorter events, 6.5 us)
Async XLA Ops:
  0.7 1.7 %copy-start = (bf16[1,128,9216]{2,1,0:T(8,128)(2,1)S(1)}, bf16[1,128,9216]{2,1,0:T(8,128)(2,1)}, u32[]{:S(2)}) copy-start(bf16[1,128,9216]{2,1,0:T(8,128)(2,1)} %param.5) | copy-start | bytes 7077892
  2.4 1.9 %copy-start.1 = (bf16[1,128,3072]{2,1,0:T(8,128)(2,1)S(1)}, bf16[1,128,3072]{2,1,0:T(8,128)(2,1)}, u32[]{:S(2)}) copy-start(bf16[1,128,3072]{2,1,0:T(8,128)(2,1)} %param.6) | copy-start | bytes 2359300
  4.2 12.8 %collective-permute-start = (bf16[4,128,1152]{2,1,0:T(8,128)(2,1)}, bf16[4,128,1152]{2,1,0:T(8,128)(2,1)S(1)}, u32[]{:S(2)}, u32[]{:S(2)}) collective-permute-start(bf16[4,128,1152]{2,1,0:T(8,128)(2,1)} %get-tuple-element.29), channel_id=1, source_target_pairs={{0,1},{1,0},{2,3},{3,2},{4,5},{5,4},{6,7},{7,6},{8,9},{9,8},{10,11... | collective-permute-start | bytes 3538952 | tf_op jit(solution)/shard_map/ppermute | solution.py:419
  5.4 34.7 %all-to-all-start = ((bf16[32,16,768]{2,1,0:T(8,128)(2,1)}), bf16[32,16,768]{2,1,0:T(8,128)(2,1)S(1)}, u32[]{:S(2)}, u32[]{:S(2)}) async-start(bf16[32,16,768]{2,1,0:T(8,128)(2,1)} %to_pieces.1), calls=%async_computation | async-start | bytes 1572864 | tf_op jit(solution)/shard_map/all_to_all | solution.py:423
  17.0 23.2 %copy-start.2 = (s32[32]{0:T(128)S(1)}, s32[32]{0:T(128)}, u32[]{:S(2)}) copy-start(s32[32]{0:T(128)} %refs_0_.3) | copy-start | bytes 388
  18.5 29.0 %collective-permute-start.1 = (bf16[256,1152]{1,0:T(8,128)(2,1)}, bf16[256,1152]{1,0:T(8,128)(2,1)S(1)}, u32[]{:S(2)}, u32[]{:S(2)}) collective-permute-start(bf16[256,1152]{1,0:T(8,128)(2,1)} %get-tuple-element.31), channel_id=1, source_target_pairs={{0,2},{1,3},{2,4},{3,5},{4,6},{5,7},{6,0},{7,1},{8,10},{9,11},{10,... | collective-permute-start | bytes 1769480 | tf_op jit(solution)/shard_map/ppermute | solution.py:414
  19.0 28.5 %collective-permute-start.2 = (bf16[256,1152]{1,0:T(8,128)(2,1)}, bf16[256,1152]{1,0:T(8,128)(2,1)S(1)}, u32[]{:S(2)}, u32[]{:S(2)}) collective-permute-start(bf16[256,1152]{1,0:T(8,128)(2,1)} %get-tuple-element.32), channel_id=1, source_target_pairs={{0,4},{1,5},{2,6},{3,7},{4,0},{5,1},{6,2},{7,3},{8,12},{9,13},{10,... | collective-permute-start | bytes 1769480 | tf_op jit(solution)/shard_map/ppermute | solution.py:414
  21.5 27.2 %collective-permute-start.3 = (bf16[256,1152]{1,0:T(8,128)(2,1)}, bf16[256,1152]{1,0:T(8,128)(2,1)}, u32[]{:S(2)}, u32[]{:S(2)}) collective-permute-start(bf16[256,1152]{1,0:T(8,128)(2,1)} %get-tuple-element.33), channel_id=1, source_target_pairs={{0,6},{1,7},{2,0},{3,1},{4,2},{5,3},{6,4},{7,5},{8,14},{9,15},{10,... | collective-permute-start | bytes 1769480 | tf_op jit(solution)/shard_map/ppermute | solution.py:414
  41.8 6.8 %copy-start.3 = (bf16[256,1152]{1,0:T(8,128)(2,1)S(1)}, bf16[256,1152]{1,0:T(8,128)(2,1)}, u32[]{:S(2)}) copy-start(bf16[256,1152]{1,0:T(8,128)(2,1)} %get-tuple-element.30.refs_0_) | copy-start | bytes 1769476
  41.8 6.8 %copy-start.7 = (s32[32]{0:T(128)S(1)}, s32[32]{0:T(128)}, u32[]{:S(2)}) copy-start(s32[32]{0:T(128)} %lengths.3) | copy-start | bytes 388
  41.8 6.8 %copy-start.8 = (s32[32]{0:T(128)S(1)}, s32[32]{0:T(128)}, u32[]{:S(2)}) copy-start(s32[32]{0:T(128)} %text_lengths.3) | copy-start | bytes 388
  41.8 27.8 %all-to-all-start.1 = ((bf16[32,16,768]{2,1,0:T(8,128)(2,1)}), bf16[32,16,768]{2,1,0:T(8,128)(2,1)S(1)}, u32[]{:S(2)}, u32[]{:S(2)}) async-start(bf16[32,16,768]{2,1,0:T(8,128)(2,1)} %reorder.2), calls=%async_computation.1 | async-start | bytes 1572864 | tf_op jit(solution)/shard_map/all_to_all | solution.py:423
  47.5 11.4 %copy-start.4 = (bf16[256,1152]{1,0:T(8,128)(2,1)}, bf16[256,1152]{1,0:T(8,128)(2,1)S(1)}, u32[]{:S(2)}) copy-start(bf16[256,1152]{1,0:T(8,128)(2,1)S(1)} %collective-permute-done.2.refs_2_) | copy-start | bytes 1769476
  58.9 12.5 %collective-permute-start.4 = (bf16[256,384]{1,0:T(8,128)(2,1)S(1)}, bf16[256,384]{1,0:T(8,128)(2,1)S(1)}, u32[]{:S(2)}, u32[]{:S(2)}) collective-permute-start(bf16[256,384]{1,0:T(8,128)(2,1)S(1)} %get-tuple-element.35), channel_id=1, source_target_pairs={{0,6},{1,7},{2,0},{3,1},{4,2},{5,3},{6,4},{7,5},{8,14},{9,15},{10,... | collective-permute-start | bytes 589832 | tf_op jit(solution)/shard_map/ppermute | solution.py:414
  60.2 11.3 %collective-permute-start.5 = (bf16[256,384]{1,0:T(8,128)(2,1)S(1)}, bf16[256,384]{1,0:T(8,128)(2,1)S(1)}, u32[]{:S(2)}, u32[]{:S(2)}) collective-permute-start(bf16[256,384]{1,0:T(8,128)(2,1)S(1)} %get-tuple-element.36), channel_id=1, source_target_pairs={{0,4},{1,5},{2,6},{3,7},{4,0},{5,1},{6,2},{7,3},{8,12},{9,13},{10,... | collective-permute-start | bytes 589832 | tf_op jit(solution)/shard_map/ppermute | solution.py:414
  61.5 10.5 %collective-permute-start.6 = (bf16[256,384]{1,0:T(8,128)(2,1)S(1)}, bf16[256,384]{1,0:T(8,128)(2,1)S(1)}, u32[]{:S(2)}, u32[]{:S(2)}) collective-permute-start(bf16[256,384]{1,0:T(8,128)(2,1)S(1)} %get-tuple-element.37), channel_id=1, source_target_pairs={{0,2},{1,3},{2,4},{3,5},{4,6},{5,7},{6,0},{7,1},{8,10},{9,11},{10,... | collective-permute-start | bytes 589832 | tf_op jit(solution)/shard_map/ppermute | solution.py:414
  71.3 1.8 %collective-permute-start.8 = (bf16[4,128,384]{2,1,0:T(8,128)(2,1)S(1)}, bf16[4,128,384]{2,1,0:T(8,128)(2,1)S(1)}, u32[]{:S(2)}, u32[]{:S(2)}) collective-permute-start(bf16[4,128,384]{2,1,0:T(8,128)(2,1)S(1)} %get-tuple-element.41), channel_id=1, source_target_pairs={{0,1},{1,0},{2,3},{3,2},{4,5},{5,4},{6,7},{7,6},{8,9},{9,8},{10,11... | collective-permute-start | bytes 1179656 | tf_op jit(solution)/shard_map/ppermute | solution.py:419
  72.6 4.6 %collective-permute-start.7 = (bf16[4,128,384]{2,1,0:T(8,128)(2,1)S(1)}, bf16[4,128,384]{2,1,0:T(8,128)(2,1)S(1)}, u32[]{:S(2)}, u32[]{:S(2)}) collective-permute-start(bf16[4,128,384]{2,1,0:T(8,128)(2,1)S(1)} %for_sibling.2), channel_id=1, source_target_pairs={{0,1},{1,0},{2,3},{3,2},{4,5},{5,4},{6,7},{7,6},{8,9},{9,8},{10,11... | collective-permute-start | bytes 1179656 | tf_op jit(solution)/shard_map/ppermute | solution.py:419
  74.1 14.7 %collective-permute-start.9 = (bf16[256,384]{1,0:T(8,128)(2,1)}, bf16[256,384]{1,0:T(8,128)(2,1)S(1)}, u32[]{:S(2)}, u32[]{:S(2)}) collective-permute-start(bf16[256,384]{1,0:T(8,128)(2,1)} %get-tuple-element.44), channel_id=1, source_target_pairs={{0,2},{1,3},{2,4},{3,5},{4,6},{5,7},{6,0},{7,1},{8,10},{9,11},{10,... | collective-permute-start | bytes 589832 | tf_op jit(solution)/shard_map/ppermute | solution.py:414
  76.2 12.6 %collective-permute-start.10 = (bf16[256,384]{1,0:T(8,128)(2,1)}, bf16[256,384]{1,0:T(8,128)(2,1)S(1)}, u32[]{:S(2)}, u32[]{:S(2)}) collective-permute-start(bf16[256,384]{1,0:T(8,128)(2,1)} %get-tuple-element.45), channel_id=1, source_target_pairs={{0,4},{1,5},{2,6},{3,7},{4,0},{5,1},{6,2},{7,3},{8,12},{9,13},{10,... | collective-permute-start | bytes 589832 | tf_op jit(solution)/shard_map/ppermute | solution.py:414
  76.8 12.1 %collective-permute-start.11 = (bf16[256,384]{1,0:T(8,128)(2,1)}, bf16[256,384]{1,0:T(8,128)(2,1)S(1)}, u32[]{:S(2)}, u32[]{:S(2)}) collective-permute-start(bf16[256,384]{1,0:T(8,128)(2,1)} %get-tuple-element.46), channel_id=1, source_target_pairs={{0,6},{1,7},{2,0},{3,1},{4,2},{5,3},{6,4},{7,5},{8,14},{9,15},{10,... | collective-permute-start | bytes 589832 | tf_op jit(solution)/shard_map/ppermute | solution.py:414
  79.1 9.7 %copy-start.6 = (bf16[256,384]{1,0:T(8,128)(2,1)S(1)}, bf16[256,384]{1,0:T(8,128)(2,1)}, u32[]{:S(2)}) copy-start(bf16[256,384]{1,0:T(8,128)(2,1)} %get-tuple-element.43.refs_4_) | copy-start | bytes 589828
  79.2 9.7 %copy-start.10 = (f32[3,1,1024]{2,1,0:T(1,128)S(1)}, f32[3,1,1024]{2,1,0:T(1,128)}, u32[]{:S(2)}) copy-start(f32[3,1,1024]{2,1,0:T(1,128)} %get-tuple-element.48.refs_9_) | copy-start | bytes 36868
  79.2 32.7 %all-to-all-start.2 = ((bf16[32,16,768]{2,1,0:T(8,128)(2,1)}), bf16[32,16,768]{2,1,0:T(8,128)(2,1)S(1)}, u32[]{:S(2)}, u32[]{:S(2)}) async-start(bf16[32,16,768]{2,1,0:T(8,128)(2,1)} %join_pieces.1), calls=%async_computation.2 | async-start | bytes 1572864 | tf_op jit(solution)/shard_map/all_to_all | solution.py:423
  88.9 1.1 copy-start.5
  90.0 1.4 copy-start.9
  104.5 17.3 %collective-permute-start.12 = (bf16[256,1152]{1,0:T(8,128)(2,1)}, bf16[256,1152]{1,0:T(8,128)(2,1)S(1)}, u32[]{:S(2)}, u32[]{:S(2)}) collective-permute-start(bf16[256,1152]{1,0:T(8,128)(2,1)} %get-tuple-element.51), channel_id=1, source_target_pairs={{0,6},{1,7},{2,0},{3,1},{4,2},{5,3},{6,4},{7,5},{8,14},{9,15},{10,... | collective-permute-start | bytes 1769480 | tf_op jit(solution)/shard_map/ppermute | solution.py:414
  107.1 26.9 %collective-permute-start.13 = (bf16[256,1152]{1,0:T(8,128)(2,1)}, bf16[256,1152]{1,0:T(8,128)(2,1)S(1)}, u32[]{:S(2)}, u32[]{:S(2)}) collective-permute-start(bf16[256,1152]{1,0:T(8,128)(2,1)} %get-tuple-element.52), channel_id=1, source_target_pairs={{0,4},{1,5},{2,6},{3,7},{4,0},{5,1},{6,2},{7,3},{8,12},{9,13},{10,... | collective-permute-start | bytes 1769480 | tf_op jit(solution)/shard_map/ppermute | solution.py:414
  108.2 25.9 %collective-permute-start.14 = (bf16[256,1152]{1,0:T(8,128)(2,1)}, bf16[256,1152]{1,0:T(8,128)(2,1)S(1)}, u32[]{:S(2)}, u32[]{:S(2)}) collective-permute-start(bf16[256,1152]{1,0:T(8,128)(2,1)} %get-tuple-element.53), channel_id=1, source_target_pairs={{0,2},{1,3},{2,4},{3,5},{4,6},{5,7},{6,0},{7,1},{8,10},{9,11},{10,... | collective-permute-start | bytes 1769480 | tf_op jit(solution)/shard_map/ppermute | solution.py:414
  113.6 29.7 %all-to-all-start.3 = ((bf16[32,16,768]{2,1,0:T(8,128)(2,1)}), bf16[32,16,768]{2,1,0:T(8,128)(2,1)S(1)}, u32[]{:S(2)}, u32[]{:S(2)}) async-start(bf16[32,16,768]{2,1,0:T(8,128)(2,1)} %reorder.3), calls=%async_computation.3 | async-start | bytes 1572864 | tf_op jit(solution)/shard_map/all_to_all | solution.py:423
  134.4 2.9 %collective-permute-start.15 = (bf16[4,128,1152]{2,1,0:T(8,128)(2,1)S(1)}, bf16[4,128,1152]{2,1,0:T(8,128)(2,1)S(1)}, u32[]{:S(2)}, u32[]{:S(2)}) collective-permute-start(bf16[4,128,1152]{2,1,0:T(8,128)(2,1)S(1)} %for_sibling.3), channel_id=1, source_target_pairs={{0,1},{1,0},{2,3},{3,2},{4,5},{5,4},{6,7},{7,6},{8,9},{9,8},{10,11... | collective-permute-start | bytes 3538952 | tf_op jit(solution)/shard_map/ppermute | solution.py:419

commit v4 on v3

--- a/solution.py
+++ b/solution.py
@@ -17,6 +17,7 @@
 GRP = MINE * DH
 WIDTH = HEADS * DH
 CHIPS = SHARDS // 2
+PIECES = (8, 4, 16, 768)
 IC = 512
 CH = 2 * ROWS
 SCALE = DH ** -0.5
@@ -75,23 +76,25 @@
     )(at, projected, *late)
 
 
-def join_gradient(at, blocks, sibling, *late):
+def join_gradient(at, parts, own, so_far, *late):
     def body(at_ref, *refs):
         out = refs[-1]
         for k in range(CHIPS):
             chip, core = place(at_ref, k)
-            mine = refs[k].at[pl.ds(0, ROWS)], 2 * chip + core
-            for src, head in (mine, (refs[CHIPS].at[k], 2 * chip + 1 - core)):
-                for t in range(3):
-                    start = pl.multiple_of(t * WIDTH + head * GRP, GRP)
-                    yield src.at[:, pl.ds(t * GRP, GRP)], out.at[:, pl.ds(start, GRP)]
-
-    return copies(body, 6 * CHIPS, 2 + CHIPS, len(late))(
-        out_shape=jax.ShapeDtypeStruct((ROWS, 3 * WIDTH), BF),
-        in_specs=[SMEM] + [ANY] * (1 + CHIPS + len(late)),
-        out_specs=ANY,
+            src = refs[k].at[pl.ds(0, ROWS)] if own else refs[0].at[k]
+            head = 2 * chip + (core if own else 1 - core)
+            for t in range(3):
+                start = pl.multiple_of(t * WIDTH + head * GRP, GRP)
+                yield src.at[:, pl.ds(t * GRP, GRP)], out.at[:, pl.ds(start, GRP)]
+
+    given = (at, *parts, *so_far)
+    return copies(body, 3 * CHIPS, len(given), len(late))(
+        out_shape=pltpu.HBM((ROWS, 3 * WIDTH), BF),
+        in_specs=[SMEM] + [ANY] * (len(given) - 1 + len(late)),
+        out_specs=ANY,
+        input_output_aliases={} if own else {2: 0},
         name="join_gradient",
-    )(at, *blocks, sibling, *late)
+    )(*given, *late)
 
 
 def pair(own, recv, *late):
@@ -129,30 +132,30 @@
 
 def to_pieces(rows, *late):
     def body(x_ref, out):
-        for a in range(8):
-            for b in range(4):
-                yield x_ref.at[pl.ds(16 * a, 16), pl.ds(768 * b, 768)], out.at[4 * a + b]
-
-    return copies(body, RANKS, 1, len(late))(
-        out_shape=jax.ShapeDtypeStruct((RANKS, 16, 768), BF),
+        for b in range(4):
+            yield x_ref.at[:, :, pl.ds(768 * b, 768)], out.at[:, b]
+
+    pieces = copies(body, 4, 1, len(late))(
+        out_shape=jax.ShapeDtypeStruct(PIECES, BF),
         in_specs=[ANY] + [ANY] * len(late),
         out_specs=ANY,
         name="to_pieces",
-    )(rows, *late)
+    )(rows.reshape(8, 16, WIDTH), *late)
+    return pieces.reshape(RANKS, 16, 768)
 
 
 def from_pieces(pieces, *late):
     def body(x_ref, out):
-        for a in range(8):
-            for b in range(4):
-                yield x_ref.at[4 * a + b], out.at[pl.ds(16 * a, 16), pl.ds(768 * b, 768)]
-
-    return copies(body, RANKS, 1, len(late))(
-        out_shape=jax.ShapeDtypeStruct((ROWS, WIDTH), BF),
+        for b in range(4):
+            yield x_ref.at[:, b], out.at[:, :, pl.ds(768 * b, 768)]
+
+    rows = copies(body, 4, 1, len(late))(
+        out_shape=jax.ShapeDtypeStruct((8, 16, WIDTH), BF),
         in_specs=[ANY] + [ANY] * len(late),
         out_specs=ANY,
         name="from_pieces",
-    )(pieces, *late)
+    )(pieces.reshape(PIECES), *late)
+    return rows.reshape(ROWS, WIDTH)
 
 
 def reorder(destinations, pieces, back, *late):
@@ -177,16 +180,15 @@
             chip, core = place(at_ref, k)
             for out, half in ((own, core), (other, 1 - core)):
                 start = pl.multiple_of(half * GRP, GRP)
-                for a in range(8):
-                    src = x_ref.at[4 * a + chip, :, pl.ds(start, GRP)]
-                    yield src, out.at[k, pl.ds(16 * a, 16)]
-
-    return copies(body, 16 * CHIPS, 2, len(late))(
-        out_shape=[jax.ShapeDtypeStruct((CHIPS, ROWS, GRP), BF)] * 2,
+                yield x_ref.at[:, chip, :, pl.ds(start, GRP)], out.at[k]
+
+    own, other = copies(body, 2 * CHIPS, 2, len(late))(
+        out_shape=[jax.ShapeDtypeStruct((CHIPS, 8, 16, GRP), BF)] * 2,
         in_specs=[SMEM, ANY] + [ANY] * len(late),
         out_specs=[ANY] * 2,
         name="split_cotangent",
-    )(at, pieces, *late)
+    )(at, pieces.reshape(PIECES), *late)
+    return own.reshape(CHIPS, ROWS, GRP), other.reshape(CHIPS, ROWS, GRP)
 
 
 def join_pieces(at, blocks, sibling, *late):
@@ -194,17 +196,17 @@
         out = refs[-1]
         for k in range(CHIPS):
             chip, core = place(at_ref, k)
-            for src, half in ((refs[k], core), (refs[CHIPS].at[k], 1 - core)):
+            for src, half in ((refs[k].at[pl.ds(0, 8)], core), (refs[CHIPS].at[k], 1 - core)):
                 start = pl.multiple_of(half * GRP, GRP)
-                for a in range(8):
-                    yield src.at[pl.ds(16 * a, 16)], out.at[4 * a + chip, :, pl.ds(start, GRP)]
-
-    return copies(body, 16 * CHIPS, 2 + CHIPS, len(late))(
-        out_shape=jax.ShapeDtypeStruct((RANKS, 16, 768), BF),
+                yield src, out.at[:, chip, :, pl.ds(start, GRP)]
+
+    pieces = copies(body, 2 * CHIPS, 2 + CHIPS, len(late))(
+        out_shape=jax.ShapeDtypeStruct(PIECES, BF),
         in_specs=[SMEM] + [ANY] * (1 + CHIPS + len(late)),
         out_specs=ANY,
         name="join_pieces",
-    )(at, *blocks, sibling, *late)
+    )(at, *(b.reshape(16, 16, GRP) for b in blocks), sibling.reshape(CHIPS, 8, 16, GRP), *late)
+    return pieces.reshape(RANKS, 16, 768)
 
 
 def live_rows(at, lengths, text_lengths):
@@ -263,35 +265,40 @@
         begin(arriving[g])
 
     live = live_rows(at, lengths, text_lengths)
+    lane = lax.broadcasted_iota(jnp.int32, (SEQ, DH), 1)
+    dead = jnp.where(live | (lane > 0), 0.0, -1e30).astype(BF)
+    unit = jnp.where(lane == 0, 1.0, 0.0).astype(BF)
+    livef = live.astype(F32)
     for g in range(MINE):
         finish(arriving[g])
-        lane = lax.broadcasted_iota(jnp.int32, (SEQ, DH), 1)
-        dead = jnp.where(live | (lane > 0), 0.0, -1e30).astype(BF)
-        unit = jnp.where(lane == 0, 1.0, 0.0).astype(BF)
-        q = jnp.concatenate([held[:, cols(0, g)], unit], axis=1)
+
+    def logits(g, n):
+        rows = slice(n * CH, (n + 1) * CH)
+        q = jnp.concatenate([held[rows, cols(0, g)], unit[rows]], axis=1)
         k = jnp.concatenate([held[:, cols(1, g)], dead], axis=1)
-        vt = held[:, cols(2, g)].T
-        livef = live.astype(F32)
-        ahead = lax.dot_general(k, q[0:CH], NT, preferred_element_type=F32)
-        for n in range(SEQ // CH):
-            part = slice(n * CH, (n + 1) * CH)
-            s = ahead
-            if n + 1 < SEQ // CH:
-                ahead = lax.dot_general(
-                    k, q[(n + 1) * CH : (n + 2) * CH], NT, preferred_element_type=F32
-                )
-            top = jnp.max(s, axis=0, keepdims=True)
-            e = jnp.exp2((s - top) * LOGIT)
-            total = jnp.sum(e, axis=0, keepdims=True)
-            norm[g, :, part] = top + jnp.log2(total) * (1.0 / LOGIT)
-            p = e.astype(BF)
-            rest = (e - p.astype(F32)).astype(BF)
-            o = jnp.dot(vt, p, preferred_element_type=F32)
-            o = o + jnp.dot(vt, rest, preferred_element_type=F32)
-            o = (o * (1.0 / total)).T
-            wide_held[g, part, :] = o
-            done[part, cols(0, g)] = (o * livef[part]).astype(BF)
-
+        return lax.dot_general(k, q, NT, preferred_element_type=F32)
+
+    steps = [(g, n) for g in range(MINE) for n in range(SEQ // CH)]
+    ahead = logits(*steps[0])
+    for step, (g, n) in enumerate(steps):
+        part = slice(n * CH, (n + 1) * CH)
+        s = ahead
+        if step + 1 < len(steps):
+            ahead = logits(*steps[step + 1])
+        if n == 0:
+            vt = held[:, cols(2, g)].T
+        top = jnp.max(s, axis=0, keepdims=True)
+        e = jnp.exp2((s - top) * LOGIT)
+        total = jnp.sum(e, axis=0, keepdims=True)
+        norm[g, :, part] = top + jnp.log2(total) * (1.0 / LOGIT)
+        p = e.astype(BF)
+        rest = (e - p.astype(F32)).astype(BF)
+        o = jnp.dot(vt, p, preferred_element_type=F32)
+        o = o + jnp.dot(vt, rest, preferred_element_type=F32)
+        o = (o * (1.0 / total)).T
+        wide_held[g, part, :] = o
+        done[part, cols(0, g)] = (o * livef[part]).astype(BF)
+    for g in range(MINE):
         begin(leaving[g])
     for g in range(MINE):
         finish(leaving[g])
@@ -313,21 +320,36 @@
     token[...] = jnp.zeros_like(token)
 
     live = live_rows(at, lengths, text_lengths)
+    lane = lax.broadcasted_iota(jnp.int32, (SEQ, DH), 1)
+    units = jnp.where(lane < 3, 1.0, 0.0).astype(BF)
+    dead = jnp.where(lane < 3, 1.0, jnp.where(live | (lane > 3), 0.0, -1e30)).astype(BF)
+
+    def three(value, rest):
+        hi, mid, low = thirds(value)
+        low = jnp.where(lane == 2, -low, rest)
+        return jnp.where(lane == 0, -hi, jnp.where(lane == 1, -mid, low)).astype(BF)
+
+    one = jnp.where(lane == 3, 1.0, 0.0)
     for g in range(MINE):
         finish(arriving[g] + coming[g])
-        lane = lax.broadcasted_iota(jnp.int32, (SEQ, DH), 1)
-        do = jnp.where(live, cot[:, cols(0, g)], jnp.zeros((), BF))
+
+    def masked(g):
+        return jnp.where(live, cot[:, cols(0, g)], jnp.zeros((), BF))
+
+    def key_value(g, n):
+        part = slice(n * IC, (n + 1) * IC)
+        slot = g % 2
+        dk = jnp.dot(dst[slot, part, :], held[:, cols(0, g)], preferred_element_type=F32) * SCALE
+        done[part, cols(1, g)] = dk.astype(BF)
+        dv = jnp.dot(pst[slot, part, :], masked(g), preferred_element_type=F32)
+        done[part, cols(2, g)] = dv.astype(BF)
+
+    for g in range(MINE):
+        do = masked(g)
         dot = jnp.sum(do.astype(F32) * wide_held[g], axis=1, keepdims=True)
-        hi, mid, low = thirds(dot)
-        less = jnp.where(lane == 0, -hi, jnp.where(lane == 1, -mid, jnp.where(lane == 2, -low, 0.0)))
-        dox = jnp.concatenate([do, less.astype(BF)], axis=1)
-        units = jnp.where(lane < 3, 1.0, 0.0).astype(BF)
+        dox = jnp.concatenate([do, three(dot, 0.0)], axis=1)
         vx = jnp.concatenate([held[:, cols(2, g)], units], axis=1)
-        hi, mid, low = thirds(norm[g].T)
-        less = jnp.where(lane == 0, -hi, jnp.where(lane == 1, -mid, jnp.where(lane == 2, -low, 0.0)))
-        less = jnp.where(lane == 3, 1.0, less).astype(BF)
-        dead = jnp.where(lane < 3, 1.0, jnp.where(live | (lane > 3), 0.0, -1e30)).astype(BF)
-        qx = jnp.concatenate([held[:, cols(0, g)], less], axis=1)
+        qx = jnp.concatenate([held[:, cols(0, g)], three(norm[g].T, one)], axis=1)
         kx = jnp.concatenate([held[:, cols(1, g)], dead], axis=1)
         kt = held[:, cols(1, g)].T
         for n in range(SEQ // IC):
@@ -335,19 +357,14 @@
             s = lax.dot_general(kx, qx[part], NT, preferred_element_type=F32)
             dp = lax.dot_general(vx, dox[part], NT, preferred_element_type=F32)
             p = jnp.exp2(s * LOGIT)
-            pst[:, part] = p.astype(BF)
+            pst[g % 2, :, part] = p.astype(BF)
             ds = (p * dp).astype(BF)
-            dst[:, part] = ds
+            dst[g % 2, :, part] = ds
             dq = jnp.dot(kt, ds, preferred_element_type=F32).T * SCALE
             done[part, cols(0, g)] = dq.astype(BF)
-        q = held[:, cols(0, g)]
         for n in range(SEQ // IC):
-            part = slice(n * IC, (n + 1) * IC)
-            dk = jnp.dot(dst[part, :], q, preferred_element_type=F32) * SCALE
-            dv = jnp.dot(pst[part, :], do, preferred_element_type=F32)
-            done[part, cols(1, g)] = dk.astype(BF)
-            done[part, cols(2, g)] = dv.astype(BF)
-
+            key_value(g, n)
+    for g in range(MINE):
         begin(leaving[g])
     for g in range(MINE):
         finish(leaving[g])
@@ -391,8 +408,8 @@
             pltpu.VMEM((SEQ, 3 * GRP), BF),
             pltpu.VMEM((SEQ, GRP), BF),
             pltpu.VMEM((SEQ, 3 * GRP), BF),
-            pltpu.VMEM((SEQ, SEQ), BF),
-            pltpu.VMEM((SEQ, SEQ), BF),
+            pltpu.VMEM((2, SEQ, SEQ), BF),
+            pltpu.VMEM((2, SEQ, SEQ), BF),
             pltpu.VMEM((MINE, SEQ, DH), F32),
             pltpu.SemaphoreType.DMA((MINE, CHIPS, 3)),
             pltpu.SemaphoreType.DMA((MINE, CHIPS, 1)),
@@ -444,7 +461,9 @@
     *gs, graded = backward(where, cs, xs, wide, norm)
     gs = turn(gs, -1)
     home = spread(reorder(destinations, halfway, True, graded))
-    projected_grad = join_gradient(at, gs, swap(for_sibling(gs)))
+    sibling = for_sibling(gs)
+    projected_grad = join_gradient(at, gs, True, (), sibling)
+    projected_grad = join_gradient(at, (swap(sibling),), False, (projected_grad,))
     attended = from_pieces(home)
     return attended[None], projected_grad[None]
 

time: 145 us -> 143 us (0.986)
  Pallas kernels: 39.8 us -> 38.2 us
    ppermute x4, waiting for transfers between devices: 3.23 us -> 1.58 us  [swap(): return lax.ppermute(block, 'seq', [(s, s ^ 1) for s in range(SHARDS)])]
    pallas_call x5 -> x6, Pallas kernels: 7.99 us -> 7.35 us  [the longest x2 3.3 us: join_gradient(): copies(body, 3 * CHIPS, len(given), len(late))]
where the time goes in v4:
time: 143 us
  starting transfers between devices  50.3 us (35%)
  waiting for transfers between devices  48.7 us (34%)
  Pallas kernels  38.2 us (27%)
  local copies, waits for them, and re-layouts  4.18 us (3%)
    all_to_all x4, starting transfers between devices, spread(): return lax.all_to_all(pieces, 'dp', split_axis=0, concat_axis=0, tiled=True)  34.4 us
    all_to_all x4, waiting for transfers between devices, spread(): return lax.all_to_all(pieces, 'dp', split_axis=0, concat_axis=0, tiled=True)  31.6 us
    ppermute x12, waiting for transfers between devices, turn(): out.append(lax.ppermute(blocks[k], 'seq', pairs))  15.6 us
    ppermute x12, starting transfers between devices, turn(): out.append(lax.ppermute(blocks[k], 'seq', pairs))  15.5 us
    pallas_call x1, Pallas kernels, backward(): pl.pallas_call(backward_kernel, grid=(1,), out_shape=[jax.ShapeDtypeStruc...  12.9 us
    pallas_call x1, Pallas kernels, forward(): pl.pallas_call(forward_kernel, grid=(1,), out_shape=[jax.ShapeDtypeStruct...  9.59 us
    unnamed x22, local copies, waits for them, and re-layouts  4.18 us
    pallas_call x2, Pallas kernels, reorder(): copies(body, RANKS, 2, len(late), 100)  3.36 us
  transfers between devices with their start and end apart: 20, of which 13 were waited for; matrix products, arithmetic and copies ran while one was open for 0% of the time, Pallas kernels for 25%

profile of v4, /device:TPU:6, one launch (start us, length us, event | category | flops | bytes accessed | tf_op | source)
XLA Modules:
  0.0 142.6 jit_solution(7870174635369752890)
XLA Ops:
  0.7 1.7 %copy-done = bf16[1,128,9216]{2,1,0:T(8,128)(2,1)S(1)} copy-done((bf16[1,128,9216]{2,1,0:T(8,128)(2,1)S(1)}, bf16[1,128,9216]{2,1,0:T(8,128)(2,1)}, u32[]{:S(2)}) %copy-start) | copy-done | bytes 2359320
  2.4 1.8 %split_projected.1 = (bf16[4,128,1152]{2,1,0:T(8,128)(2,1)S(1)}, bf16[4,128,1152]{2,1,0:T(8,128)(2,1)}) custom-call(s32[2]{0:T(128)S(1)} %pad_add_fusion.refs_0_.at, bf16[128,9216]{1,0:T(8,128)(2,1)S(1)} %bitcast.19), custom_call_target="tpu_custom_call" | custom-call | bytes 4194304 | tf_op jit(solution)/shard_map/split_projected/pallas_call | solution.py:71
  5.2 11.5 %all-to-all-start = ((bf16[32,16,768]{2,1,0:T(8,128)(2,1)}), bf16[32,16,768]{2,1,0:T(8,128)(2,1)S(1)}, u32[]{:S(2)}, u32[]{:S(2)}) async-start(bf16[32,16,768]{2,1,0:T(8,128)(2,1)} %bitcast.9), calls=%async_computation | async-start | bytes 1572864 | tf_op jit(solution)/shard_map/all_to_all | solution.py:440
  16.7 1.5 %pair.2 = (bf16[256,1152]{1,0:T(8,128)(2,1)}, bf16[256,1152]{1,0:T(8,128)(2,1)}, bf16[256,1152]{1,0:T(8,128)(2,1)}, bf16[256,1152]{1,0:T(8,128)(2,1)}, f32[8,128]{1,0:T(8,128)S(1)}) custom-call(bf16[4,128,1152]{2,1,0:T(8,128)(2,1)S(1)} %get-tuple-element.28.refs_0_, bf16[4,128,1152]{2,1,0:T(8,128)(2,1)S(1)} %collective-permute-done.refs_1_), custom_call_target="tpu_custom_call" | custom-call | bytes 4194304 | tf_op jit(solution)/shard_map/pair/pallas_call | solution.py:109
  18.8 2.4 %collective-permute-start.2 = (bf16[256,1152]{1,0:T(8,128)(2,1)}, bf16[256,1152]{1,0:T(8,128)(2,1)S(1)}, u32[]{:S(2)}, u32[]{:S(2)}) collective-permute-start(bf16[256,1152]{1,0:T(8,128)(2,1)} %get-tuple-element.32), channel_id=1, source_target_pairs={{0,4},{1,5},{2,6},{3,7},{4,0},{5,1},{6,2},{7,3},{8,12},{9,13},{10,... | collective-permute-start | bytes 1769480 | tf_op jit(solution)/shard_map/ppermute | solution.py:431
  21.2 18.7 %all-to-all-done.refs_1_ = bf16[32,16,768]{2,1,0:T(8,128)(2,1)S(1)} async-done(((bf16[32,16,768]{2,1,0:T(8,128)(2,1)}), bf16[32,16,768]{2,1,0:T(8,128)(2,1)S(1)}, u32[]{:S(2)}, u32[]{:S(2)}) %all-to-all-start) | async-done | bytes 786464 | tf_op jit(solution)/shard_map/all_to_all | solution.py:440
  39.9 1.7 %reorder.2 = bf16[32,16,768]{2,1,0:T(8,128)(2,1)} custom-call(s32[32]{0:T(128)S(1)} %copy-done.2, bf16[32,16,768]{2,1,0:T(8,128)(2,1)S(1)} %all-to-all-done.refs_1_, f32[8,128]{1,0:T(8,128)S(1)} %get-tuple-element.38.refs_2_), custom_call_target="tpu_custom_call" | custom-call | bytes 104857600 | tf_op jit(solution)/shard_map/reorder/pallas_call | solution.py:169
  41.6 5.6 %all-to-all-start.1 = ((bf16[32,16,768]{2,1,0:T(8,128)(2,1)}), bf16[32,16,768]{2,1,0:T(8,128)(2,1)S(1)}, u32[]{:S(2)}, u32[]{:S(2)}) async-start(bf16[32,16,768]{2,1,0:T(8,128)(2,1)} %reorder.2), calls=%async_computation.1 | async-start | bytes 1572864 | tf_op jit(solution)/shard_map/all_to_all | solution.py:440
  47.3 1.1 collective-permute-done.3.refs_3_
  48.4 9.6 %attend.1 = (bf16[256,384]{1,0:T(8,128)(2,1)S(1)}, bf16[256,384]{1,0:T(8,128)(2,1)S(1)}, bf16[256,384]{1,0:T(8,128)(2,1)S(1)}, bf16[256,384]{1,0:T(8,128)(2,1)S(...) custom-call(s32[2]{0:T(128)S(1)} %pad_add_fusion.refs_0_.at, s32[32]{0:T(128)S(1)} %copy-done.7, ...), custom_call_target="tpu_custom_call" | custom-call | flops 80530636800 | bytes 12582912 | tf_op jit(solution)/shard_map/attend/pallas_call | solution.py:377
  58.0 1.0 collective-permute-start.4
  59.1 1.4 collective-permute-start.5
  60.5 2.0 %collective-permute-start.6 = (bf16[256,384]{1,0:T(8,128)(2,1)S(1)}, bf16[256,384]{1,0:T(8,128)(2,1)S(1)}, u32[]{:S(2)}, u32[]{:S(2)}) collective-permute-start(bf16[256,384]{1,0:T(8,128)(2,1)S(1)} %get-tuple-element.37), channel_id=1, source_target_pairs={{0,2},{1,3},{2,4},{3,5},{4,6},{5,7},{6,0},{7,1},{8,10},{9,11},{10,... | collective-permute-start | bytes 589832 | tf_op jit(solution)/shard_map/ppermute | solution.py:431
  62.5 6.9 %all-to-all-done.1 = bf16[32,16,768]{2,1,0:T(8,128)(2,1)S(1)} async-done(((bf16[32,16,768]{2,1,0:T(8,128)(2,1)}), bf16[32,16,768]{2,1,0:T(8,128)(2,1)S(1)}, u32[]{:S(2)}, u32[]{:S(2)}) %all-to-all-start.1) | async-done | bytes 786464 | tf_op jit(solution)/shard_map/all_to_all | solution.py:440
  73.0 2.2 %collective-permute-start.9 = (bf16[256,384]{1,0:T(8,128)(2,1)}, bf16[256,384]{1,0:T(8,128)(2,1)S(1)}, u32[]{:S(2)}, u32[]{:S(2)}) collective-permute-start(bf16[256,384]{1,0:T(8,128)(2,1)} %get-tuple-element.44), channel_id=1, source_target_pairs={{0,2},{1,3},{2,4},{3,5},{4,6},{5,7},{6,0},{7,1},{8,10},{9,11},{10,... | collective-permute-start | bytes 589832 | tf_op jit(solution)/shard_map/ppermute | solution.py:431
  76.1 1.5 %join_pieces.1 = bf16[8,4,16,768]{3,2,1,0:T(8,128)(2,1)} custom-call(s32[2]{0:T(128)S(1)} %pad_add_fusion.refs_0_.at, bf16[16,16,384]{2,1,0:T(8,128)(2,1)S(1)} %bitcast.20, bf16[16,16,384]{2,1,0:T(8,128)(2,1)S(1)} %bitcast.21, bf16[16,16,384]{2,1,0:T(8,128)(2,1)S(1)} %bitcast.22, bf16[16,16,384]{2,1,0:T(8,128)(2,1)S(1)} %bitcast.23, ...), custom_call_target="tpu_custom_call" | custom-call | bytes 4194304 | tf_op jit(solution)/shard_map/join_pieces/pallas_call | solution.py:203
  77.6 9.6 %all-to-all-start.2 = ((bf16[32,16,768]{2,1,0:T(8,128)(2,1)}), bf16[32,16,768]{2,1,0:T(8,128)(2,1)S(1)}, u32[]{:S(2)}, u32[]{:S(2)}) async-start(bf16[32,16,768]{2,1,0:T(8,128)(2,1)} %bitcast.13), calls=%async_computation.2 | async-start | bytes 1572864 | tf_op jit(solution)/shard_map/all_to_all | solution.py:440
  87.8 1.1 copy-done.5
  88.9 1.4 copy-done.9
  90.3 12.9 %attend_grad.1 = (bf16[256,1152]{1,0:T(8,128)(2,1)S(1)}, bf16[256,1152]{1,0:T(8,128)(2,1)}, bf16[256,1152]{1,0:T(8,128)(2,1)}, bf16[256,1152]{1,0:T(8,128)(2,1)}, f32[8,128]{1,0:T(8,128)S(1)}) custom-call(s32[2]{0:T(128)S(1)} %pad_add_fusion.refs_0_.at, s32[32]{0:T(128)S(1)} %copy-done.7, s32[32]{0:T(128)S(1)} %copy-done.8, bf16[256,1152]{1,0:T(8,128)(2,1)S(1)} %copy-done.3, ...), custom_call_target="tpu_custom_call" | custom-call | flops 128849018880 | bytes 16777216 | tf_op jit(solution)/shard_map/attend_grad/pallas_call | solution.py:401
  103.2 2.1 %collective-permute-start.12 = (bf16[256,1152]{1,0:T(8,128)(2,1)}, bf16[256,1152]{1,0:T(8,128)(2,1)S(1)}, u32[]{:S(2)}, u32[]{:S(2)}) collective-permute-start(bf16[256,1152]{1,0:T(8,128)(2,1)} %get-tuple-element.51), channel_id=1, source_target_pairs={{0,6},{1,7},{2,0},{3,1},{4,2},{5,3},{6,4},{7,5},{8,14},{9,15},{10,... | collective-permute-start | bytes 1769480 | tf_op jit(solution)/shard_map/ppermute | solution.py:431
  105.3 1.2 collective-permute-start.13
  106.5 1.6 %collective-permute-start.14 = (bf16[256,1152]{1,0:T(8,128)(2,1)}, bf16[256,1152]{1,0:T(8,128)(2,1)S(1)}, u32[]{:S(2)}, u32[]{:S(2)}) collective-permute-start(bf16[256,1152]{1,0:T(8,128)(2,1)} %get-tuple-element.53), channel_id=1, source_target_pairs={{0,2},{1,3},{2,4},{3,5},{4,6},{5,7},{6,0},{7,1},{8,10},{9,11},{10,... | collective-permute-start | bytes 1769480 | tf_op jit(solution)/shard_map/ppermute | solution.py:431
  108.1 2.2 %all-to-all-done.2.refs_1_ = bf16[32,16,768]{2,1,0:T(8,128)(2,1)S(1)} async-done(((bf16[32,16,768]{2,1,0:T(8,128)(2,1)}), bf16[32,16,768]{2,1,0:T(8,128)(2,1)S(1)}, u32[]{:S(2)}, u32[]{:S(2)}) %all-to-all-start.2) | async-done | bytes 786464 | tf_op jit(solution)/shard_map/all_to_all | solution.py:440
  110.3 1.7 %reorder.3 = bf16[32,16,768]{2,1,0:T(8,128)(2,1)} custom-call(s32[32]{0:T(128)S(1)} %copy-done.2, bf16[32,16,768]{2,1,0:T(8,128)(2,1)S(1)} %all-to-all-done.2.refs_1_, f32[8,128]{1,0:T(8,128)S(1)} %get-tuple-element.49.refs_2_), custom_call_target="tpu_custom_call" | custom-call | bytes 104857600 | tf_op jit(solution)/shard_map/reorder/pallas_call | solution.py:169
  112.0 7.6 %all-to-all-start.3 = ((bf16[32,16,768]{2,1,0:T(8,128)(2,1)}), bf16[32,16,768]{2,1,0:T(8,128)(2,1)S(1)}, u32[]{:S(2)}, u32[]{:S(2)}) async-start(bf16[32,16,768]{2,1,0:T(8,128)(2,1)} %reorder.3), calls=%async_computation.3 | async-start | bytes 1572864 | tf_op jit(solution)/shard_map/all_to_all | solution.py:440
  119.6 1.3 collective-permute-done.12.refs_1_.refs_2_
  121.0 11.3 %collective-permute-done.13.refs_2_.refs_3_ = bf16[256,1152]{1,0:T(8,128)(2,1)S(1)} collective-permute-done((bf16[256,1152]{1,0:T(8,128)(2,1)}, bf16[256,1152]{1,0:T(8,128)(2,1)S(1)}, u32[]{:S(2)}, u32[]{:S(2)}) %collective-permute-start.13) | collective-permute-done | bytes 589856 | tf_op jit(solution)/shard_map/ppermute | solution.py:431
  133.2 1.6 %join_gradient.2.refs_2_ = bf16[128,9216]{1,0:T(8,128)(2,1)} custom-call(s32[2]{0:T(128)S(1)} %pad_add_fusion.refs_0_.at, bf16[256,1152]{1,0:T(8,128)(2,1)S(1)} %get-tuple-element.50.refs_0_.refs_1_, bf16[256,1152]{1,0:T(8,128)(2,1)S(1)} %collective-permute-done.12.refs_1_.refs_2_, bf16[256,1152]{1,0:T(8,128)(2,1)S(1)} %collective-permute-done.13.refs_2_.refs_3_, ...), custom_call_target="tpu_custom_call" | custom-call | bytes 4194304 | tf_op jit(solution)/shard_map/join_gradient/pallas_call | solution.py:91
  134.9 1.2 collective-permute-done.15.refs_1_
  136.1 1.6 %join_gradient.3 = bf16[128,9216]{1,0:T(8,128)(2,1)} custom-call(s32[2]{0:T(128)S(1)} %pad_add_fusion.refs_0_.at, bf16[4,128,1152]{2,1,0:T(8,128)(2,1)S(1)} %collective-permute-done.15.refs_1_, bf16[128,9216]{1,0:T(8,128)(2,1)} %join_gradient.2.refs_2_), custom_call_target="tpu_custom_call", output_to_operand_aliasing={{}: (2, {})} | custom-call | bytes 4194304 | tf_op jit(solution)/shard_map/join_gradient/pallas_call | solution.py:91
  137.7 3.8 %all-to-all-done.3 = bf16[32,16,768]{2,1,0:T(8,128)(2,1)S(1)} async-done(((bf16[32,16,768]{2,1,0:T(8,128)(2,1)}), bf16[32,16,768]{2,1,0:T(8,128)(2,1)S(1)}, u32[]{:S(2)}, u32[]{:S(2)}) %all-to-all-start.3) | async-done | bytes 786464 | tf_op jit(solution)/shard_map/all_to_all | solution.py:440
  (46 shorter events, 8.6 us)
Async XLA Ops:
  0.7 1.7 %copy-start = (bf16[1,128,9216]{2,1,0:T(8,128)(2,1)S(1)}, bf16[1,128,9216]{2,1,0:T(8,128)(2,1)}, u32[]{:S(2)}) copy-start(bf16[1,128,9216]{2,1,0:T(8,128)(2,1)} %param.5) | copy-start | bytes 7077892
  2.4 1.9 %copy-start.1 = (bf16[1,128,3072]{2,1,0:T(8,128)(2,1)S(1)}, bf16[1,128,3072]{2,1,0:T(8,128)(2,1)}, u32[]{:S(2)}) copy-start(bf16[1,128,3072]{2,1,0:T(8,128)(2,1)} %param.6) | copy-start | bytes 2359300
  4.2 12.5 %collective-permute-start = (bf16[4,128,1152]{2,1,0:T(8,128)(2,1)}, bf16[4,128,1152]{2,1,0:T(8,128)(2,1)S(1)}, u32[]{:S(2)}, u32[]{:S(2)}) collective-permute-start(bf16[4,128,1152]{2,1,0:T(8,128)(2,1)} %get-tuple-element.29), channel_id=1, source_target_pairs={{0,1},{1,0},{2,3},{3,2},{4,5},{5,4},{6,7},{7,6},{8,9},{9,8},{10,11... | collective-permute-start | bytes 3538952 | tf_op jit(solution)/shard_map/ppermute | solution.py:436
  5.2 34.7 %all-to-all-start = ((bf16[32,16,768]{2,1,0:T(8,128)(2,1)}), bf16[32,16,768]{2,1,0:T(8,128)(2,1)S(1)}, u32[]{:S(2)}, u32[]{:S(2)}) async-start(bf16[32,16,768]{2,1,0:T(8,128)(2,1)} %bitcast.9), calls=%async_computation | async-start | bytes 1572864 | tf_op jit(solution)/shard_map/all_to_all | solution.py:440
  16.7 23.2 %copy-start.2 = (s32[32]{0:T(128)S(1)}, s32[32]{0:T(128)}, u32[]{:S(2)}) copy-start(s32[32]{0:T(128)} %refs_0_.3) | copy-start | bytes 388
  18.2 29.0 %collective-permute-start.1 = (bf16[256,1152]{1,0:T(8,128)(2,1)}, bf16[256,1152]{1,0:T(8,128)(2,1)S(1)}, u32[]{:S(2)}, u32[]{:S(2)}) collective-permute-start(bf16[256,1152]{1,0:T(8,128)(2,1)} %get-tuple-element.31), channel_id=1, source_target_pairs={{0,2},{1,3},{2,4},{3,5},{4,6},{5,7},{6,0},{7,1},{8,10},{9,11},{10,... | collective-permute-start | bytes 1769480 | tf_op jit(solution)/shard_map/ppermute | solution.py:431
  18.8 28.5 %collective-permute-start.2 = (bf16[256,1152]{1,0:T(8,128)(2,1)}, bf16[256,1152]{1,0:T(8,128)(2,1)S(1)}, u32[]{:S(2)}, u32[]{:S(2)}) collective-permute-start(bf16[256,1152]{1,0:T(8,128)(2,1)} %get-tuple-element.32), channel_id=1, source_target_pairs={{0,4},{1,5},{2,6},{3,7},{4,0},{5,1},{6,2},{7,3},{8,12},{9,13},{10,... | collective-permute-start | bytes 1769480 | tf_op jit(solution)/shard_map/ppermute | solution.py:431
  21.2 27.2 %collective-permute-start.3 = (bf16[256,1152]{1,0:T(8,128)(2,1)}, bf16[256,1152]{1,0:T(8,128)(2,1)}, u32[]{:S(2)}, u32[]{:S(2)}) collective-permute-start(bf16[256,1152]{1,0:T(8,128)(2,1)} %get-tuple-element.33), channel_id=1, source_target_pairs={{0,6},{1,7},{2,0},{3,1},{4,2},{5,3},{6,4},{7,5},{8,14},{9,15},{10,... | collective-permute-start | bytes 1769480 | tf_op jit(solution)/shard_map/ppermute | solution.py:431
  41.6 6.8 %copy-start.3 = (bf16[256,1152]{1,0:T(8,128)(2,1)S(1)}, bf16[256,1152]{1,0:T(8,128)(2,1)}, u32[]{:S(2)}) copy-start(bf16[256,1152]{1,0:T(8,128)(2,1)} %get-tuple-element.30.refs_0_) | copy-start | bytes 1769476
  41.6 6.8 %copy-start.7 = (s32[32]{0:T(128)S(1)}, s32[32]{0:T(128)}, u32[]{:S(2)}) copy-start(s32[32]{0:T(128)} %lengths.3) | copy-start | bytes 388
  41.6 6.8 %copy-start.8 = (s32[32]{0:T(128)S(1)}, s32[32]{0:T(128)}, u32[]{:S(2)}) copy-start(s32[32]{0:T(128)} %text_lengths.3) | copy-start | bytes 388
  41.6 27.8 %all-to-all-start.1 = ((bf16[32,16,768]{2,1,0:T(8,128)(2,1)}), bf16[32,16,768]{2,1,0:T(8,128)(2,1)S(1)}, u32[]{:S(2)}, u32[]{:S(2)}) async-start(bf16[32,16,768]{2,1,0:T(8,128)(2,1)} %reorder.2), calls=%async_computation.1 | async-start | bytes 1572864 | tf_op jit(solution)/shard_map/all_to_all | solution.py:440
  47.3 10.7 %copy-start.4 = (bf16[256,1152]{1,0:T(8,128)(2,1)}, bf16[256,1152]{1,0:T(8,128)(2,1)S(1)}, u32[]{:S(2)}) copy-start(bf16[256,1152]{1,0:T(8,128)(2,1)S(1)} %collective-permute-done.2.refs_2_) | copy-start | bytes 1769476
  58.0 12.3 %collective-permute-start.4 = (bf16[256,384]{1,0:T(8,128)(2,1)S(1)}, bf16[256,384]{1,0:T(8,128)(2,1)S(1)}, u32[]{:S(2)}, u32[]{:S(2)}) collective-permute-start(bf16[256,384]{1,0:T(8,128)(2,1)S(1)} %get-tuple-element.35), channel_id=1, source_target_pairs={{0,6},{1,7},{2,0},{3,1},{4,2},{5,3},{6,4},{7,5},{8,14},{9,15},{10,... | collective-permute-start | bytes 589832 | tf_op jit(solution)/shard_map/ppermute | solution.py:431
  59.1 11.3 %collective-permute-start.5 = (bf16[256,384]{1,0:T(8,128)(2,1)S(1)}, bf16[256,384]{1,0:T(8,128)(2,1)S(1)}, u32[]{:S(2)}, u32[]{:S(2)}) collective-permute-start(bf16[256,384]{1,0:T(8,128)(2,1)S(1)} %get-tuple-element.36), channel_id=1, source_target_pairs={{0,4},{1,5},{2,6},{3,7},{4,0},{5,1},{6,2},{7,3},{8,12},{9,13},{10,... | collective-permute-start | bytes 589832 | tf_op jit(solution)/shard_map/ppermute | solution.py:431
  60.5 10.5 %collective-permute-start.6 = (bf16[256,384]{1,0:T(8,128)(2,1)S(1)}, bf16[256,384]{1,0:T(8,128)(2,1)S(1)}, u32[]{:S(2)}, u32[]{:S(2)}) collective-permute-start(bf16[256,384]{1,0:T(8,128)(2,1)S(1)} %get-tuple-element.37), channel_id=1, source_target_pairs={{0,2},{1,3},{2,4},{3,5},{4,6},{5,7},{6,0},{7,1},{8,10},{9,11},{10,... | collective-permute-start | bytes 589832 | tf_op jit(solution)/shard_map/ppermute | solution.py:431
  70.2 1.8 %collective-permute-start.8 = (bf16[4,128,384]{2,1,0:T(8,128)(2,1)S(1)}, bf16[4,128,384]{2,1,0:T(8,128)(2,1)S(1)}, u32[]{:S(2)}, u32[]{:S(2)}) collective-permute-start(bf16[4,128,384]{2,1,0:T(8,128)(2,1)S(1)} %bitcast.27), channel_id=1, source_target_pairs={{0,1},{1,0},{2,3},{3,2},{4,5},{5,4},{6,7},{7,6},{8,9},{9,8},{10,11... | collective-permute-start | bytes 1179656 | tf_op jit(solution)/shard_map/ppermute | solution.py:436
  71.5 4.6 %collective-permute-start.7 = (bf16[4,128,384]{2,1,0:T(8,128)(2,1)S(1)}, bf16[4,128,384]{2,1,0:T(8,128)(2,1)S(1)}, u32[]{:S(2)}, u32[]{:S(2)}) collective-permute-start(bf16[4,128,384]{2,1,0:T(8,128)(2,1)S(1)} %for_sibling.2), channel_id=1, source_target_pairs={{0,1},{1,0},{2,3},{3,2},{4,5},{5,4},{6,7},{7,6},{8,9},{9,8},{10,11... | collective-permute-start | bytes 1179656 | tf_op jit(solution)/shard_map/ppermute | solution.py:436
  73.0 14.3 %collective-permute-start.9 = (bf16[256,384]{1,0:T(8,128)(2,1)}, bf16[256,384]{1,0:T(8,128)(2,1)S(1)}, u32[]{:S(2)}, u32[]{:S(2)}) collective-permute-start(bf16[256,384]{1,0:T(8,128)(2,1)} %get-tuple-element.44), channel_id=1, source_target_pairs={{0,2},{1,3},{2,4},{3,5},{4,6},{5,7},{6,0},{7,1},{8,10},{9,11},{10,... | collective-permute-start | bytes 589832 | tf_op jit(solution)/shard_map/ppermute | solution.py:431
  75.2 12.1 %collective-permute-start.10 = (bf16[256,384]{1,0:T(8,128)(2,1)}, bf16[256,384]{1,0:T(8,128)(2,1)S(1)}, u32[]{:S(2)}, u32[]{:S(2)}) collective-permute-start(bf16[256,384]{1,0:T(8,128)(2,1)} %get-tuple-element.45), channel_id=1, source_target_pairs={{0,4},{1,5},{2,6},{3,7},{4,0},{5,1},{6,2},{7,3},{8,12},{9,13},{10,... | collective-permute-start | bytes 589832 | tf_op jit(solution)/shard_map/ppermute | solution.py:431
  75.7 12.1 %collective-permute-start.11 = (bf16[256,384]{1,0:T(8,128)(2,1)}, bf16[256,384]{1,0:T(8,128)(2,1)S(1)}, u32[]{:S(2)}, u32[]{:S(2)}) collective-permute-start(bf16[256,384]{1,0:T(8,128)(2,1)} %get-tuple-element.46), channel_id=1, source_target_pairs={{0,6},{1,7},{2,0},{3,1},{4,2},{5,3},{6,4},{7,5},{8,14},{9,15},{10,... | collective-permute-start | bytes 589832 | tf_op jit(solution)/shard_map/ppermute | solution.py:431
  77.6 10.2 %copy-start.6 = (bf16[256,384]{1,0:T(8,128)(2,1)S(1)}, bf16[256,384]{1,0:T(8,128)(2,1)}, u32[]{:S(2)}) copy-start(bf16[256,384]{1,0:T(8,128)(2,1)} %get-tuple-element.43.refs_4_) | copy-start | bytes 589828
  77.6 10.2 %copy-start.10 = (f32[3,1,1024]{2,1,0:T(1,128)S(1)}, f32[3,1,1024]{2,1,0:T(1,128)}, u32[]{:S(2)}) copy-start(f32[3,1,1024]{2,1,0:T(1,128)} %get-tuple-element.48.refs_9_) | copy-start | bytes 36868
  77.6 32.7 %all-to-all-start.2 = ((bf16[32,16,768]{2,1,0:T(8,128)(2,1)}), bf16[32,16,768]{2,1,0:T(8,128)(2,1)S(1)}, u32[]{:S(2)}, u32[]{:S(2)}) async-start(bf16[32,16,768]{2,1,0:T(8,128)(2,1)} %bitcast.13), calls=%async_computation.2 | async-start | bytes 1572864 | tf_op jit(solution)/shard_map/all_to_all | solution.py:440
  87.8 1.1 copy-start.5
  88.9 1.4 copy-start.9
  103.2 17.8 %collective-permute-start.12 = (bf16[256,1152]{1,0:T(8,128)(2,1)}, bf16[256,1152]{1,0:T(8,128)(2,1)S(1)}, u32[]{:S(2)}, u32[]{:S(2)}) collective-permute-start(bf16[256,1152]{1,0:T(8,128)(2,1)} %get-tuple-element.51), channel_id=1, source_target_pairs={{0,6},{1,7},{2,0},{3,1},{4,2},{5,3},{6,4},{7,5},{8,14},{9,15},{10,... | collective-permute-start | bytes 1769480 | tf_op jit(solution)/shard_map/ppermute | solution.py:431
  105.3 27.0 %collective-permute-start.13 = (bf16[256,1152]{1,0:T(8,128)(2,1)}, bf16[256,1152]{1,0:T(8,128)(2,1)S(1)}, u32[]{:S(2)}, u32[]{:S(2)}) collective-permute-start(bf16[256,1152]{1,0:T(8,128)(2,1)} %get-tuple-element.52), channel_id=1, source_target_pairs={{0,4},{1,5},{2,6},{3,7},{4,0},{5,1},{6,2},{7,3},{8,12},{9,13},{10,... | collective-permute-start | bytes 1769480 | tf_op jit(solution)/shard_map/ppermute | solution.py:431
  106.5 26.4 %collective-permute-start.14 = (bf16[256,1152]{1,0:T(8,128)(2,1)}, bf16[256,1152]{1,0:T(8,128)(2,1)S(1)}, u32[]{:S(2)}, u32[]{:S(2)}) collective-permute-start(bf16[256,1152]{1,0:T(8,128)(2,1)} %get-tuple-element.53), channel_id=1, source_target_pairs={{0,2},{1,3},{2,4},{3,5},{4,6},{5,7},{6,0},{7,1},{8,10},{9,11},{10,... | collective-permute-start | bytes 1769480 | tf_op jit(solution)/shard_map/ppermute | solution.py:431
  112.0 29.5 %all-to-all-start.3 = ((bf16[32,16,768]{2,1,0:T(8,128)(2,1)}), bf16[32,16,768]{2,1,0:T(8,128)(2,1)S(1)}, u32[]{:S(2)}, u32[]{:S(2)}) async-start(bf16[32,16,768]{2,1,0:T(8,128)(2,1)} %reorder.3), calls=%async_computation.3 | async-start | bytes 1572864 | tf_op jit(solution)/shard_map/all_to_all | solution.py:440
  133.1 2.9 %collective-permute-start.15 = (bf16[4,128,1152]{2,1,0:T(8,128)(2,1)S(1)}, bf16[4,128,1152]{2,1,0:T(8,128)(2,1)S(1)}, u32[]{:S(2)}, u32[]{:S(2)}) collective-permute-start(bf16[4,128,1152]{2,1,0:T(8,128)(2,1)S(1)} %for_sibling.3.refs_5_), channel_id=1, source_target_pairs={{0,1},{1,0},{2,3},{3,2},{4,5},{5,4},{6,7},{7,6},{8,9},{9,8},{10,11... | collective-permute-start | bytes 3538952 | tf_op jit(solution)/shard_map/ppermute | solution.py:436

commit v5 on v4

--- a/solution.py
+++ b/solution.py
@@ -59,21 +59,44 @@
     return lax.bitwise_and(lax.shift_right_logical(at[0], 1) + k, CHIPS - 1), at[0] & 1
 
 
-def split_projected(at, projected, *late):
-    def body(at_ref, x_ref, own, other):
-        for k in range(CHIPS):
-            chip, core = place(at_ref, k)
-            for out, head in ((own, 2 * chip + core), (other, 2 * chip + 1 - core)):
-                for t in range(3):
-                    start = pl.multiple_of(t * WIDTH + head * GRP, GRP)
-                    yield x_ref.at[:, pl.ds(start, GRP)], out.at[k, :, pl.ds(t * GRP, GRP)]
-
-    return copies(body, 6 * CHIPS, 2, len(late))(
-        out_shape=[jax.ShapeDtypeStruct((CHIPS, ROWS, 3 * GRP), BF)] * 2,
-        in_specs=[SMEM, ANY] + [ANY] * len(late),
+def split_kernel(at, x_ref, own, other, mine, theirs, in_sems, out_sems):
+    arriving, leaving = [], []
+    for k in range(CHIPS):
+        chip, core = place(at, k)
+        for side, (held, head) in enumerate(((theirs, 2 * chip + 1 - core), (mine, 2 * chip + core))):
+            group = []
+            for t in range(3):
+                start = pl.multiple_of(t * WIDTH + head * GRP, GRP)
+                src = x_ref.at[:, pl.ds(start, GRP)]
+                dst = held.at[k, :, pl.ds(t * GRP, GRP)]
+                group.append(pltpu.make_async_copy(src, dst, in_sems.at[k, side, t]))
+            arriving.append(group)
+            out = (other, own)[side].at[k]
+            leaving.append(pltpu.make_async_copy(held.at[k], out, out_sems.at[k, side]))
+    for group in arriving:
+        begin(group)
+    for group, cp in zip(arriving, leaving):
+        finish(group)
+        cp.start()
+    finish(leaving)
+
+
+def split_projected(at, projected):
+    return pl.pallas_call(
+        split_kernel,
+        out_shape=[pltpu.HBM((CHIPS, ROWS, 3 * GRP), BF)] * 2,
+        in_specs=[SMEM, ANY],
         out_specs=[ANY] * 2,
+        scratch_shapes=[
+            pltpu.VMEM((CHIPS, ROWS, 3 * GRP), BF),
+            pltpu.VMEM((CHIPS, ROWS, 3 * GRP), BF),
+            pltpu.SemaphoreType.DMA((CHIPS, 2, 3)),
+            pltpu.SemaphoreType.DMA((CHIPS, 2)),
+        ],
+        compiler_params=pltpu.CompilerParams(vmem_limit_bytes=62 << 20),
+        cost_estimate=pl.CostEstimate(flops=0, bytes_accessed=4 << 20, transcendentals=0),
         name="split_projected",
-    )(at, projected, *late)
+    )(at, projected)
 
 
 def join_gradient(at, parts, own, so_far, *late):

time: 143 us -> 145 us (1.014)
  Pallas kernels: 38.2 us -> 39.8 us
    pallas_call x1, Pallas kernels: 1.8 us -> 3.4 us  [split_projected(): pl.pallas_call(split_kernel, out_shape=[pltpu.HBM((CHIPS, ROWS, 3 * GRP),...]
    unnamed x22 -> x26, local copies, waits for them, and re-layouts: 4.18 us -> 3.65 us
  transfers between devices with their start and end apart: 20 -> 20, of which waited for: 13 -> 12; matrix products, arithmetic and copies ran while one was open for 0% -> 0% of each run, Pallas kernels for 25% -> 25%
where the time goes in v5:
time: 145 us; the launch traced here: 144 us
  starting transfers between devices  50.3 us (35%)
  waiting for transfers between devices  48.8 us (34%)
  Pallas kernels  39.8 us (27%)
  local copies, waits for them, and re-layouts  3.65 us (3%)
    all_to_all x4, starting transfers between devices, spread(): return lax.all_to_all(pieces, 'dp', split_axis=0, concat_axis=0, tiled=True)  34.5 us
    all_to_all x4, waiting for transfers between devices, spread(): return lax.all_to_all(pieces, 'dp', split_axis=0, concat_axis=0, tiled=True)  31.7 us
    ppermute x12, waiting for transfers between devices, turn(): out.append(lax.ppermute(blocks[k], 'seq', pairs))  15.6 us
    ppermute x12, starting transfers between devices, turn(): out.append(lax.ppermute(blocks[k], 'seq', pairs))  15.5 us
    pallas_call x1, Pallas kernels, backward(): pl.pallas_call(backward_kernel, grid=(1,), out_shape=[jax.ShapeDtypeStruc...  12.9 us
    pallas_call x1, Pallas kernels, forward(): pl.pallas_call(forward_kernel, grid=(1,), out_shape=[jax.ShapeDtypeStruct...  9.59 us
    unnamed x26, local copies, waits for them, and re-layouts  3.65 us
    pallas_call x1, Pallas kernels, split_projected(): pl.pallas_call(split_kernel, out_shape=[pltpu.HBM((CHIPS, ROWS, 3 * GRP),...  3.4 us
  transfers between devices with their start and end apart: 20, of which 12 were waited for; matrix products, arithmetic and copies ran while one was open for 0% of the time, Pallas kernels for 25%

profile of v5, /device:TPU:6, one launch (start us, length us, event | category | flops | bytes accessed | tf_op | source)
XLA Modules:
  0.0 144.4 jit_solution(15600047104665543830)
XLA Ops:
  1.3 3.4 %split_projected.1 = (bf16[4,128,1152]{2,1,0:T(8,128)(2,1)}, bf16[4,128,1152]{2,1,0:T(8,128)(2,1)}) custom-call(s32[2]{0:T(128)} %pad_add_fusion.at.refs_0_, bf16[128,9216]{1,0:T(8,128)(2,1)} %bitcast.28), custom_call_target="tpu_custom_call" | custom-call | bytes 4194304 | tf_op jit(solution)/shard_map/split_projected/pallas_call | solution.py:85
  4.8 1.1 copy-done.1
  6.9 11.6 %all-to-all-start = ((bf16[32,16,768]{2,1,0:T(8,128)(2,1)}), bf16[32,16,768]{2,1,0:T(8,128)(2,1)S(1)}, u32[]{:S(2)}, u32[]{:S(2)}) async-start(bf16[32,16,768]{2,1,0:T(8,128)(2,1)} %bitcast.9), calls=%async_computation | async-start | bytes 1572864 | tf_op jit(solution)/shard_map/all_to_all | solution.py:463
  18.5 1.5 %pair.2 = (bf16[256,1152]{1,0:T(8,128)(2,1)}, bf16[256,1152]{1,0:T(8,128)(2,1)}, bf16[256,1152]{1,0:T(8,128)(2,1)}, bf16[256,1152]{1,0:T(8,128)(2,1)}, f32[8,128]{1,0:T(8,128)S(1)}) custom-call(bf16[4,128,1152]{2,1,0:T(8,128)(2,1)S(1)} %copy-done, bf16[4,128,1152]{2,1,0:T(8,128)(2,1)S(1)} %collective-permute-done.refs_1_), custom_call_target="tpu_custom_call" | custom-call | bytes 4194304 | tf_op jit(solution)/shard_map/pair/pallas_call | solution.py:132
  20.6 2.4 %collective-permute-start.2 = (bf16[256,1152]{1,0:T(8,128)(2,1)}, bf16[256,1152]{1,0:T(8,128)(2,1)S(1)}, u32[]{:S(2)}, u32[]{:S(2)}) collective-permute-start(bf16[256,1152]{1,0:T(8,128)(2,1)} %get-tuple-element.32), channel_id=1, source_target_pairs={{0,4},{1,5},{2,6},{3,7},{4,0},{5,1},{6,2},{7,3},{8,12},{9,13},{10,... | collective-permute-start | bytes 1769480 | tf_op jit(solution)/shard_map/ppermute | solution.py:454
  23.0 18.7 %all-to-all-done.refs_1_ = bf16[32,16,768]{2,1,0:T(8,128)(2,1)S(1)} async-done(((bf16[32,16,768]{2,1,0:T(8,128)(2,1)}), bf16[32,16,768]{2,1,0:T(8,128)(2,1)S(1)}, u32[]{:S(2)}, u32[]{:S(2)}) %all-to-all-start) | async-done | bytes 786464 | tf_op jit(solution)/shard_map/all_to_all | solution.py:463
  41.7 1.7 %reorder.2 = bf16[32,16,768]{2,1,0:T(8,128)(2,1)} custom-call(s32[32]{0:T(128)S(1)} %copy-done.3, bf16[32,16,768]{2,1,0:T(8,128)(2,1)S(1)} %all-to-all-done.refs_1_, f32[8,128]{1,0:T(8,128)S(1)} %get-tuple-element.38.refs_2_), custom_call_target="tpu_custom_call" | custom-call | bytes 104857600 | tf_op jit(solution)/shard_map/reorder/pallas_call | solution.py:192
  43.4 5.6 %all-to-all-start.1 = ((bf16[32,16,768]{2,1,0:T(8,128)(2,1)}), bf16[32,16,768]{2,1,0:T(8,128)(2,1)S(1)}, u32[]{:S(2)}, u32[]{:S(2)}) async-start(bf16[32,16,768]{2,1,0:T(8,128)(2,1)} %reorder.2), calls=%async_computation.1 | async-start | bytes 1572864 | tf_op jit(solution)/shard_map/all_to_all | solution.py:463
  49.1 1.1 collective-permute-done.3.refs_3_
  50.2 9.6 %attend.1 = (bf16[256,384]{1,0:T(8,128)(2,1)S(1)}, bf16[256,384]{1,0:T(8,128)(2,1)S(1)}, bf16[256,384]{1,0:T(8,128)(2,1)S(1)}, bf16[256,384]{1,0:T(8,128)(2,1)S(...) custom-call(s32[2]{0:T(128)S(1)} %copy-done.2, s32[32]{0:T(128)S(1)} %copy-done.9, ...), custom_call_target="tpu_custom_call" | custom-call | flops 80530636800 | bytes 12582912 | tf_op jit(solution)/shard_map/attend/pallas_call | solution.py:400
  59.8 1.0 collective-permute-start.4
  60.9 1.4 collective-permute-start.5
  62.2 2.0 %collective-permute-start.6 = (bf16[256,384]{1,0:T(8,128)(2,1)S(1)}, bf16[256,384]{1,0:T(8,128)(2,1)S(1)}, u32[]{:S(2)}, u32[]{:S(2)}) collective-permute-start(bf16[256,384]{1,0:T(8,128)(2,1)S(1)} %get-tuple-element.37), channel_id=1, source_target_pairs={{0,2},{1,3},{2,4},{3,5},{4,6},{5,7},{6,0},{7,1},{8,10},{9,11},{10,... | collective-permute-start | bytes 589832 | tf_op jit(solution)/shard_map/ppermute | solution.py:454
  64.3 7.0 %all-to-all-done.1 = bf16[32,16,768]{2,1,0:T(8,128)(2,1)S(1)} async-done(((bf16[32,16,768]{2,1,0:T(8,128)(2,1)}), bf16[32,16,768]{2,1,0:T(8,128)(2,1)S(1)}, u32[]{:S(2)}, u32[]{:S(2)}) %all-to-all-start.1) | async-done | bytes 786464 | tf_op jit(solution)/shard_map/all_to_all | solution.py:463
  74.8 2.2 %collective-permute-start.9 = (bf16[256,384]{1,0:T(8,128)(2,1)}, bf16[256,384]{1,0:T(8,128)(2,1)S(1)}, u32[]{:S(2)}, u32[]{:S(2)}) collective-permute-start(bf16[256,384]{1,0:T(8,128)(2,1)} %get-tuple-element.44), channel_id=1, source_target_pairs={{0,2},{1,3},{2,4},{3,5},{4,6},{5,7},{6,0},{7,1},{8,10},{9,11},{10,... | collective-permute-start | bytes 589832 | tf_op jit(solution)/shard_map/ppermute | solution.py:454
  77.9 1.5 %join_pieces.1 = bf16[8,4,16,768]{3,2,1,0:T(8,128)(2,1)} custom-call(s32[2]{0:T(128)S(1)} %copy-done.2, bf16[16,16,384]{2,1,0:T(8,128)(2,1)S(1)} %bitcast.19, bf16[16,16,384]{2,1,0:T(8,128)(2,1)S(1)} %bitcast.20, bf16[16,16,384]{2,1,0:T(8,128)(2,1)S(1)} %bitcast.21, bf16[16,16,384]{2,1,0:T(8,128)(2,1)S(1)} %bitcast.22, bf16[4,8,16,384]{3,2,1,0:T(8,128)(2,1)S(1)} %bitcast.25, ...), custom_call_target="tpu_custom_call" | custom-call | bytes 4194304 | tf_op jit(solution)/shard_map/join_pieces/pallas_call | solution.py:226
  79.4 9.6 %all-to-all-start.2 = ((bf16[32,16,768]{2,1,0:T(8,128)(2,1)}), bf16[32,16,768]{2,1,0:T(8,128)(2,1)S(1)}, u32[]{:S(2)}, u32[]{:S(2)}) async-start(bf16[32,16,768]{2,1,0:T(8,128)(2,1)} %bitcast.13), calls=%async_computation.2 | async-start | bytes 1572864 | tf_op jit(solution)/shard_map/all_to_all | solution.py:463
  89.6 1.1 copy-done.7
  90.7 1.4 copy-done.11
  92.1 12.9 %attend_grad.1 = (bf16[256,1152]{1,0:T(8,128)(2,1)S(1)}, bf16[256,1152]{1,0:T(8,128)(2,1)}, bf16[256,1152]{1,0:T(8,128)(2,1)}, bf16[256,1152]{1,0:T(8,128)(2,1)}, f32[8,128]{1,0:T(8,128)S(1)}) custom-call(s32[2]{0:T(128)S(1)} %copy-done.2, s32[32]{0:T(128)S(1)} %copy-done.9, s32[32]{0:T(128)S(1)} %copy-done.10, bf16[256,1152]{1,0:T(8,128)(2,1)S(1)} %copy-done.5, ...), custom_call_target="tpu_custom_call" | custom-call | flops 128849018880 | bytes 16777216 | tf_op jit(solution)/shard_map/attend_grad/pallas_call | solution.py:424
  105.0 2.1 %collective-permute-start.12 = (bf16[256,1152]{1,0:T(8,128)(2,1)}, bf16[256,1152]{1,0:T(8,128)(2,1)S(1)}, u32[]{:S(2)}, u32[]{:S(2)}) collective-permute-start(bf16[256,1152]{1,0:T(8,128)(2,1)} %get-tuple-element.51), channel_id=1, source_target_pairs={{0,6},{1,7},{2,0},{3,1},{4,2},{5,3},{6,4},{7,5},{8,14},{9,15},{10,... | collective-permute-start | bytes 1769480 | tf_op jit(solution)/shard_map/ppermute | solution.py:454
  107.1 1.2 collective-permute-start.13
  108.3 1.6 %collective-permute-start.14 = (bf16[256,1152]{1,0:T(8,128)(2,1)}, bf16[256,1152]{1,0:T(8,128)(2,1)S(1)}, u32[]{:S(2)}, u32[]{:S(2)}) collective-permute-start(bf16[256,1152]{1,0:T(8,128)(2,1)} %get-tuple-element.53), channel_id=1, source_target_pairs={{0,2},{1,3},{2,4},{3,5},{4,6},{5,7},{6,0},{7,1},{8,10},{9,11},{10,... | collective-permute-start | bytes 1769480 | tf_op jit(solution)/shard_map/ppermute | solution.py:454
  109.9 2.2 %all-to-all-done.2.refs_1_ = bf16[32,16,768]{2,1,0:T(8,128)(2,1)S(1)} async-done(((bf16[32,16,768]{2,1,0:T(8,128)(2,1)}), bf16[32,16,768]{2,1,0:T(8,128)(2,1)S(1)}, u32[]{:S(2)}, u32[]{:S(2)}) %all-to-all-start.2) | async-done | bytes 786464 | tf_op jit(solution)/shard_map/all_to_all | solution.py:463
  112.1 1.7 %reorder.3 = bf16[32,16,768]{2,1,0:T(8,128)(2,1)} custom-call(s32[32]{0:T(128)S(1)} %copy-done.4, bf16[32,16,768]{2,1,0:T(8,128)(2,1)S(1)} %all-to-all-done.2.refs_1_, f32[8,128]{1,0:T(8,128)S(1)} %get-tuple-element.49.refs_2_), custom_call_target="tpu_custom_call" | custom-call | bytes 104857600 | tf_op jit(solution)/shard_map/reorder/pallas_call | solution.py:192
  113.8 7.6 %all-to-all-start.3 = ((bf16[32,16,768]{2,1,0:T(8,128)(2,1)}), bf16[32,16,768]{2,1,0:T(8,128)(2,1)S(1)}, u32[]{:S(2)}, u32[]{:S(2)}) async-start(bf16[32,16,768]{2,1,0:T(8,128)(2,1)} %reorder.3), calls=%async_computation.3 | async-start | bytes 1572864 | tf_op jit(solution)/shard_map/all_to_all | solution.py:463
  121.4 1.4 collective-permute-done.12.refs_1_.refs_2_
  122.8 11.3 %collective-permute-done.13.refs_2_.refs_3_ = bf16[256,1152]{1,0:T(8,128)(2,1)S(1)} collective-permute-done((bf16[256,1152]{1,0:T(8,128)(2,1)}, bf16[256,1152]{1,0:T(8,128)(2,1)S(1)}, u32[]{:S(2)}, u32[]{:S(2)}) %collective-permute-start.13) | collective-permute-done | bytes 589856 | tf_op jit(solution)/shard_map/ppermute | solution.py:454
  135.0 1.6 %join_gradient.2.refs_2_ = bf16[128,9216]{1,0:T(8,128)(2,1)} custom-call(s32[2]{0:T(128)S(1)} %copy-done.2, bf16[256,1152]{1,0:T(8,128)(2,1)S(1)} %get-tuple-element.50.refs_0_.refs_1_, bf16[256,1152]{1,0:T(8,128)(2,1)S(1)} %collective-permute-done.12.refs_1_.refs_2_, bf16[256,1152]{1,0:T(8,128)(2,1)S(1)} %collective-permute-done.13.refs_2_.refs_3_, ...), custom_call_target="tpu_custom_call" | custom-call | bytes 4194304 | tf_op jit(solution)/shard_map/join_gradient/pallas_call | solution.py:114
  136.7 1.2 collective-permute-done.15.refs_1_
  137.9 1.6 %join_gradient.3 = bf16[128,9216]{1,0:T(8,128)(2,1)} custom-call(s32[2]{0:T(128)S(1)} %copy-done.2, bf16[4,128,1152]{2,1,0:T(8,128)(2,1)S(1)} %collective-permute-done.15.refs_1_, bf16[128,9216]{1,0:T(8,128)(2,1)} %join_gradient.2.refs_2_), custom_call_target="tpu_custom_call", output_to_operand_aliasing={{}: (2, {})} | custom-call | bytes 4194304 | tf_op jit(solution)/shard_map/join_gradient/pallas_call | solution.py:114
  139.5 3.8 %all-to-all-done.3 = bf16[32,16,768]{2,1,0:T(8,128)(2,1)S(1)} async-done(((bf16[32,16,768]{2,1,0:T(8,128)(2,1)}), bf16[32,16,768]{2,1,0:T(8,128)(2,1)S(1)}, u32[]{:S(2)}, u32[]{:S(2)}) %all-to-all-start.3) | async-done | bytes 786464 | tf_op jit(solution)/shard_map/all_to_all | solution.py:463
  (50 shorter events, 9.2 us)
Async XLA Ops:
  4.7 13.8 %collective-permute-start = (bf16[4,128,1152]{2,1,0:T(8,128)(2,1)}, bf16[4,128,1152]{2,1,0:T(8,128)(2,1)S(1)}, u32[]{:S(2)}, u32[]{:S(2)}) collective-permute-start(bf16[4,128,1152]{2,1,0:T(8,128)(2,1)} %get-tuple-element.29), channel_id=1, source_target_pairs={{0,1},{1,0},{2,3},{3,2},{4,5},{5,4},{6,7},{7,6},{8,9},{9,8},{10,11... | collective-permute-start | bytes 3538952 | tf_op jit(solution)/shard_map/ppermute | solution.py:459
  4.8 1.1 copy-start.1
  6.9 11.7 %copy-start = (bf16[4,128,1152]{2,1,0:T(8,128)(2,1)S(1)}, bf16[4,128,1152]{2,1,0:T(8,128)(2,1)}, u32[]{:S(2)}) copy-start(bf16[4,128,1152]{2,1,0:T(8,128)(2,1)} %get-tuple-element.28.refs_0_) | copy-start | bytes 3538948
  6.9 34.8 %all-to-all-start = ((bf16[32,16,768]{2,1,0:T(8,128)(2,1)}), bf16[32,16,768]{2,1,0:T(8,128)(2,1)S(1)}, u32[]{:S(2)}, u32[]{:S(2)}) async-start(bf16[32,16,768]{2,1,0:T(8,128)(2,1)} %bitcast.9), calls=%async_computation | async-start | bytes 1572864 | tf_op jit(solution)/shard_map/all_to_all | solution.py:463
  18.5 23.2 %copy-start.3 = (s32[32]{0:T(128)S(1)}, s32[32]{0:T(128)}, u32[]{:S(2)}) copy-start(s32[32]{0:T(128)} %refs_0_.3) | copy-start | bytes 388
  20.0 29.1 %collective-permute-start.1 = (bf16[256,1152]{1,0:T(8,128)(2,1)}, bf16[256,1152]{1,0:T(8,128)(2,1)S(1)}, u32[]{:S(2)}, u32[]{:S(2)}) collective-permute-start(bf16[256,1152]{1,0:T(8,128)(2,1)} %get-tuple-element.31), channel_id=1, source_target_pairs={{0,2},{1,3},{2,4},{3,5},{4,6},{5,7},{6,0},{7,1},{8,10},{9,11},{10,... | collective-permute-start | bytes 1769480 | tf_op jit(solution)/shard_map/ppermute | solution.py:454
  20.6 28.5 %collective-permute-start.2 = (bf16[256,1152]{1,0:T(8,128)(2,1)}, bf16[256,1152]{1,0:T(8,128)(2,1)S(1)}, u32[]{:S(2)}, u32[]{:S(2)}) collective-permute-start(bf16[256,1152]{1,0:T(8,128)(2,1)} %get-tuple-element.32), channel_id=1, source_target_pairs={{0,4},{1,5},{2,6},{3,7},{4,0},{5,1},{6,2},{7,3},{8,12},{9,13},{10,... | collective-permute-start | bytes 1769480 | tf_op jit(solution)/shard_map/ppermute | solution.py:454
  23.0 27.2 %collective-permute-start.3 = (bf16[256,1152]{1,0:T(8,128)(2,1)}, bf16[256,1152]{1,0:T(8,128)(2,1)}, u32[]{:S(2)}, u32[]{:S(2)}) collective-permute-start(bf16[256,1152]{1,0:T(8,128)(2,1)} %get-tuple-element.33), channel_id=1, source_target_pairs={{0,6},{1,7},{2,0},{3,1},{4,2},{5,3},{6,4},{7,5},{8,14},{9,15},{10,... | collective-permute-start | bytes 1769480 | tf_op jit(solution)/shard_map/ppermute | solution.py:454
  43.4 6.8 %copy-start.2 = (s32[2]{0:T(128)S(1)}, s32[2]{0:T(128)}, u32[]{:S(2)}) copy-start(s32[2]{0:T(128)} %pad_add_fusion.at.refs_0_) | copy-start | bytes 28
  43.4 6.8 %copy-start.5 = (bf16[256,1152]{1,0:T(8,128)(2,1)S(1)}, bf16[256,1152]{1,0:T(8,128)(2,1)}, u32[]{:S(2)}) copy-start(bf16[256,1152]{1,0:T(8,128)(2,1)} %get-tuple-element.30.refs_0_) | copy-start | bytes 1769476
  43.4 6.8 %copy-start.9 = (s32[32]{0:T(128)S(1)}, s32[32]{0:T(128)}, u32[]{:S(2)}) copy-start(s32[32]{0:T(128)} %lengths.3) | copy-start | bytes 388
  43.4 6.8 %copy-start.10 = (s32[32]{0:T(128)S(1)}, s32[32]{0:T(128)}, u32[]{:S(2)}) copy-start(s32[32]{0:T(128)} %text_lengths.3) | copy-start | bytes 388
  43.4 27.8 %all-to-all-start.1 = ((bf16[32,16,768]{2,1,0:T(8,128)(2,1)}), bf16[32,16,768]{2,1,0:T(8,128)(2,1)S(1)}, u32[]{:S(2)}, u32[]{:S(2)}) async-start(bf16[32,16,768]{2,1,0:T(8,128)(2,1)} %reorder.2), calls=%async_computation.1 | async-start | bytes 1572864 | tf_op jit(solution)/shard_map/all_to_all | solution.py:463
  49.1 10.7 %copy-start.6 = (bf16[256,1152]{1,0:T(8,128)(2,1)}, bf16[256,1152]{1,0:T(8,128)(2,1)S(1)}, u32[]{:S(2)}) copy-start(bf16[256,1152]{1,0:T(8,128)(2,1)S(1)} %collective-permute-done.2.refs_2_) | copy-start | bytes 1769476
  59.8 12.3 %collective-permute-start.4 = (bf16[256,384]{1,0:T(8,128)(2,1)S(1)}, bf16[256,384]{1,0:T(8,128)(2,1)S(1)}, u32[]{:S(2)}, u32[]{:S(2)}) collective-permute-start(bf16[256,384]{1,0:T(8,128)(2,1)S(1)} %get-tuple-element.35), channel_id=1, source_target_pairs={{0,6},{1,7},{2,0},{3,1},{4,2},{5,3},{6,4},{7,5},{8,14},{9,15},{10,... | collective-permute-start | bytes 589832 | tf_op jit(solution)/shard_map/ppermute | solution.py:454
  60.9 11.3 %collective-permute-start.5 = (bf16[256,384]{1,0:T(8,128)(2,1)S(1)}, bf16[256,384]{1,0:T(8,128)(2,1)S(1)}, u32[]{:S(2)}, u32[]{:S(2)}) collective-permute-start(bf16[256,384]{1,0:T(8,128)(2,1)S(1)} %get-tuple-element.36), channel_id=1, source_target_pairs={{0,4},{1,5},{2,6},{3,7},{4,0},{5,1},{6,2},{7,3},{8,12},{9,13},{10,... | collective-permute-start | bytes 589832 | tf_op jit(solution)/shard_map/ppermute | solution.py:454
  62.2 10.5 %collective-permute-start.6 = (bf16[256,384]{1,0:T(8,128)(2,1)S(1)}, bf16[256,384]{1,0:T(8,128)(2,1)S(1)}, u32[]{:S(2)}, u32[]{:S(2)}) collective-permute-start(bf16[256,384]{1,0:T(8,128)(2,1)S(1)} %get-tuple-element.37), channel_id=1, source_target_pairs={{0,2},{1,3},{2,4},{3,5},{4,6},{5,7},{6,0},{7,1},{8,10},{9,11},{10,... | collective-permute-start | bytes 589832 | tf_op jit(solution)/shard_map/ppermute | solution.py:454
  72.0 1.8 %collective-permute-start.8 = (bf16[4,128,384]{2,1,0:T(8,128)(2,1)S(1)}, bf16[4,128,384]{2,1,0:T(8,128)(2,1)S(1)}, u32[]{:S(2)}, u32[]{:S(2)}) collective-permute-start(bf16[4,128,384]{2,1,0:T(8,128)(2,1)S(1)} %bitcast.26), channel_id=1, source_target_pairs={{0,1},{1,0},{2,3},{3,2},{4,5},{5,4},{6,7},{7,6},{8,9},{9,8},{10,11... | collective-permute-start | bytes 1179656 | tf_op jit(solution)/shard_map/ppermute | solution.py:459
  73.3 4.6 %collective-permute-start.7 = (bf16[4,128,384]{2,1,0:T(8,128)(2,1)S(1)}, bf16[4,128,384]{2,1,0:T(8,128)(2,1)S(1)}, u32[]{:S(2)}, u32[]{:S(2)}) collective-permute-start(bf16[4,128,384]{2,1,0:T(8,128)(2,1)S(1)} %for_sibling.2), channel_id=1, source_target_pairs={{0,1},{1,0},{2,3},{3,2},{4,5},{5,4},{6,7},{7,6},{8,9},{9,8},{10,11... | collective-permute-start | bytes 1179656 | tf_op jit(solution)/shard_map/ppermute | solution.py:459
  74.8 14.3 %collective-permute-start.9 = (bf16[256,384]{1,0:T(8,128)(2,1)}, bf16[256,384]{1,0:T(8,128)(2,1)S(1)}, u32[]{:S(2)}, u32[]{:S(2)}) collective-permute-start(bf16[256,384]{1,0:T(8,128)(2,1)} %get-tuple-element.44), channel_id=1, source_target_pairs={{0,2},{1,3},{2,4},{3,5},{4,6},{5,7},{6,0},{7,1},{8,10},{9,11},{10,... | collective-permute-start | bytes 589832 | tf_op jit(solution)/shard_map/ppermute | solution.py:454
  76.9 12.1 %collective-permute-start.10 = (bf16[256,384]{1,0:T(8,128)(2,1)}, bf16[256,384]{1,0:T(8,128)(2,1)S(1)}, u32[]{:S(2)}, u32[]{:S(2)}) collective-permute-start(bf16[256,384]{1,0:T(8,128)(2,1)} %get-tuple-element.45), channel_id=1, source_target_pairs={{0,4},{1,5},{2,6},{3,7},{4,0},{5,1},{6,2},{7,3},{8,12},{9,13},{10,... | collective-permute-start | bytes 589832 | tf_op jit(solution)/shard_map/ppermute | solution.py:454
  77.5 12.1 %collective-permute-start.11 = (bf16[256,384]{1,0:T(8,128)(2,1)}, bf16[256,384]{1,0:T(8,128)(2,1)S(1)}, u32[]{:S(2)}, u32[]{:S(2)}) collective-permute-start(bf16[256,384]{1,0:T(8,128)(2,1)} %get-tuple-element.46), channel_id=1, source_target_pairs={{0,6},{1,7},{2,0},{3,1},{4,2},{5,3},{6,4},{7,5},{8,14},{9,15},{10,... | collective-permute-start | bytes 589832 | tf_op jit(solution)/shard_map/ppermute | solution.py:454
  79.4 10.2 %copy-start.8 = (bf16[256,384]{1,0:T(8,128)(2,1)S(1)}, bf16[256,384]{1,0:T(8,128)(2,1)}, u32[]{:S(2)}) copy-start(bf16[256,384]{1,0:T(8,128)(2,1)} %get-tuple-element.43.refs_4_) | copy-start | bytes 589828
  79.4 10.2 %copy-start.12 = (f32[3,1,1024]{2,1,0:T(1,128)S(1)}, f32[3,1,1024]{2,1,0:T(1,128)}, u32[]{:S(2)}) copy-start(f32[3,1,1024]{2,1,0:T(1,128)} %get-tuple-element.48.refs_9_) | copy-start | bytes 36868
  79.4 32.7 %all-to-all-start.2 = ((bf16[32,16,768]{2,1,0:T(8,128)(2,1)}), bf16[32,16,768]{2,1,0:T(8,128)(2,1)S(1)}, u32[]{:S(2)}, u32[]{:S(2)}) async-start(bf16[32,16,768]{2,1,0:T(8,128)(2,1)} %bitcast.13), calls=%async_computation.2 | async-start | bytes 1572864 | tf_op jit(solution)/shard_map/all_to_all | solution.py:463
  90.7 1.4 copy-start.11
  92.1 20.1 %copy-start.4 = (s32[32]{0:T(128)S(1)}, s32[32]{0:T(128)}, u32[]{:S(2)}) copy-start(s32[32]{0:T(128)} %refs_0_.3) | copy-start | bytes 388
  105.0 17.8 %collective-permute-start.12 = (bf16[256,1152]{1,0:T(8,128)(2,1)}, bf16[256,1152]{1,0:T(8,128)(2,1)S(1)}, u32[]{:S(2)}, u32[]{:S(2)}) collective-permute-start(bf16[256,1152]{1,0:T(8,128)(2,1)} %get-tuple-element.51), channel_id=1, source_target_pairs={{0,6},{1,7},{2,0},{3,1},{4,2},{5,3},{6,4},{7,5},{8,14},{9,15},{10,... | collective-permute-start | bytes 1769480 | tf_op jit(solution)/shard_map/ppermute | solution.py:454
  107.1 26.9 %collective-permute-start.13 = (bf16[256,1152]{1,0:T(8,128)(2,1)}, bf16[256,1152]{1,0:T(8,128)(2,1)S(1)}, u32[]{:S(2)}, u32[]{:S(2)}) collective-permute-start(bf16[256,1152]{1,0:T(8,128)(2,1)} %get-tuple-element.52), channel_id=1, source_target_pairs={{0,4},{1,5},{2,6},{3,7},{4,0},{5,1},{6,2},{7,3},{8,12},{9,13},{10,... | collective-permute-start | bytes 1769480 | tf_op jit(solution)/shard_map/ppermute | solution.py:454
  108.3 26.4 %collective-permute-start.14 = (bf16[256,1152]{1,0:T(8,128)(2,1)}, bf16[256,1152]{1,0:T(8,128)(2,1)S(1)}, u32[]{:S(2)}, u32[]{:S(2)}) collective-permute-start(bf16[256,1152]{1,0:T(8,128)(2,1)} %get-tuple-element.53), channel_id=1, source_target_pairs={{0,2},{1,3},{2,4},{3,5},{4,6},{5,7},{6,0},{7,1},{8,10},{9,11},{10,... | collective-permute-start | bytes 1769480 | tf_op jit(solution)/shard_map/ppermute | solution.py:454
  113.8 29.5 %all-to-all-start.3 = ((bf16[32,16,768]{2,1,0:T(8,128)(2,1)}), bf16[32,16,768]{2,1,0:T(8,128)(2,1)S(1)}, u32[]{:S(2)}, u32[]{:S(2)}) async-start(bf16[32,16,768]{2,1,0:T(8,128)(2,1)} %reorder.3), calls=%async_computation.3 | async-start | bytes 1572864 | tf_op jit(solution)/shard_map/all_to_all | solution.py:463
  134.9 2.9 %collective-permute-start.15 = (bf16[4,128,1152]{2,1,0:T(8,128)(2,1)S(1)}, bf16[4,128,1152]{2,1,0:T(8,128)(2,1)S(1)}, u32[]{:S(2)}, u32[]{:S(2)}) collective-permute-start(bf16[4,128,1152]{2,1,0:T(8,128)(2,1)S(1)} %for_sibling.3.refs_5_), channel_id=1, source_target_pairs={{0,1},{1,0},{2,3},{3,2},{4,5},{5,4},{6,7},{7,6},{8,9},{9,8},{10,11... | collective-permute-start | bytes 3538952 | tf_op jit(solution)/shard_map/ppermute | solution.py:459
  (1 other events, 1.1 us)
